TPU v7x, 128 devices: a whole 4x4x4 slice. The times are simulated.
128 devices in a mesh: wide: 16 (over x, y), narrow: 8 (over z, core).
Axes of the slice: x: 4, y: 4, z: 4, core: 2. Of those that a mesh axis runs over, the one named last changes fastest.
Arguments:
- features: bfloat16 [16, 8, 8, 48, 9216], P('wide', 'narrow'), may hold values from -6 to 6
- patch_ids: int32 [16, 8, 8], P('wide', 'narrow'), may hold values from 0 to 991, as said below
- patch_count: int32 [16, 8], P('wide', 'narrow'), may hold values from 6 to 8, as said below
- labels: int32 [1536, 1536], P('wide', 'narrow'), may hold values from 0 to 117
- mlp_weight: bfloat16 [48, 48], replicated, may hold values from -0.875 to 0.875
- mlp_bias: float32 [48], replicated, may hold values from -3 to 3
- out_weight: bfloat16 [118, 48], replicated
- out_bias: float32 [118], replicated, may hold values from -4 to 4
Outputs:
- blended: bfloat16 [118, 1536, 1536], P(None, 'wide', 'narrow')
- dice: float32 [118], replicated
- slab_sums: float32 [16, 8, 2, 118], P('wide', 'narrow')
Inputs may be any that keep to these rules, and one draw needn't show every extreme that they name: `patch_ids`: each device lists patches whose start quadrant row lies in its own band of 4 rows along y (at most 1536 / 48 - 2); the start columns of one device's listed patches share one parity and are pairwise more than one apart, so one device sends at most 4 quadrants to one x slab; entries beyond the count are arbitrary ids. `patch_count`: some device lists 8 patches.
All inputs are finite; a program needn't handle non-finite values.
Results may differ from a plain program's by a relative error of at most 0.0035.
The roundings to bfloat16 on the way count: a program that leaves them out, or rounds other values in their place, can miss the bound.
Values may be sent and summed in bfloat16 or wider, within the bound.
No kernel may reach another device: no remote copies, remote signals or barrier semaphores. Data moves between devices by JAX's collectives and lax.ppermute only.
A program may use at most 192 MiB of HBM per device.

v0:
```python
import jax
import jax.numpy as jnp
from jax import lax
from jax.sharding import PartitionSpec as P

PATCH = 96


def from_behind(shard, axis, by):
    devices = lax.axis_size(axis)
    pairs = [(i, i + by) for i in range(devices) if 0 <= i + by < devices]
    return lax.ppermute(shard, axis, pairs)


def padded_2(block, sides, width):
    for axis, dim in sides:
        count = lax.axis_size(axis)
        forward = [(i, i + 1) for i in range(count - 1)]
        backward = [(target, source) for source, target in forward]
        low = lax.ppermute(
            lax.slice_in_dim(block, block.shape[dim] - width, None, axis=dim), axis, forward
        )
        high = lax.ppermute(lax.slice_in_dim(block, 0, width, axis=dim), axis, backward)
        block = jnp.concatenate([low, block, high], axis=dim)
    return block


def gauss_table(size):
    axis_pos = jnp.arange(size, dtype=jnp.float32) - (size - 1) / 2.0
    sigma = 0.125 * size
    squared = axis_pos[:, None] * axis_pos[:, None] + axis_pos[None, :] * axis_pos[None, :]
    return jnp.exp(-squared / (2.0 * sigma * sigma)).reshape(size * size)


def mlp_section(feats, mlp_weight, mlp_bias):
    hidden = jnp.einsum("oc,kcv->kov", mlp_weight, feats, preferred_element_type=jnp.float32)
    return (feats.astype(jnp.float32) + jax.nn.relu(hidden + mlp_bias[None, :, None])).astype(
        jnp.bfloat16
    )


def output_section(acts, out_weight, out_bias, gain):
    logits = jnp.einsum("oc,...cv->...ov", out_weight, acts, preferred_element_type=jnp.float32)
    probs = jax.nn.softmax(logits + out_bias[:, None], axis=-2)
    return (probs * gain[..., None, :]).astype(jnp.bfloat16)


def quarters(field, half_edge):
    count, depth = (field.shape[0], field.shape[1])
    split = field.reshape(count, depth, 2, half_edge, 2, half_edge)
    return split.transpose(0, 2, 4, 1, 3, 5).reshape(count * 4, depth, half_edge * half_edge)


def edge_core(padded):
    centre = padded[:, 1:-1, 1:-1]
    low = jnp.minimum(
        jnp.minimum(padded[:, :-2, 1:-1], padded[:, 2:, 1:-1]),
        jnp.minimum(padded[:, 1:-1, :-2], padded[:, 1:-1, 2:]),
    )
    return centre - jnp.minimum(centre, low)


def spread_core(padded):
    centre = padded[:, 1:-1, 1:-1]
    high = jnp.maximum(
        jnp.maximum(padded[:, :-2, 1:-1], padded[:, 2:, 1:-1]),
        jnp.maximum(padded[:, 1:-1, :-2], padded[:, 1:-1, 2:]),
    )
    return jnp.maximum(centre, high)


def on_device(features, patch_ids, patch_count, labels, mlp_weight, mlp_bias, out_weight, out_bias):
    n_wide = lax.axis_size("wide")
    slots = features.shape[2]
    classes = out_weight.shape[0]
    quad = PATCH // 2
    area = quad * quad
    span_x, span_y = labels.shape
    rows = span_y // quad
    rows_q = rows * lax.axis_size("narrow")
    band = lax.axis_index("narrow") * rows
    gauss = gauss_table(PATCH)
    gauss_quads = gauss.reshape(2, quad, 2, quad).transpose(0, 2, 1, 3).reshape(4, area)
    feats = features[0, 0]
    ids = patch_ids[0, 0]
    count = patch_count[0, 0]
    active = mlp_section(feats, mlp_weight, mlp_bias)
    slot_ids = jnp.arange(slots, dtype=jnp.int32)
    listed = slot_ids < count
    start_x = ids // rows_q
    start_y = ids % rows_q
    halves = jnp.arange(2, dtype=jnp.int32)
    across = start_x[:, None, None] + halves[None, :, None]
    upward = start_y[:, None, None] + halves[None, None, :]
    owner = across // 2
    local_col = across % 2
    local_row = upward - band
    kind = 2 * halves[None, :, None] + halves[None, None, :]
    place = owner * 4 + 2 * halves[None, None, :] + local_col
    source = slot_ids[:, None, None] * 4 + kind
    listed_all = jnp.broadcast_to(listed[:, None, None], place.shape)
    target = jnp.where(listed_all, place, n_wide * 4).reshape(-1)
    empty = jnp.full((n_wide * 4,), -1, jnp.int32)
    pick = empty.at[target].set(source.reshape(-1), mode="drop")
    label_tag = (local_row * 4 + kind).reshape(-1)
    send_tag = empty.at[target].set(label_tag, mode="drop").reshape(n_wide, 4)
    present = pick >= 0
    pick_safe = jnp.maximum(pick, 0)
    weighted = output_section(active, out_weight, out_bias, gauss[None, :])
    parts = quarters(weighted, quad)
    payload = jnp.where(present[:, None, None], parts[pick_safe], jnp.zeros((), jnp.bfloat16))
    payload = payload.reshape(n_wide, 4, classes, area)
    received, got_tag = (
        lax.all_to_all(payload, "wide", split_axis=0, concat_axis=0, tiled=True),
        lax.all_to_all(send_tag, "wide", split_axis=0, concat_axis=0, tiled=True),
    )
    received = received.reshape(n_wide * 4, classes, area)
    tags = got_tag.reshape(-1)
    valid = tags >= 0
    tiles = 2 * (rows + 1)
    tile_of = tags // 4 * 2 + jnp.arange(n_wide * 4, dtype=jnp.int32) % 2
    choose = valid[:, None] & (tile_of[:, None] == jnp.arange(tiles, dtype=jnp.int32)[None, :])
    total = jnp.einsum(
        "st,scv->tcv", choose.astype(jnp.bfloat16), received, preferred_element_type=jnp.float32
    )
    kind_hot = (
        valid[:, None] & ((tags % 4)[:, None] == jnp.arange(4, dtype=jnp.int32)[None, :])
    ).astype(jnp.float32)
    gains = jnp.dot(kind_hot, gauss_quads, precision=lax.Precision.HIGHEST)
    norm = jnp.dot(choose.astype(jnp.float32).T, gains, precision=lax.Precision.HIGHEST)
    came_total, came_norm = from_behind((total[2 * rows :], norm[2 * rows :]), "narrow", 1)
    total = total[: 2 * rows].at[0:2].add(came_total)
    norm = norm[: 2 * rows].at[0:2].add(came_norm)
    total = (
        total.reshape(rows, 2, classes, quad, quad)
        .transpose(2, 1, 3, 0, 4)
        .reshape(classes, span_x, span_y)
    )
    norm = norm.reshape(rows, 2, quad, quad).transpose(1, 2, 0, 3).reshape(span_x, span_y)
    background = (jnp.arange(classes) == 0).astype(jnp.float32)[:, None, None]
    blended = ((total + 0.001 * background) / (norm + 0.001)[None]).astype(jnp.bfloat16)
    label_wide = padded_2(labels + 1, (("wide", 0), ("narrow", 1)), 2)
    truth = (label_wide[None] == (jnp.arange(classes, dtype=jnp.int32) + 1)[:, None, None]).astype(
        jnp.bfloat16
    )
    truth_edge_wide = edge_core(truth)
    truth_edge = truth_edge_wide[:, 1:-1, 1:-1]
    truth_spread = spread_core(truth_edge_wide)
    prob_cycle = padded_2(blended, (("wide", 1), ("narrow", 2)), 1)
    prob_edge = edge_core(prob_cycle.astype(jnp.float32))
    edge_cycle = padded_2(prob_edge.astype(jnp.bfloat16), (("wide", 1), ("narrow", 2)), 1).astype(
        prob_edge.dtype
    )
    prob_spread = spread_core(edge_cycle)
    numer = jnp.sum(
        prob_edge * truth_spread.astype(jnp.float32) + truth_edge.astype(jnp.float32) * prob_spread,
        axis=(1, 2),
    )
    denom = jnp.sum(prob_edge + truth_edge.astype(jnp.float32), axis=(1, 2))
    slab_sums = (jnp.stack([numer, denom]) / jnp.float32(span_x)).reshape(1, 1, 2, classes)
    all_numer, all_denom = lax.psum((numer, denom), ("wide", "narrow"))
    dice = (all_numer + 1.0) / (all_denom + 1.0)
    return (blended, dice, slab_sums)


def solution(mesh):
    return jax.shard_map(
        on_device,
        mesh=mesh,
        in_specs=(
            P("wide", "narrow", None, None, None),
            P("wide", "narrow", None),
            P("wide", "narrow"),
            P("wide", "narrow"),
            P(),
            P(),
            P(),
            P(),
        ),
        out_specs=(P(None, "wide", "narrow"), P(), P("wide", "narrow", None, None)),
        check_vma=False,
    )
```

profile of v0, /device:TPU:1, one launch (start us, length us, event | category | flops | bytes accessed | tf_op | source)
XLA Modules:
  0.0 1124.9 jit_solution(1319736581817266215)
XLA Ops:
  3.9 7.6 all-to-all-start
  12.5 10.8 fusion.10
  23.3 19.3 %multiply_convert_fusion = bf16[8,118,9216]{2,1,0:T(8,128)(2,1)} fusion(f32[9216]{0:T(1024)S(1)} %exp.23, f32[118]{0:T(128)S(1)} %copy-done.4, bf16[8,48,9216]{2,1,0:T(8,128)(2,1)} %fusion.10, bf16[118,48]{0,1:T(8,128)(2,1)S(1)} %copy-done), kind=kOutput, calls=%fused_computation.9 | convolution fusion | flops 878838016 | bytes 24526360 | tf_op jit(solution)/shard_map/div | solution.py:44
  42.6 22.9 %copy.26 = bf16[8,118,9216]{1,2,0:T(8,128)(2,1)} copy(bf16[8,118,9216]{2,1,0:T(8,128)(2,1)} %multiply_convert_fusion) | data formatting | bytes 34799616 | tf_op jit(solution)/shard_map/convert_element_type | solution.py:45
  65.5 18.3 %copy.27 = bf16[8,2,2,118,48,48]{3,5,4,2,1,0:T(8,128)(2,1)} copy(bf16[8,2,2,118,48,48]{3,5,2,4,1,0:T(8,128)(2,1)} %bitcast.83) | data formatting | bytes 34799616 | tf_op jit(solution)/shard_map/transpose | solution.py:51
  83.8 23.2 %copy.28 = bf16[32,118,2304]{2,1,0:T(8,128)(2,1)} copy(bf16[32,118,2304]{1,2,0:T(8,128)(2,1)} %bitcast.84) | data formatting | bytes 34799616 | tf_op jit(solution)/shard_map/reshape | solution.py:51
  107.1 18.9 %gather_fusion = bf16[64,118,2304]{2,1,0:T(8,128)(2,1)} fusion(bf16[32,118,2304]{2,1,0:T(8,128)(2,1)} %copy.28, s32[1024]{0:T(1024)S(1)} %pad_clamp_fusion), kind=kCustom, calls=%fused_computation | custom fusion | bytes 69599488 | tf_op jit(solution)/shard_map/gather | solution.py:111
  126.0 27.6 %copy_select_fusion = bf16[16,4,118,2304]{3,1,2,0:T(4,128)(2,1)} fusion(bf16[16,4,118,2304]{3,2,1,0:T(8,128)(2,1)} %bitcast.82, pred[16,4]{1,0:T(8,128)(4,1)S(1)} %broadcast_in_dim.26), kind=kLoop, calls=%fused_computation.10 | loop fusion | flops 17399808 | bytes 69599296 | tf_op jit(solution)/shard_map/jit(_where)/select_n | solution.py:111
  153.6 6.8 all-to-all-start.1
  166.6 632.9 %all-to-all-done.1 = bf16[16,4,118,2304]{3,1,2,0:T(4,128)(2,1)} async-done(((bf16[16,4,118,2304]{3,1,2,0:T(4,128)(2,1)}), bf16[16,4,118,2304]{3,1,2,0:T(4,128)(2,1)}, u32[]{:S(2)}, u32[]{:S(2)}) %all-to-all-start.1) | async-done | bytes 34799648 | tf_op jit(solution)/shard_map/all_to_all | solution.py:114
  799.5 23.9 %copy.30 = bf16[16,4,118,2304]{3,1,0,2:T(4,128)(2,1)} copy(bf16[16,4,118,2304]{3,1,2,0:T(4,128)(2,1)} %all-to-all-done.1) | data formatting | bytes 69599232 | tf_op jit(solution)/shard_map/all_to_all | solution.py:114
  823.4 53.1 %reshape.545 = bf16[64,118,2304]{2,0,1:T(8,128)(2,1)} reshape(bf16[16,4,118,2304]{3,1,0,2:T(4,128)(2,1)} %copy.30) | data formatting | bytes 69599232 | tf_op jit(solution)/shard_map/reshape | solution.py:117
  876.5 19.8 %fusion.40 = f32[10,118,2304]{2,0,1:T(8,128)} fusion(bf16[64,118,2304]{2,0,1:T(8,128)(2,1)} %reshape.545, s32[64]{0:T(128)S(1)} %get-tuple-element.48, pred[64]{0:T(512)(128)(4,1)S(1)} %broadcast_compare_fusion.1), kind=kOutput, calls=%fused_computation.73 | convolution fusion | flops 347997440 | bytes 45674816 | tf_op jit(solution)/shard_map/st,scv->tcv/dot_general | solution.py:123
  900.4 7.8 collective-permute-start
  911.0 21.2 %collective-permute-done.1 = f32[2,2304]{1,0:T(2,128)S(1)} collective-permute-done((f32[2,2304]{1,0:T(2,128)S(1)}, f32[2,2304]{1,0:T(2,128)S(1)}, u32[]{:S(2)}, u32[]{:S(2)}) %collective-permute-start.1) | collective-permute-done | bytes 18464 | tf_op jit(solution)/shard_map/ppermute | solution.py:12
  932.7 7.4 slice.194
  940.1 6.6 fusion.21
  946.7 9.5 copy.31
  987.1 5.9 maximum_convert_fusion
  993.0 7.5 fusion.58
  1017.5 9.7 minimum_subtract_fusion.1
  1027.2 6.0 maximum_convert_fusion.1
  1033.2 23.8 %fusion.12 = (f32[118]{0:T(128)S(1)}, f32[118]{0:T(128)S(1)}) fusion(f32[118,98,194]{0,2,1:T(8,128)S(1)} %maximum_convert_fusion.1, f32[118,96,192]{0,2,1:T(8,128)} %get-tuple-element.32, bf16[118,98,194]{0,2,1:T(8,128)(2,1)} %minimum_subtract_fusion.1), kind=kLoop, calls=%fused_computation.21 | loop fusion | flops 34799380 | bytes 73950128 | tf_op jit(solution)/shard_map/reduce_sum | solution.py:155
  1057.0 66.8 %all-reduce = (f32[118]{0:T(128)S(1)}, f32[118]{0:T(128)S(1)}) all-reduce(f32[118]{0:T(128)S(1)} %get-tuple-element.28, f32[118]{0:T(128)S(1)} %get-tuple-element.27), channel_id=1, replica_groups=mesh['wide'=16,'narrow'=8] {'wide','narrow'}, use_global_device_ids=true, to_apply=%region_7.8 | all-reduce | flops 236 | bytes 1888 | tf_op jit(solution)/shard_map/psum | solution.py:161
  (98 shorter events, 65.8 us)
Async XLA Ops:
  0.6 22.7 %copy-start = (bf16[118,48]{0,1:T(8,128)(2,1)S(1)}, bf16[118,48]{0,1:T(8,128)(2,1)}, u32[]{:S(2)}) copy-start(bf16[118,48]{0,1:T(8,128)(2,1)} %param.18) | copy-start | bytes 33988
  0.6 22.6 %copy-start.4 = (f32[118]{0:T(128)S(1)}, f32[118]{0:T(128)}, u32[]{:S(2)}) copy-start(f32[118]{0:T(128)} %param.19) | copy-start | bytes 1420
  3.9 149.7 %all-to-all-start = ((s32[16,1,4]{2,1,0:T(1,128)}), s32[16,1,4]{2,1,0:T(1,128)S(1)}, u32[]{:S(2)}, u32[]{:S(2)}) async-start(s32[16,1,4]{2,1,0:T(1,128)} %bitcast.3), calls=%async_computation | async-start | bytes 16384 | tf_op jit(solution)/shard_map/all_to_all | solution.py:115
  153.6 6.8 copy-start.3
  153.6 646.0 %all-to-all-start.1 = ((bf16[16,4,118,2304]{3,1,2,0:T(4,128)(2,1)}), bf16[16,4,118,2304]{3,1,2,0:T(4,128)(2,1)}, u32[]{:S(2)}, u32[]{:S(2)}) async-start(bf16[16,4,118,2304]{3,1,2,0:T(4,128)(2,1)} %copy_select_fusion), calls=%async_computation.1 | async-start | bytes 69599232 | tf_op jit(solution)/shard_map/all_to_all | solution.py:114
  160.4 750.6 %collective-permute-start.6 = (s32[2,192]{1,0:T(2,128)S(1)}, s32[2,192]{1,0:T(2,128)S(1)}, u32[]{:S(2)}, u32[]{:S(2)}) collective-permute-start(s32[2,192]{1,0:T(2,128)S(1)} %get-tuple-element.43), channel_id=1, source_target_pairs={{0,8},{8,16},{16,24},{24,32},{32,40},{40,48},{48,56},{56,64},{64,7... | collective-permute-start | bytes 4616 | tf_op jit(solution)/shard_map/ppermute | solution.py:20
  163.6 747.3 %collective-permute-start.7 = (s32[2,192]{1,0:T(2,128)S(1)}, s32[2,192]{1,0:T(2,128)S(1)}, u32[]{:S(2)}, u32[]{:S(2)}) collective-permute-start(s32[2,192]{1,0:T(2,128)S(1)} %get-tuple-element.44), channel_id=1, source_target_pairs={{8,0},{16,8},{24,16},{32,24},{40,32},{48,40},{56,48},{64,56},{72,6... | collective-permute-start | bytes 4616 | tf_op jit(solution)/shard_map/ppermute | solution.py:23
  900.4 39.7 %collective-permute-start = (f32[2,118,2304]{2,0,1:T(2,128)S(1)}, f32[2,118,2304]{2,0,1:T(2,128)}, u32[]{:S(2)}, u32[]{:S(2)}) collective-permute-start(f32[2,118,2304]{2,0,1:T(2,128)S(1)} %slice.196), channel_id=1, source_target_pairs={{0,1},{1,2},{2,3},{3,4},{4,5},{5,6},{6,7},{8,9},{9,10},{10,11},{11... | collective-permute-start | bytes 6524936 | tf_op jit(solution)/shard_map/ppermute | solution.py:12
  909.0 23.2 %collective-permute-start.1 = (f32[2,2304]{1,0:T(2,128)S(1)}, f32[2,2304]{1,0:T(2,128)S(1)}, u32[]{:S(2)}, u32[]{:S(2)}) collective-permute-start(f32[2,2304]{1,0:T(2,128)S(1)} %slice.199), channel_id=1, source_target_pairs={{0,1},{1,2},{2,3},{3,4},{4,5},{5,6},{6,7},{8,9},{9,10},{10,11},{11... | collective-permute-start | bytes 55304 | tf_op jit(solution)/shard_map/ppermute | solution.py:12
  964.3 22.8 %copy-start.2 = (bf16[118,96,192]{0,2,1:T(8,128)(2,1)}, bf16[118,96,192]{0,2,1:T(8,128)(2,1)S(1)}, u32[]{:S(2)}) copy-start(bf16[118,96,192]{0,2,1:T(8,128)(2,1)S(1)} %divide_convert_fusion) | copy-start | bytes 13049860
  964.3 13.6 %collective-permute-start.2 = (bf16[118,1,192]{0,2,1:T(8,128)(2,1)S(1)}, bf16[118,1,192]{0,2,1:T(8,128)(2,1)S(1)}, u32[]{:S(2)}, u32[]{:S(2)}) collective-permute-start(bf16[118,1,192]{0,2,1:T(8,128)(2,1)S(1)} %get-tuple-element.39), channel_id=1, source_target_pairs={{0,8},{8,16},{16,24},{24,32},{32,40},{40,48},{48,56},{56,64},{64,7... | collective-permute-start | bytes 135944 | tf_op jit(solution)/shard_map/ppermute | solution.py:20
  969.9 8.0 collective-permute-start.3
  971.3 12.3 %collective-permute-start.8 = (s32[100,2]{1,0:T(8,128)S(1)}, s32[100,2]{1,0:T(8,128)S(1)}, u32[]{:S(2)}, u32[]{:S(2)}) collective-permute-start(s32[100,2]{1,0:T(8,128)S(1)} %get-tuple-element.41), channel_id=1, source_target_pairs={{0,1},{1,2},{2,3},{3,4},{4,5},{5,6},{6,7},{8,9},{9,10},{10,11},{11... | collective-permute-start | bytes 2408 | tf_op jit(solution)/shard_map/ppermute | solution.py:20
  976.0 7.7 collective-permute-start.9
  978.1 5.7 collective-permute-start.4
  981.7 5.4 collective-permute-start.5
  1001.3 9.2 collective-permute-start.10
  1005.6 4.9 collective-permute-start.11
  1011.6 15.6 %collective-permute-start.12 = (bf16[118,98,1]{0,2,1:T(2,128)(2,1)S(1)}, bf16[118,98,1]{0,2,1:T(2,128)(2,1)S(1)}, u32[]{:S(2)}, u32[]{:S(2)}) collective-permute-start(bf16[118,98,1]{0,2,1:T(2,128)(2,1)S(1)} %get-tuple-element.33), channel_id=1, source_target_pairs={{0,1},{1,2},{2,3},{3,4},{4,5},{5,6},{6,7},{8,9},{9,10},{10,11},{11... | collective-permute-start | bytes 69392 | tf_op jit(solution)/shard_map/ppermute | solution.py:20
  1015.1 12.1 %slice-start = ((s8[4718592]{0:T(1024)(128)(4,1)}), s8[4194304]{0:T(1024)(128)(4,1)S(1)}, s32[]{:S(2)}) async-start(s8[4718592]{0:T(1024)(128)(4,1)} %bitcast.85), calls=%async_computation.2 | async-start | bytes 8388608
  1015.1 12.1 %slice-start.1 = ((s8[4718592]{0:T(1024)(128)(4,1)}), s8[524288]{0:T(1024)(128)(4,1)S(1)}, s32[]{:S(2)}) async-start(s8[4718592]{0:T(1024)(128)(4,1)} %bitcast.85), calls=%async_computation.3 | async-start | bytes 1048576
  1015.1 12.1 %collective-permute-start.13 = (bf16[118,98,1]{0,2,1:T(2,128)(2,1)S(1)}, bf16[118,98,1]{0,2,1:T(2,128)(2,1)S(1)}, u32[]{:S(2)}, u32[]{:S(2)}) collective-permute-start(bf16[118,98,1]{0,2,1:T(2,128)(2,1)S(1)} %get-tuple-element.34), channel_id=1, source_target_pairs={{1,0},{2,1},{3,2},{4,3},{5,4},{6,5},{7,6},{9,8},{10,9},{11,10},{12... | collective-permute-start | bytes 69392 | tf_op jit(solution)/shard_map/ppermute | solution.py:23
  1033.2 91.7 %copy-start.1 = (bf16[118,48]{0,1:T(8,128)(2,1)S(1)}, bf16[118,48]{0,1:T(8,128)(2,1)}, u32[]{:S(2)}) copy-start(bf16[118,48]{0,1:T(8,128)(2,1)} %param.18) | copy-start | bytes 33988
where the time goes:
time: 1130 us; the launch traced here: 1120 us
  waiting for transfers between devices  657 us (58%)
  local copies, waits for them, and re-layouts  191 us (17%)
  other arithmetic  98 us (9%)
  blocking collectives  66.8 us (6%)
  starting transfers between devices  59.2 us (5%)
  matrix products  50.6 us (4%)
    all_to_all x1, waiting for transfers between devices, on_device(): lax.all_to_all(payload, 'wide', split_axis=0, concat_axis=0, tiled=True)  633 us
    psum x1, blocking collectives, on_device(): all_numer, all_denom = lax.psum((numer, denom), ('wide', 'narrow'))  66.8 us
    reshape x1, local copies, waits for them, and re-layouts, on_device(): received = received.reshape(n_wide * 4, classes, area)  53.1 us
    select_n x1, other arithmetic, on_device(): jnp.where(present[:, None, None], parts[pick_safe], jnp.zeros((), jnp.bfl...  27.6 us
    ppermute x6, starting transfers between devices, padded_2(): lax.ppermute(lax.slice_in_dim(block, block.shape[dim] - width, None, axis...  24.8 us
    all_to_all x1, local copies, waits for them, and re-layouts, on_device(): lax.all_to_all(payload, 'wide', split_axis=0, concat_axis=0, tiled=True)  23.9 us
    reduce_sum x1, other arithmetic, on_device(): jnp.sum(prob_edge * truth_spread.astype(jnp.float32) + truth_edge.astype(...  23.8 us
    reshape x1, local copies, waits for them, and re-layouts, quarters(): split.transpose(0, 2, 4, 1, 3, 5)  23.2 us
  transfers between devices with their start and end apart: 16, of which 3 were waited for; matrix products, arithmetic and copies ran while one was open for 24% of the time, Pallas kernels for 0%

commit v1 on v0

v1 whole, which is shorter than its diff:
```python
import functools

import jax
import jax.numpy as jnp
from jax import lax
from jax.experimental import pallas as pl
from jax.experimental.pallas import tpu as pltpu
from jax.sharding import PartitionSpec as P

PATCH = 96
QUAD = 48
TILE = 128
RING = 256
ROWS = 4
CHUNKS = ((0, 16), (16, 16), (32, 16))
VMEM_LIMIT = 50 * 1024 * 1024


def pack_kernel(first, rows, pick_ref, feats_ref, out_ref, sems):
    width = rows * PATCH

    def copy_of(column):
        source = jnp.maximum(pick_ref[column], 0)
        start = first if column % 2 == 0 else QUAD - first - rows
        lane = pl.multiple_of((source % 2) * (QUAD * PATCH) + start * PATCH, TILE)
        return pltpu.make_async_copy(
            feats_ref.at[source // 2, :, pl.ds(lane, width)], out_ref.at[column], sems.at[column]
        )

    columns = out_ref.shape[0]
    for column in range(columns):
        copy_of(column).start()
    for column in range(columns):
        copy_of(column).wait()


def pack(feats, pick, first, rows):
    columns = pick.shape[0]
    width = rows * PATCH
    return pl.pallas_call(
        functools.partial(pack_kernel, first, rows),
        out_shape=jax.ShapeDtypeStruct((columns, feats.shape[1], width), feats.dtype),
        in_specs=[pl.BlockSpec(memory_space=pltpu.SMEM), pl.BlockSpec(memory_space=pl.ANY)],
        out_specs=pl.BlockSpec(memory_space=pl.ANY),
        scratch_shapes=[pltpu.SemaphoreType.DMA((columns,))],
        cost_estimate=pl.CostEstimate(
            flops=0, bytes_accessed=columns * width * feats.shape[1] * 4, transcendentals=0
        ),
        name="pack",
    )(pick, feats)


def spread_rows(tiles, lane):
    one, two, three = tiles
    return (
        one,
        jnp.where(lane < 32, pltpu.roll(one, 32, 1), pltpu.roll(two, 32, 1)),
        jnp.where(lane < 64, pltpu.roll(two, 64, 1), pltpu.roll(three, 64, 1)),
        pltpu.roll(three, 96, 1),
    )


def head_kernel(
    first, rows, classes, code_ref, recv_ref, mlp_ref, bias_ref, head_ref, gauss_ref,
    own_ref, up_ref, down_ref, acc_ref, edge_ref,
):
    feat = recv_ref.shape[1]
    padded = head_ref.shape[0]
    lane_feat = lax.broadcasted_iota(jnp.int32, (feat, TILE), 1)
    lane = lax.broadcasted_iota(jnp.int32, (padded, TILE), 1)
    real = lax.broadcasted_iota(jnp.int32, (padded, TILE), 0) < classes
    mlp = mlp_ref[...]
    head = head_ref[...]
    extra = jnp.ones((head.shape[1] - feat, 4 * TILE), jnp.bfloat16)

    @pl.loop(0, ROWS)
    def _(which):
        @pl.loop(0, 2 * rows)
        def _(row):
            acc_ref[which, row] = jnp.zeros((padded, TILE), jnp.float32)

    edge_ref[...] = jnp.zeros_like(edge_ref)

    @pl.loop(0, code_ref[2 * 16])
    def _(item):
        code = code_ref[item]
        slot = code // 8
        which = (code // 2) % 4
        side = slot % 2
        start = (code % 2) * QUAD + jnp.where(side == 0, first, QUAD - first - rows)
        for group in range(rows // 4):
            at = group * 3 * TILE
            tiles = [
                recv_ref[slot, :, at + i * TILE : at + (i + 1) * TILE].astype(jnp.float32)
                for i in range(3)
            ]
            voxels = jnp.concatenate(spread_rows(tiles, lane_feat), axis=1)
            hidden = jnp.dot(
                mlp, voxels.astype(jnp.bfloat16), preferred_element_type=jnp.float32
            )
            bias = jnp.concatenate([bias_ref[...]] * 4, axis=1)
            active = (voxels + jnp.maximum(hidden + bias, 0.0)).astype(jnp.bfloat16)
            logits = jnp.dot(
                head, jnp.concatenate([active, extra], axis=0), preferred_element_type=jnp.float32
            )
            for i in range(4):
                part = logits[:, i * TILE : (i + 1) * TILE]
                top = jnp.max(part, axis=0, keepdims=True)
                raised = jnp.where(real, jnp.exp(part - top), 0.0)
                scale = gauss_ref[pl.ds(start + group * 4 + i, 1), :] / jnp.sum(
                    raised, axis=0, keepdims=True
                )
                row = side * rows + group * 4 + i
                acc_ref[which, row] += (
                    (raised * scale).astype(jnp.bfloat16).astype(jnp.float32)
                )

    def merged(row):
        a0, a1, a2, a3 = [acc_ref[which, row] for which in range(ROWS)]
        a1 = pltpu.roll(a1, 48, 1)
        a2 = pltpu.roll(a2, 96, 1)
        low = a0 + jnp.where(lane >= 48, a1, 0.0) + jnp.where(lane >= 96, a2, 0.0)
        high = (
            jnp.where(lane < 48, a1, 0.0)
            + jnp.where(lane < 96, a2, 0.0)
            + pltpu.roll(a3, 16, 1)
        )
        own_ref[row, :, 0:TILE] = low
        own_ref[row, :, TILE:RING] = high
        edge_ref[...] = jnp.where(
            (lane == 2 * row) | (lane == 2 * row + 1), pltpu.roll(low, 2 * row, 1), edge_ref[...]
        )
        return high

    @pl.loop(0, rows)
    def _(pair):
        even = merged(2 * pair)
        odd = merged(2 * pair + 1)
        up_ref[pair] = jnp.where(lane < 64, pltpu.roll(even, 66, 1), pltpu.roll(odd, 2, 1)).astype(
            jnp.bfloat16
        )

    down_ref[...] = edge_ref[...].astype(jnp.bfloat16)


def head_of(recv, codes, mlp_weight, bias_tile, head_weight, gauss, first, rows, classes):
    padded = head_weight.shape[0]
    whole = pl.BlockSpec(memory_space=pltpu.VMEM)
    return pl.pallas_call(
        functools.partial(head_kernel, first, rows, classes),
        out_shape=(
            jax.ShapeDtypeStruct((2 * rows, padded, RING), jnp.float32),
            jax.ShapeDtypeStruct((rows, padded, TILE), jnp.bfloat16),
            jax.ShapeDtypeStruct((padded, TILE), jnp.bfloat16),
        ),
        in_specs=[pl.BlockSpec(memory_space=pltpu.SMEM)] + [whole] * 5,
        out_specs=(whole, whole, whole),
        scratch_shapes=[
            pltpu.VMEM((ROWS, 2 * rows, padded, TILE), jnp.float32),
            pltpu.VMEM((padded, TILE), jnp.float32),
        ],
        compiler_params=pltpu.CompilerParams(vmem_limit_bytes=VMEM_LIMIT),
        cost_estimate=pl.CostEstimate(
            flops=rows * 900_000_000 // 48, bytes_accessed=rows * 25_000_000 // 48,
            transcendentals=rows * 12_000_000 // 48,
        ),
        name="head",
    )(codes, recv, mlp_weight, bias_tile, head_weight, gauss)


def blend_kernel(own_ref, up_ref, down_ref, inv_ref, prob_ref):
    rows, padded, _ = own_ref.shape
    lane = lax.broadcasted_iota(jnp.int32, (padded, TILE), 1)
    first = lax.broadcasted_iota(jnp.int32, (padded, TILE), 0) == 0
    extra = jnp.where(first, 0.001, 0.0)
    down = down_ref[...].astype(jnp.float32)

    def one(row, came, shift):
        came = pltpu.roll(came, shift, 1)
        low = own_ref[row, :, 0:TILE] + jnp.where(lane < 48, came, 0.0)
        high = own_ref[row, :, TILE:RING] + jnp.where(lane >= 126, came, 0.0)
        after = pltpu.roll(down, lax.rem(192 - 2 * row, TILE), 1)
        high = high + jnp.where((lane == 64) | (lane == 65), after, 0.0)
        scale = inv_ref[pl.ds(row, 1), :]
        prob_ref[row, :, 0:TILE] = ((low + extra) * scale[:, 0:TILE]).astype(jnp.bfloat16)
        prob_ref[row, :, TILE:RING] = ((high + extra) * scale[:, TILE:RING]).astype(jnp.bfloat16)

    @pl.loop(0, rows // 2)
    def _(pair):
        came = up_ref[pair].astype(jnp.float32)
        one(2 * pair, came, 126)
        one(2 * pair + 1, came, 62)


def blend_of(own, up, down, inv):
    whole = pl.BlockSpec(memory_space=pltpu.VMEM)
    return pl.pallas_call(
        blend_kernel,
        out_shape=jax.ShapeDtypeStruct(own.shape, jnp.bfloat16),
        in_specs=[whole] * 4,
        out_specs=whole,
        compiler_params=pltpu.CompilerParams(vmem_limit_bytes=VMEM_LIMIT),
        cost_estimate=pl.CostEstimate(
            flops=own.size * 4, bytes_accessed=own.size * 7, transcendentals=0
        ),
        name="blend",
    )(own, up, down, inv)


def turn(tiles, forward, lane):
    low, high = tiles
    shift, at = (1, 0) if forward else (TILE - 1, TILE - 1)
    low, high = pltpu.roll(low, shift, 1), pltpu.roll(high, shift, 1)
    return jnp.where(lane == at, high, low), jnp.where(lane == at, low, high)


def dice_kernel(prob_ref, label_ref, sums_ref, edge_ref, numer_ref, denom_ref):
    padded = prob_ref.shape[1]
    rows = prob_ref.shape[0] - 4
    lane = lax.broadcasted_iota(jnp.int32, (8, TILE), 1)
    klass = lax.broadcasted_iota(jnp.int32, (8, TILE), 0) + 1
    owned = (lane < TILE, lane < 64)

    def tiles_of(ref, row, group):
        return [
            ref[row, group : group + 8, i * TILE : (i + 1) * TILE].astype(jnp.float32)
            for i in range(2)
        ]

    @pl.loop(0, rows + 2)
    def _(row):
        for group in range(0, padded, 8):
            centre = tiles_of(prob_ref, row + 1, group)
            before, after = tiles_of(prob_ref, row, group), tiles_of(prob_ref, row + 2, group)
            left, right = turn(centre, True, lane), turn(centre, False, lane)
            for i in range(2):
                low = jnp.minimum(
                    jnp.minimum(before[i], after[i]), jnp.minimum(left[i], right[i])
                )
                edge_ref[row, group : group + 8, i * TILE : (i + 1) * TILE] = centre[
                    i
                ] - jnp.minimum(centre[i], low)

    numer_ref[...] = jnp.zeros_like(numer_ref)
    denom_ref[...] = jnp.zeros_like(denom_ref)

    @pl.loop(0, rows)
    def _(row):
        def labels_of(at):
            line = label_ref[pl.ds(at, 1), :]
            return [
                jnp.broadcast_to(line[:, i * TILE : (i + 1) * TILE], (8, TILE)) for i in range(2)
            ]

        middle = labels_of(row + 1)
        near = (labels_of(row), labels_of(row + 2), turn(middle, True, lane), turn(middle, False, lane))
        for group in range(0, padded, 8):
            centre = tiles_of(edge_ref, row + 1, group)
            before, after = tiles_of(edge_ref, row, group), tiles_of(edge_ref, row + 2, group)
            left, right = turn(centre, True, lane), turn(centre, False, lane)
            numer = numer_ref[group : group + 8, :]
            denom = denom_ref[group : group + 8, :]
            for i in range(2):
                wide = jnp.maximum(
                    jnp.maximum(centre[i], jnp.maximum(before[i], after[i])),
                    jnp.maximum(left[i], right[i]),
                )
                here = middle[i] == klass + group
                about = here
                for other in near:
                    about = about | (other[i] == klass + group)
                value = jnp.where(about, centre[i], 0.0) + jnp.where(here, wide, 0.0)
                total = centre[i] + jnp.where(here, 1.0, 0.0)
                if i == 1:
                    value = jnp.where(owned[i], value, 0.0)
                    total = jnp.where(owned[i], total, 0.0)
                numer = numer + value
                denom = denom + total
            numer_ref[group : group + 8, :] = numer
            denom_ref[group : group + 8, :] = denom

    sums_ref[0] = jnp.broadcast_to(
        jnp.sum(numer_ref[...], axis=1, keepdims=True), (padded, TILE)
    )
    sums_ref[1] = jnp.broadcast_to(
        jnp.sum(denom_ref[...], axis=1, keepdims=True), (padded, TILE)
    )


def dice_of(prob, label):
    rows, padded, _ = prob.shape
    whole = pl.BlockSpec(memory_space=pltpu.VMEM)
    return pl.pallas_call(
        dice_kernel,
        out_shape=jax.ShapeDtypeStruct((2, padded, TILE), jnp.float32),
        in_specs=[whole] * 2,
        out_specs=whole,
        scratch_shapes=[
            pltpu.VMEM((rows - 2, padded, RING), jnp.float32),
            pltpu.VMEM((padded, TILE), jnp.float32),
            pltpu.VMEM((padded, TILE), jnp.float32),
        ],
        compiler_params=pltpu.CompilerParams(vmem_limit_bytes=VMEM_LIMIT),
        cost_estimate=pl.CostEstimate(
            flops=prob.size * 30, bytes_accessed=prob.size * 2, transcendentals=0
        ),
        name="dice",
    )(prob, label)


def shifted(block, axis, by):
    devices = lax.axis_size(axis)
    pairs = [(i, i + by) for i in range(devices) if 0 <= i + by < devices]
    return lax.ppermute(block, axis, pairs)


def padded_2(block, sides, width):
    for axis, dim in sides:
        low = shifted(lax.slice_in_dim(block, block.shape[dim] - width, None, axis=dim), axis, 1)
        high = shifted(lax.slice_in_dim(block, 0, width, axis=dim), axis, -1)
        block = jnp.concatenate([low, block, high], axis=dim)
    return block


def gauss_line():
    position = jnp.arange(PATCH, dtype=jnp.float32) - (PATCH - 1) / 2.0
    sigma = 0.125 * PATCH
    return position * position / (2.0 * sigma * sigma)


def gauss_table():
    line = gauss_line()
    table = jnp.exp(-(line[:, None] + line[None, :]))
    return jnp.pad(table, ((0, 0), (0, TILE - PATCH)))


def three_parts(values):
    high = values.astype(jnp.bfloat16)
    rest = values - high.astype(jnp.float32)
    middle = rest.astype(jnp.bfloat16)
    low = (rest - middle.astype(jnp.float32)).astype(jnp.bfloat16)
    return jnp.stack([high, middle, low], axis=1)


def head_matrix(out_weight, out_bias):
    classes, feat = out_weight.shape
    matrix = jnp.concatenate(
        [out_weight, three_parts(out_bias), jnp.zeros((classes, 13), jnp.bfloat16)], axis=1
    )
    return jnp.concatenate([matrix, matrix[-2:]], axis=0)


def ring_of(plane):
    gap = jnp.zeros((plane.shape[0], RING - plane.shape[1]), plane.dtype)
    return jnp.concatenate([plane[:, 2:], gap, plane[:, :2]], axis=1)


def rows_of(plane, first, rows):
    span = plane.shape[0]
    return jnp.concatenate(
        [plane[first : first + rows], plane[span - first - rows : span - first]], axis=0
    )


def on_device(features, patch_ids, patch_count, labels, mlp_weight, mlp_bias, out_weight, out_bias):
    wide, narrow = lax.axis_size("wide"), lax.axis_size("narrow")
    here_wide, here_narrow = lax.axis_index("wide"), lax.axis_index("narrow")
    feat = features.shape[3]
    slots = features.shape[2]
    classes = out_weight.shape[0]
    span_x, span_y = labels.shape
    rows_q = ROWS * narrow
    feats = features[0, 0]

    slot_ids = jnp.arange(slots, dtype=jnp.int32)
    halves = jnp.arange(2, dtype=jnp.int32)
    columns = jnp.arange(2 * wide, dtype=jnp.int32)
    listed = slot_ids < patch_count[0, 0]
    column_of = patch_ids[0, 0][:, None] // rows_q + halves[None, :]
    hit = listed[:, None, None] & (column_of[:, :, None] == columns[None, None, :])
    pick = jnp.max(
        jnp.where(hit, (2 * slot_ids[:, None] + halves[None, :])[:, :, None], -1), axis=(0, 1)
    )

    payloads = [pack(feats, pick, first, rows) for first, rows in CHUNKS]
    received = [
        lax.all_to_all(
            payload.reshape(wide, 2, feat, payload.shape[2]), "wide", 0, 0, tiled=True
        ).reshape(2 * wide, feat, payload.shape[2])
        for payload in payloads
    ]

    listing = jnp.concatenate([patch_ids[0, 0], patch_count[0]])
    listing = lax.all_gather(listing, "wide")
    all_ids, all_count = listing[:, :slots], listing[:, slots]
    all_listed = slot_ids[None, :] < all_count[:, None]
    mine = 2 * here_wide + halves
    all_column = (all_ids // rows_q)[:, :, None] + halves[None, None, :]
    match = all_listed[:, :, None, None] & (all_column[:, :, :, None] == mine)
    kind = (all_ids % rows_q - ROWS * here_narrow)[:, :, None] * 2 + halves[None, None, :]
    tag = jnp.max(jnp.where(match, kind[:, :, :, None], -1), axis=(1, 2)).reshape(-1)
    valid = tag >= 0
    order = jnp.cumsum(valid.astype(jnp.int32)) - 1
    code = jnp.where(valid, columns * 8 + tag, 0)
    place = valid[:, None] & (order[:, None] == columns[None, :])
    codes = jnp.concatenate(
        [
            jnp.sum(jnp.where(place, code[:, None], 0), axis=0),
            jnp.sum(valid.astype(jnp.int32))[None],
        ]
    )

    table = gauss_table()
    line = table[:, :PATCH]
    kinds = jnp.arange(2 * ROWS, dtype=jnp.int32)
    counts = jnp.sum(
        (tag.reshape(wide, 2, 1) == kinds).astype(jnp.float32), axis=0
    ).reshape(2, ROWS, 2)
    square = line.reshape(2, QUAD, PATCH)
    by_row = jnp.sum(
        counts[:, :, :, None, None] * square[None, None], axis=2
    )
    by_row = by_row.transpose(1, 0, 2, 3).reshape(ROWS, span_x, PATCH)
    norm = sum(
        jnp.pad(by_row[i], ((0, 0), (QUAD * i, QUAD * (ROWS - 1 - i)))) for i in range(ROWS)
    )
    came_low = shifted(norm[:, span_y - 2 :], "narrow", 1)
    came_high = shifted(norm[:, :2], "narrow", -1)
    norm = jnp.concatenate(
        [
            came_low[:, :2],
            norm[:, :QUAD] + came_low[:, 2:],
            norm[:, QUAD:span_y],
            norm[:, span_y : span_y + 2] + came_high,
        ],
        axis=1,
    )
    across = ROWS * QUAD * here_narrow - 2 + jnp.arange(span_y + 4, dtype=jnp.int32)
    inside = (across >= 0) & (across < narrow * span_y)
    inverse = ring_of(jnp.where(inside[None, :], 1.0 / (norm + 0.001), 0.0))

    label_wide = padded_2(labels + 1, (("wide", 0), ("narrow", 1)), 2)
    centre = label_wide[1:-1, 1:-1]
    same = (
        (label_wide[:-2, 1:-1] == centre)
        & (label_wide[2:, 1:-1] == centre)
        & (label_wide[1:-1, :-2] == centre)
        & (label_wide[1:-1, 2:] == centre)
    )
    boundary = jnp.where(same, 0, centre)
    boundary = ring_of(jnp.pad(boundary, ((0, 0), (1, 1))))

    head_weight = head_matrix(out_weight, out_bias)
    bias_tile = jnp.broadcast_to(mlp_bias[:, None], (feat, TILE))
    probs = []
    for (first, rows), recv in zip(CHUNKS, received):
        own, up, down = head_of(
            recv, codes, mlp_weight, bias_tile, head_weight, table, first, rows, classes
        )
        up = shifted(up, "narrow", 1)
        down = shifted(down, "narrow", -1)
        probs.append(blend_of(own, up, down, rows_of(inverse, first, rows)))
    edge_rows = CHUNKS[0][1]
    before = shifted(probs[0][2 * edge_rows - 2 :], "wide", 1)
    after = shifted(probs[0][:2], "wide", -1)
    pieces = [prob[:rows] for prob, (_, rows) in zip(probs, CHUNKS)]
    pieces += [prob[rows:] for prob, (_, rows) in zip(probs[::-1], CHUNKS[::-1])]
    prob = jnp.concatenate([before] + pieces + [after], axis=0)
    blended = prob[2:-2, :classes, :span_y].transpose(1, 0, 2)
    sums = dice_of(prob, boundary)[:, :classes, 0]
    slab_sums = (sums / jnp.float32(span_x)).reshape(1, 1, 2, classes)
    whole = lax.psum(sums, ("wide", "narrow"))
    dice = (whole[0] + 1.0) / (whole[1] + 1.0)
    return (blended, dice, slab_sums)


def solution(mesh):
    return jax.shard_map(
        on_device,
        mesh=mesh,
        in_specs=(
            P("wide", "narrow", None, None, None),
            P("wide", "narrow", None),
            P("wide", "narrow"),
            P("wide", "narrow"),
            P(),
            P(),
            P(),
            P(),
        ),
        out_specs=(P(None, "wide", "narrow"), P(), P("wide", "narrow", None, None)),
        check_vma=False,
    )
```

time: 1130 us -> 864 us (0.76)
  waiting for transfers between devices: 657 us -> 49.5 us
  Pallas kernels: 0 us -> 556 us
  local copies, waits for them, and re-layouts: 191 us -> 22.6 us
  blocking collectives: 66.8 us -> 174 us
  other arithmetic: 98 us -> 5.85 us
  matrix products: 50.6 us -> 0 us
    all_to_all x2 -> x3, waiting for transfers between devices: 633 us -> 0.01 us  [on_device(): lax.all_to_all(payload.reshape(wide, 2, feat, payload.shape[2]), 'wide',...]
    pallas_call x0 -> x10, Pallas kernels: none -> 556 us  [the longest x3 435 us: pack(): pl.pallas_call(functools.partial(pack_kernel, first, rows), out_shape=jax...]
    reshape x3 -> x1, local copies, waits for them, and re-layouts: 76.4 us -> 0.09 us  [on_device(): jnp.max(jnp.where(match, kind[:, :, :, None], -1), axis=(1, 2)).reshape(-1)]
    unnamed x0 -> x1, blocking collectives: none -> 68.5 us
    psum x1, blocking collectives: 66.8 us -> 106 us  [on_device(): whole = lax.psum(sums, ('wide', 'narrow'))]
    dot_general x4 -> x0, matrix products: 31.3 us -> none  [the longest x1 19.8 us: on_device(): jnp.einsum('st,scv->tcv', choose.astype(jnp.bfloat16), received, preferre...]
    select_n x5, other arithmetic: 28.3 us -> 1.03 us  [the longest x1 0.67 us: on_device(): column_of = patch_ids[0, 0][:, None] // rows_q + halves[None, :]]
    convert_element_type x5 -> x1, other arithmetic: 25.9 us -> 0.01 us  [on_device(): order = jnp.cumsum(valid.astype(jnp.int32)) - 1]
  transfers between devices with their start and end apart: 16 -> 17, of which waited for: 3 -> 4; matrix products, arithmetic and copies ran while one was open for 24% -> 1% of each run, Pallas kernels for 0% -> 44%
where the time goes in v1:
time: 864 us; the launch traced here: 868 us
  Pallas kernels  556 us (64%)
  blocking collectives  174 us (20%)
  starting transfers between devices  56.6 us (7%)
  waiting for transfers between devices  49.5 us (6%)
  local copies, waits for them, and re-layouts  22.6 us (3%)
    pallas_call x3, Pallas kernels, pack(): pl.pallas_call(functools.partial(pack_kernel, first, rows), out_shape=jax...  435 us
    psum x1, blocking collectives, on_device(): whole = lax.psum(sums, ('wide', 'narrow'))  106 us
    pallas_call x3, Pallas kernels, head_of(): pl.pallas_call(functools.partial(head_kernel, first, rows, classes), out_...  81.3 us
    unnamed x1, blocking collectives  68.5 us
    ppermute x14, waiting for transfers between devices, shifted(): return lax.ppermute(block, axis, pairs)  49.5 us
    ppermute x14, starting transfers between devices, shifted(): return lax.ppermute(block, axis, pairs)  37.5 us
    pallas_call x1, Pallas kernels, dice_of(): pl.pallas_call(dice_kernel, out_shape=jax.ShapeDtypeStruct((2, padded, TI...  27.8 us
    all_to_all x3, starting transfers between devices, on_device(): lax.all_to_all(payload.reshape(wide, 2, feat, payload.shape[2]), 'wide',...  19 us
  transfers between devices with their start and end apart: 17, of which 4 were waited for; matrix products, arithmetic and copies ran while one was open for 1% of the time, Pallas kernels for 44%

profile of v1, /device:TPU:1, one launch (start us, length us, event | category | flops | bytes accessed | tf_op | source)
XLA Modules:
  0.0 868.0 jit_solution(13957636308663036955)
XLA Ops:
  2.7 145.0 %pack.4 = bf16[32,48,1536]{2,1,0:T(8,128)(2,1)} custom-call(s32[32]{0:T(128)} %select_reduce_fusion.2.pick_ref, bf16[8,48,9216]{2,1,0:T(8,128)(2,1)} %bitcast.33), custom_call_target="tpu_custom_call" | custom-call | bytes 9437184 | tf_op jit(solution)/shard_map/pack/pallas_call | solution.py:40
  147.7 7.6 all-to-all-start.1
  155.3 145.0 %pack.3 = bf16[32,48,1536]{2,1,0:T(8,128)(2,1)} custom-call(s32[32]{0:T(128)} %select_reduce_fusion.2.pick_ref, bf16[8,48,9216]{2,1,0:T(8,128)(2,1)} %bitcast.34), custom_call_target="tpu_custom_call" | custom-call | bytes 9437184 | tf_op jit(solution)/shard_map/pack/pallas_call | solution.py:40
  300.3 6.7 all-to-all-start
  308.5 68.5 %all-reduce.6 = s32[144]{0:T(256)S(1)} all-reduce(s32[144]{0:T(256)S(1)} %add_dynamic-update-slice_fusion), channel_id=2, replica_groups=mesh['wide'=16,'narrow'=8] {'wide'}, use_global_device_ids=true, to_apply=%add.6 | all-reduce | flops 144 | bytes 1152
  378.0 7.9 collective-permute-start.3
  386.0 3.4 collective-permute-start.2
  389.4 145.0 %pack.5 = bf16[32,48,1536]{2,1,0:T(8,128)(2,1)} custom-call(s32[32]{0:T(128)} %select_reduce_fusion.2.pick_ref, bf16[8,48,9216]{2,1,0:T(8,128)(2,1)} %bitcast.35), custom_call_target="tpu_custom_call" | custom-call | bytes 9437184 | tf_op jit(solution)/shard_map/pack/pallas_call | solution.py:40
  534.5 4.7 all-to-all-start.2
  546.8 32.9 %collective-permute-done.10 = s32[2,192]{1,0:T(2,128)S(1)} collective-permute-done((s32[2,192]{1,0:T(2,128)S(1)}, s32[2,192]{1,0:T(2,128)S(1)}, u32[]{:S(2)}, u32[]{:S(2)}) %collective-permute-start.10) | collective-permute-done | bytes 1568 | tf_op jit(solution)/shard_map/ppermute | solution.py:314
  579.7 9.2 %collective-permute-done.11 = s32[2,192]{1,0:T(2,128)S(1)} collective-permute-done((s32[2,192]{1,0:T(2,128)S(1)}, s32[2,192]{1,0:T(2,128)S(1)}, u32[]{:S(2)}, u32[]{:S(2)}) %collective-permute-start.11) | collective-permute-done | bytes 1568 | tf_op jit(solution)/shard_map/ppermute | solution.py:314
  593.5 3.7 collective-permute-done.13
  598.1 27.1 %head.3 = (f32[32,120,256]{2,1,0:T(8,128)}, bf16[16,120,128]{2,1,0:T(8,128)(2,1)S(1)}, bf16[120,128]{1,0:T(8,128)(2,1)S(1)}) custom-call(s32[33]{0:T(128)S(1)} %pad_add_fusion.10.code_ref, bf16[32,48,1536]{2,1,0:T(8,128)(2,1)} %bitcast.7.recv_ref, bf16[48,48]{1,0:T(8,128)(2,1)S(1)} %copy-done, f32[48,128]{1,0:T(8,128)S(1)} %broadcast_in_dim.103.bias_ref, ...), custom_call_target="tpu_custom_call" | custom-call | flops 300000000 | bytes 8333333 | tf_op jit(solution)/shard_map/head/pallas_call | solution.py:149
  629.8 27.1 %head.4 = (f32[32,120,256]{2,1,0:T(8,128)}, bf16[16,120,128]{2,1,0:T(8,128)(2,1)S(1)}, bf16[120,128]{1,0:T(8,128)(2,1)S(1)}) custom-call(s32[33]{0:T(128)S(1)} %pad_add_fusion.10.code_ref, bf16[32,48,1536]{2,1,0:T(8,128)(2,1)} %bitcast.17.recv_ref, bf16[48,48]{1,0:T(8,128)(2,1)S(1)} %copy-done, f32[48,128]{1,0:T(8,128)S(1)} %broadcast_in_dim.103.bias_ref, ...), custom_call_target="tpu_custom_call" | custom-call | flops 300000000 | bytes 8333333 | tf_op jit(solution)/shard_map/head/pallas_call | solution.py:149
  656.9 3.6 collective-permute-start.4
  660.6 27.1 %head.5 = (f32[32,120,256]{2,1,0:T(8,128)}, bf16[16,120,128]{2,1,0:T(8,128)(2,1)S(1)}, bf16[120,128]{1,0:T(8,128)(2,1)S(1)}) custom-call(s32[33]{0:T(128)S(1)} %pad_add_fusion.10.code_ref, bf16[32,48,1536]{2,1,0:T(8,128)(2,1)} %bitcast.19.recv_ref, bf16[48,48]{1,0:T(8,128)(2,1)S(1)} %copy-done, f32[48,128]{1,0:T(8,128)S(1)} %broadcast_in_dim.103.bias_ref, ...), custom_call_target="tpu_custom_call" | custom-call | flops 300000000 | bytes 8333333 | tf_op jit(solution)/shard_map/head/pallas_call | solution.py:149
  690.6 4.1 blend.3
  700.0 3.7 collective-permute-done.5.down_ref
  705.0 4.1 blend.4
  709.1 4.1 blend.5
  719.2 27.8 %dice.1 = f32[2,120,128]{2,1,0:T(8,128)S(1)} custom-call(bf16[100,120,256]{2,1,0:T(8,128)(2,1)} %copy-done.2, s32[98,256]{1,0:T(8,128)S(1)} %pad_add_fusion.8.label_ref), custom_call_target="tpu_custom_call" | custom-call | flops 92160000 | bytes 6144000 | tf_op jit(solution)/shard_map/dice/pallas_call | solution.py:293
  747.6 106.0 %psum.7 = f32[2,118]{1,0:T(2,128)S(1)} all-reduce(f32[2,118]{1,0:T(2,128)S(1)} %get-tuple-element.37), channel_id=1, replica_groups=mesh['wide'=16,'narrow'=8] {'wide','narrow'}, use_global_device_ids=true, to_apply=%region_7.8 | all-reduce | flops 236 | bytes 1888 | tf_op jit(solution)/shard_map/psum | solution.py:472
  854.1 5.6 slice_bitcast_fusion
  859.7 8.2 copy.49
  (128 shorter events, 37.2 us)
Async XLA Ops:
  147.7 152.7 %all-to-all-start.1 = ((bf16[16,2,48,1536]{3,2,1,0:T(8,128)(2,1)}), bf16[16,2,48,1536]{3,2,1,0:T(8,128)(2,1)}, u32[]{:S(2)}, u32[]{:S(2)}) async-start(bf16[16,2,48,1536]{3,2,1,0:T(8,128)(2,1)} %bitcast.38), calls=%async_computation.1 | async-start | bytes 9437184 | tf_op jit(solution)/shard_map/all_to_all | solution.py:387
  300.3 6.7 copy-start.8
  300.3 8.0 copy-start.6
  300.3 234.1 %all-to-all-start = ((bf16[16,2,48,1536]{3,2,1,0:T(8,128)(2,1)}), bf16[16,2,48,1536]{3,2,1,0:T(8,128)(2,1)}, u32[]{:S(2)}, u32[]{:S(2)}) async-start(bf16[16,2,48,1536]{3,2,1,0:T(8,128)(2,1)} %bitcast.37), calls=%async_computation | async-start | bytes 9437184 | tf_op jit(solution)/shard_map/all_to_all | solution.py:387
  378.0 215.4 %collective-permute-start.3 = (f32[96,2]{1,0:T(8,128)S(1)}, f32[96,2]{1,0:T(8,128)S(1)}, u32[]{:S(2)}, u32[]{:S(2)}) collective-permute-start(f32[96,2]{1,0:T(8,128)S(1)} %slice.194), channel_id=1, source_target_pairs={{1,0},{2,1},{3,2},{4,3},{5,4},{6,5},{7,6},{9,8},{10,9},{11,10},{12... | collective-permute-start | bytes 2312 | tf_op jit(solution)/shard_map/ppermute | solution.py:314
  386.0 211.7 %collective-permute-start.2 = (f32[96,50]{1,0:T(8,128)S(1)}, f32[96,50]{1,0:T(8,128)S(1)}, u32[]{:S(2)}, u32[]{:S(2)}) collective-permute-start(f32[96,50]{1,0:T(8,128)S(1)} %slice.188), channel_id=1, source_target_pairs={{0,1},{1,2},{2,3},{3,4},{4,5},{5,6},{6,7},{8,9},{9,10},{10,11},{11... | collective-permute-start | bytes 57608 | tf_op jit(solution)/shard_map/ppermute | solution.py:314
  534.5 4.8 copy-start.3
  534.5 9.6 %copy-start.7 = (f32[118]{0:T(128)S(1)}, f32[118]{0:T(128)}, u32[]{:S(2)}) copy-start(f32[118]{0:T(128)} %param.15) | copy-start | bytes 1420
  534.5 10.1 %copy-start.4 = (bf16[118,48]{0,1:T(8,128)(2,1)S(1)}, bf16[118,48]{0,1:T(8,128)(2,1)}, u32[]{:S(2)}) copy-start(bf16[118,48]{0,1:T(8,128)(2,1)} %param.14) | copy-start | bytes 33988
  534.5 63.5 %copy-start.5 = (f32[48]{0:T(128)S(1)}, f32[48]{0:T(128)}, u32[]{:S(2)}) copy-start(f32[48]{0:T(128)} %param.13) | copy-start | bytes 580
  534.5 63.6 %copy-start = (bf16[48,48]{1,0:T(8,128)(2,1)S(1)}, bf16[48,48]{1,0:T(8,128)(2,1)}, u32[]{:S(2)}) copy-start(bf16[48,48]{1,0:T(8,128)(2,1)} %mlp_ref.5) | copy-start | bytes 13828
  534.5 126.0 %all-to-all-start.2 = ((bf16[16,2,48,1536]{3,2,1,0:T(8,128)(2,1)}), bf16[16,2,48,1536]{3,2,1,0:T(8,128)(2,1)}, u32[]{:S(2)}, u32[]{:S(2)}) async-start(bf16[16,2,48,1536]{3,2,1,0:T(8,128)(2,1)} %bitcast.36), calls=%async_computation.2 | async-start | bytes 9437184 | tf_op jit(solution)/shard_map/all_to_all | solution.py:387
  539.3 40.4 %collective-permute-start.10 = (s32[2,192]{1,0:T(2,128)S(1)}, s32[2,192]{1,0:T(2,128)S(1)}, u32[]{:S(2)}, u32[]{:S(2)}) collective-permute-start(s32[2,192]{1,0:T(2,128)S(1)} %get-tuple-element.56), channel_id=1, source_target_pairs={{0,8},{8,16},{16,24},{24,32},{32,40},{40,48},{48,56},{56,64},{64,7... | collective-permute-start | bytes 4616 | tf_op jit(solution)/shard_map/ppermute | solution.py:314
  542.4 46.6 %collective-permute-start.11 = (s32[2,192]{1,0:T(2,128)S(1)}, s32[2,192]{1,0:T(2,128)S(1)}, u32[]{:S(2)}, u32[]{:S(2)}) collective-permute-start(s32[2,192]{1,0:T(2,128)S(1)} %get-tuple-element.57), channel_id=1, source_target_pairs={{8,0},{16,8},{24,16},{32,24},{40,32},{48,40},{56,48},{64,56},{72,6... | collective-permute-start | bytes 4616 | tf_op jit(solution)/shard_map/ppermute | solution.py:314
  589.1 4.4 collective-permute-start.12
  591.0 6.2 collective-permute-start.13
  625.2 65.4 %collective-permute-start = (bf16[16,120,128]{2,1,0:T(8,128)(2,1)S(1)}, bf16[16,120,128]{2,1,0:T(8,128)(2,1)S(1)}, u32[]{:S(2)}, u32[]{:S(2)}) collective-permute-start(bf16[16,120,128]{2,1,0:T(8,128)(2,1)S(1)} %get-tuple-element.13), channel_id=1, source_target_pairs={{0,1},{1,2},{2,3},{3,4},{4,5},{5,6},{6,7},{8,9},{9,10},{10,11},{11... | collective-permute-start | bytes 1474568 | tf_op jit(solution)/shard_map/ppermute | solution.py:314
  627.9 62.7 %collective-permute-start.1 = (bf16[120,128]{1,0:T(8,128)(2,1)S(1)}, bf16[120,128]{1,0:T(8,128)(2,1)S(1)}, u32[]{:S(2)}, u32[]{:S(2)}) collective-permute-start(bf16[120,128]{1,0:T(8,128)(2,1)S(1)} %get-tuple-element.14), channel_id=1, source_target_pairs={{1,0},{2,1},{3,2},{4,3},{5,4},{6,5},{7,6},{9,8},{10,9},{11,10},{12... | collective-permute-start | bytes 92168 | tf_op jit(solution)/shard_map/ppermute | solution.py:314
  656.9 48.0 %collective-permute-start.4 = (bf16[16,120,128]{2,1,0:T(8,128)(2,1)S(1)}, bf16[16,120,128]{2,1,0:T(8,128)(2,1)S(1)}, u32[]{:S(2)}, u32[]{:S(2)}) collective-permute-start(bf16[16,120,128]{2,1,0:T(8,128)(2,1)S(1)} %get-tuple-element.16), channel_id=1, source_target_pairs={{0,1},{1,2},{2,3},{3,4},{4,5},{5,6},{6,7},{8,9},{9,10},{10,11},{11... | collective-permute-start | bytes 1474568 | tf_op jit(solution)/shard_map/ppermute | solution.py:314
  687.6 21.4 %collective-permute-start.6 = (bf16[16,120,128]{2,1,0:T(8,128)(2,1)S(1)}, bf16[16,120,128]{2,1,0:T(8,128)(2,1)S(1)}, u32[]{:S(2)}, u32[]{:S(2)}) collective-permute-start(bf16[16,120,128]{2,1,0:T(8,128)(2,1)S(1)} %get-tuple-element.19), channel_id=1, source_target_pairs={{0,1},{1,2},{2,3},{3,4},{4,5},{5,6},{6,7},{8,9},{9,10},{10,11},{11... | collective-permute-start | bytes 1474568 | tf_op jit(solution)/shard_map/ppermute | solution.py:314
  694.7 18.4 %collective-permute-start.8 = (bf16[2,120,256]{2,1,0:T(8,128)(2,1)S(1)}, bf16[2,120,256]{2,1,0:T(8,128)(2,1)S(1)}, u32[]{:S(2)}, u32[]{:S(2)}) collective-permute-start(bf16[2,120,256]{2,1,0:T(8,128)(2,1)S(1)} %get-tuple-element.39), channel_id=1, source_target_pairs={{0,8},{8,16},{16,24},{24,32},{32,40},{40,48},{48,56},{56,64},{64,7... | collective-permute-start | bytes 368648 | tf_op jit(solution)/shard_map/ppermute | solution.py:314
  696.1 7.6 collective-permute-start.5
  698.0 11.0 %collective-permute-start.7 = (bf16[120,128]{1,0:T(8,128)(2,1)S(1)}, bf16[120,128]{1,0:T(8,128)(2,1)S(1)}, u32[]{:S(2)}, u32[]{:S(2)}) collective-permute-start(bf16[120,128]{1,0:T(8,128)(2,1)S(1)} %get-tuple-element.20), channel_id=1, source_target_pairs={{1,0},{2,1},{3,2},{4,3},{5,4},{6,5},{7,6},{9,8},{10,9},{11,10},{12... | collective-permute-start | bytes 92168 | tf_op jit(solution)/shard_map/ppermute | solution.py:314
  703.7 10.3 %collective-permute-start.9 = (bf16[2,120,256]{2,1,0:T(8,128)(2,1)S(1)}, bf16[2,120,256]{2,1,0:T(8,128)(2,1)S(1)}, u32[]{:S(2)}, u32[]{:S(2)}) collective-permute-start(bf16[2,120,256]{2,1,0:T(8,128)(2,1)S(1)} %get-tuple-element.38), channel_id=1, source_target_pairs={{8,0},{16,8},{24,16},{32,24},{40,32},{48,40},{56,48},{64,56},{72,6... | collective-permute-start | bytes 368648 | tf_op jit(solution)/shard_map/ppermute | solution.py:314
  (2 other events, 5.2 us)

commit v2 on v1

--- a/solution.py
+++ b/solution.py
@@ -20,7 +20,7 @@
     width = rows * PATCH
 
     def copy_of(column):
-        source = jnp.maximum(pick_ref[column], 0)
+        source = pick_ref[column]
         start = first if column % 2 == 0 else QUAD - first - rows
         lane = pl.multiple_of((source % 2) * (QUAD * PATCH) + start * PATCH, TILE)
         return pltpu.make_async_copy(
@@ -29,9 +29,16 @@
 
     columns = out_ref.shape[0]
     for column in range(columns):
-        copy_of(column).start()
+
+        @pl.when(pick_ref[column] >= 0)
+        def _():
+            copy_of(column).start()
+
     for column in range(columns):
-        copy_of(column).wait()
+
+        @pl.when(pick_ref[column] >= 0)
+        def _():
+            copy_of(column).wait()
 
 
 def pack(feats, pick, first, rows):
@@ -41,8 +48,9 @@
         functools.partial(pack_kernel, first, rows),
         out_shape=jax.ShapeDtypeStruct((columns, feats.shape[1], width), feats.dtype),
         in_specs=[pl.BlockSpec(memory_space=pltpu.SMEM), pl.BlockSpec(memory_space=pl.ANY)],
-        out_specs=pl.BlockSpec(memory_space=pl.ANY),
+        out_specs=pl.BlockSpec(memory_space=pltpu.VMEM),
         scratch_shapes=[pltpu.SemaphoreType.DMA((columns,))],
+        compiler_params=pltpu.CompilerParams(vmem_limit_bytes=VMEM_LIMIT),
         cost_estimate=pl.CostEstimate(
             flops=0, bytes_accessed=columns * width * feats.shape[1] * 4, transcendentals=0
         ),
@@ -62,7 +70,7 @@
 
 def head_kernel(
     first, rows, classes, code_ref, recv_ref, mlp_ref, bias_ref, head_ref, gauss_ref,
-    own_ref, up_ref, down_ref, acc_ref, edge_ref,
+    own_ref, up_ref, down_ref, acc_ref, edge_ref, act_ref,
 ):
     feat = recv_ref.shape[1]
     padded = head_ref.shape[0]
@@ -71,7 +79,7 @@
     real = lax.broadcasted_iota(jnp.int32, (padded, TILE), 0) < classes
     mlp = mlp_ref[...]
     head = head_ref[...]
-    extra = jnp.ones((head.shape[1] - feat, 4 * TILE), jnp.bfloat16)
+    act_ref[feat:, :] = jnp.ones((act_ref.shape[0] - feat, act_ref.shape[1]), jnp.bfloat16)
 
     @pl.loop(0, ROWS)
     def _(which):
@@ -88,32 +96,28 @@
         which = (code // 2) % 4
         side = slot % 2
         start = (code % 2) * QUAD + jnp.where(side == 0, first, QUAD - first - rows)
+        flat = recv_ref[slot]
+        hidden = jnp.dot(mlp, flat, preferred_element_type=jnp.float32)
         for group in range(rows // 4):
-            at = group * 3 * TILE
-            tiles = [
-                recv_ref[slot, :, at + i * TILE : at + (i + 1) * TILE].astype(jnp.float32)
-                for i in range(3)
-            ]
-            voxels = jnp.concatenate(spread_rows(tiles, lane_feat), axis=1)
-            hidden = jnp.dot(
-                mlp, voxels.astype(jnp.bfloat16), preferred_element_type=jnp.float32
+            tiles = []
+            for i in range(3):
+                part = slice((group * 3 + i) * TILE, (group * 3 + i + 1) * TILE)
+                tiles.append(
+                    flat[:, part].astype(jnp.float32)
+                    + jnp.maximum(hidden[:, part] + bias_ref[...], 0.0)
+                )
+            for i, tile in enumerate(spread_rows(tiles, lane_feat)):
+                at = (group * 4 + i) * TILE
+                act_ref[0:feat, at : at + TILE] = tile.astype(jnp.bfloat16)
+        logits = jnp.dot(head, act_ref[...], preferred_element_type=jnp.float32)
+        for i in range(rows):
+            part = logits[:, i * TILE : (i + 1) * TILE]
+            top = jnp.max(part, axis=0, keepdims=True)
+            raised = jnp.where(real, jnp.exp(part - top), 0.0)
+            scale = gauss_ref[pl.ds(start + i, 1), :] / jnp.sum(raised, axis=0, keepdims=True)
+            acc_ref[which, side * rows + i] += (
+                (raised * scale).astype(jnp.bfloat16).astype(jnp.float32)
             )
-            bias = jnp.concatenate([bias_ref[...]] * 4, axis=1)
-            active = (voxels + jnp.maximum(hidden + bias, 0.0)).astype(jnp.bfloat16)
-            logits = jnp.dot(
-                head, jnp.concatenate([active, extra], axis=0), preferred_element_type=jnp.float32
-            )
-            for i in range(4):
-                part = logits[:, i * TILE : (i + 1) * TILE]
-                top = jnp.max(part, axis=0, keepdims=True)
-                raised = jnp.where(real, jnp.exp(part - top), 0.0)
-                scale = gauss_ref[pl.ds(start + group * 4 + i, 1), :] / jnp.sum(
-                    raised, axis=0, keepdims=True
-                )
-                row = side * rows + group * 4 + i
-                acc_ref[which, row] += (
-                    (raised * scale).astype(jnp.bfloat16).astype(jnp.float32)
-                )
 
     def merged(row):
         a0, a1, a2, a3 = [acc_ref[which, row] for which in range(ROWS)]
@@ -158,6 +162,7 @@
         scratch_shapes=[
             pltpu.VMEM((ROWS, 2 * rows, padded, TILE), jnp.float32),
             pltpu.VMEM((padded, TILE), jnp.float32),
+            pltpu.VMEM((head_weight.shape[1], rows * TILE), jnp.bfloat16),
         ],
         compiler_params=pltpu.CompilerParams(vmem_limit_bytes=VMEM_LIMIT),
         cost_estimate=pl.CostEstimate(
@@ -308,6 +313,60 @@
     )(prob, label)
 
 
+def emit_kernel(low, high, prob_ref, *refs):
+    out_ref, turned_ref, sems = refs[-3:]
+    rows, padded, _ = prob_ref.shape
+    classes, _, span_y = out_ref.shape
+    half = rows // 2
+
+    @pl.loop(0, padded // 8)
+    def _(index):
+        group = pl.multiple_of(index * 8, 8)
+        for at in range(0, rows, 8):
+            for i in range(2):
+                lanes = slice(i * TILE, min((i + 1) * TILE, span_y))
+                block = prob_ref[at : at + 8, pl.ds(group, 8), i * TILE : (i + 1) * TILE]
+                block = jnp.transpose(block.astype(jnp.float32), (1, 0, 2))
+                turned_ref[pl.ds(group, 8), at : at + 8, lanes] = block[
+                    :, :, : lanes.stop - lanes.start
+                ].astype(jnp.bfloat16)
+
+    copies = [
+        pltpu.make_async_copy(
+            turned_ref.at[pl.ds(0, classes), pl.ds(i * half, half), :],
+            out_ref.at[:, pl.ds(at, half), :],
+            sems.at[i],
+        )
+        for i, at in enumerate((low, high))
+    ]
+    for copy in copies:
+        copy.start()
+    for copy in copies:
+        copy.wait()
+
+
+def emit(prob, low, high, shape, out=None):
+    rows, padded, _ = prob.shape
+    anywhere = pl.BlockSpec(memory_space=pl.ANY)
+    before = () if out is None else (out,)
+    return pl.pallas_call(
+        functools.partial(emit_kernel, low, high),
+        out_shape=jax.ShapeDtypeStruct(shape, prob.dtype),
+        in_specs=[pl.BlockSpec(memory_space=pltpu.VMEM)] + [anywhere] * len(before),
+        out_specs=anywhere,
+        input_output_aliases={1: 0} if before else {},
+        scratch_shapes=[
+            pltpu.VMEM((padded, rows, shape[2]), prob.dtype),
+            pltpu.SemaphoreType.DMA((2,)),
+        ],
+        compiler_params=pltpu.CompilerParams(vmem_limit_bytes=VMEM_LIMIT),
+        cost_estimate=pl.CostEstimate(
+            flops=prob.size * 4, bytes_accessed=prob.size * 4, transcendentals=0
+        ),
+        name="emit",
+    )(prob, *before)
+
+
 def shifted(block, axis, by):
     devices = lax.axis_size(axis)
     pairs = [(i, i + by) for i in range(devices) if 0 <= i + by < devices]
@@ -390,15 +449,9 @@
         for payload in payloads
     ]
 
-    listing = jnp.concatenate([patch_ids[0, 0], patch_count[0]])
-    listing = lax.all_gather(listing, "wide")
-    all_ids, all_count = listing[:, :slots], listing[:, slots]
-    all_listed = slot_ids[None, :] < all_count[:, None]
-    mine = 2 * here_wide + halves
-    all_column = (all_ids // rows_q)[:, :, None] + halves[None, None, :]
-    match = all_listed[:, :, None, None] & (all_column[:, :, :, None] == mine)
-    kind = (all_ids % rows_q - ROWS * here_narrow)[:, :, None] * 2 + halves[None, None, :]
-    tag = jnp.max(jnp.where(match, kind[:, :, :, None], -1), axis=(1, 2)).reshape(-1)
+    kind = (patch_ids[0, 0] % rows_q - ROWS * here_narrow)[:, None] * 2 + halves[None, :]
+    tag = jnp.max(jnp.where(hit, kind[:, :, None], -1), axis=(0, 1)).reshape(wide, 2)
+    tag = lax.all_to_all(tag, "wide", 0, 0, tiled=True).reshape(-1)
     valid = tag >= 0
     order = jnp.cumsum(valid.astype(jnp.int32)) - 1
     code = jnp.where(valid, columns * 8 + tag, 0)
@@ -453,24 +506,36 @@
     head_weight = head_matrix(out_weight, out_bias)
     bias_tile = jnp.broadcast_to(mlp_bias[:, None], (feat, TILE))
     probs = []
+    blended = None
     for (first, rows), recv in zip(CHUNKS, received):
         own, up, down = head_of(
             recv, codes, mlp_weight, bias_tile, head_weight, table, first, rows, classes
         )
         up = shifted(up, "narrow", 1)
         down = shifted(down, "narrow", -1)
-        probs.append(blend_of(own, up, down, rows_of(inverse, first, rows)))
+        prob = blend_of(own, up, down, rows_of(inverse, first, rows))
+        probs.append(prob)
+        blended = emit(
+            prob, first, span_x - first - rows, (classes, span_x, span_y), blended
+        )
     edge_rows = CHUNKS[0][1]
     before = shifted(probs[0][2 * edge_rows - 2 :], "wide", 1)
     after = shifted(probs[0][:2], "wide", -1)
-    pieces = [prob[:rows] for prob, (_, rows) in zip(probs, CHUNKS)]
-    pieces += [prob[rows:] for prob, (_, rows) in zip(probs[::-1], CHUNKS[::-1])]
-    prob = jnp.concatenate([before] + pieces + [after], axis=0)
-    blended = prob[2:-2, :classes, :span_y].transpose(1, 0, 2)
-    sums = dice_of(prob, boundary)[:, :classes, 0]
-    slab_sums = (sums / jnp.float32(span_x)).reshape(1, 1, 2, classes)
-    whole = lax.psum(sums, ("wide", "narrow"))
-    dice = (whole[0] + 1.0) / (whole[1] + 1.0)
+    last, last_rows = CHUNKS[-1]
+    lows = [prob[:rows] for prob, (_, rows) in zip(probs, CHUNKS)]
+    highs = [prob[rows:] for prob, (_, rows) in zip(probs, CHUNKS)]
+    low = jnp.concatenate([before] + lows[:-1], axis=0)
+    high = jnp.concatenate(highs[:-1][::-1] + [after], axis=0)
+    middle = jnp.concatenate([lows[-2][-4:], probs[-1], highs[-2][:4]], axis=0)
+    sums = (
+        dice_of(low, boundary[:last])
+        + dice_of(high, boundary[span_x - last + 2 :])
+        + dice_of(middle, boundary[last - 2 : span_x - last + 4])
+    )[:, :, 0]
+    whole = jnp.broadcast_to(sums[None], (wide * narrow,) + sums.shape)
+    whole = jnp.sum(lax.all_to_all(whole, ("wide", "narrow"), 0, 0, tiled=True), axis=0)
+    dice = ((whole[0] + 1.0) / (whole[1] + 1.0))[:classes]
+    slab_sums = (sums[:, :classes] / jnp.float32(span_x)).reshape(1, 1, 2, classes)
     return (blended, dice, slab_sums)
 
 

time: 864 us -> 367 us (0.42)
  Pallas kernels: 556 us -> 113 us
  blocking collectives: 174 us -> 0 us
  waiting for transfers between devices: 49.5 us -> 115 us
  starting transfers between devices: 56.6 us -> 108 us
    pallas_call x3, Pallas kernels: 435 us -> 14.1 us  [pack(): pl.pallas_call(functools.partial(pack_kernel, first, rows), out_shape=jax...]
    psum x1 -> x0, blocking collectives: 106 us -> none  [on_device(): whole = lax.psum(sums, ('wide', 'narrow'))]
    all_to_all x3, waiting for transfers between devices: 0.01 us -> 101 us  [on_device(): lax.all_to_all(payload.reshape(wide, 2, feat, payload.shape[2]), 'wide',...]
    unnamed x1 -> x0, blocking collectives: 68.5 us -> none
    ppermute x14, waiting for transfers between devices: 49.5 us -> 3.86 us  [shifted(): return lax.ppermute(block, axis, pairs)]
    all_to_all x0 -> x2, starting transfers between devices: none -> 30.6 us  [the longest x1 23.1 us: on_device(): lax.all_to_all(whole, ('wide', 'narrow'), 0, 0, tiled=True)]
    pallas_call x3, Pallas kernels: 81.3 us -> 54.1 us  [head_of(): pl.pallas_call(functools.partial(head_kernel, first, rows, classes), out_...]
    ppermute x14, starting transfers between devices: 37.5 us -> 53 us  [shifted(): return lax.ppermute(block, axis, pairs)]
  transfers between devices with their start and end apart: 17 -> 19, of which waited for: 4 -> 5; matrix products, arithmetic and copies ran while one was open for 1% -> 6% of each run, Pallas kernels for 44% -> 29%
where the time goes in v2:
time: 367 us; the launch traced here: 362 us
  waiting for transfers between devices  115 us (31%)
  Pallas kernels  113 us (31%)
  starting transfers between devices  108 us (29%)
  local copies, waits for them, and re-layouts  17.1 us (5%)
  other arithmetic  7.14 us (2%)
    all_to_all x3, waiting for transfers between devices, on_device(): lax.all_to_all(payload.reshape(wide, 2, feat, payload.shape[2]), 'wide',...  101 us
    pallas_call x3, Pallas kernels, head_of(): pl.pallas_call(functools.partial(head_kernel, first, rows, classes), out_...  54.1 us
    ppermute x14, starting transfers between devices, shifted(): return lax.ppermute(block, axis, pairs)  53 us
    pallas_call x3, Pallas kernels, dice_of(): pl.pallas_call(dice_kernel, out_shape=jax.ShapeDtypeStruct((2, padded, TI...  25.7 us
    all_to_all x3, starting transfers between devices, on_device(): lax.all_to_all(payload.reshape(wide, 2, feat, payload.shape[2]), 'wide',...  24 us
    all_to_all x1, starting transfers between devices, on_device(): lax.all_to_all(whole, ('wide', 'narrow'), 0, 0, tiled=True)  23.1 us
    pallas_call x3, Pallas kernels, pack(): pl.pallas_call(functools.partial(pack_kernel, first, rows), out_shape=jax...  14.1 us
    pallas_call x3, Pallas kernels, blend_of(): pl.pallas_call(blend_kernel, out_shape=jax.ShapeDtypeStruct(own.shape, jn...  12.2 us
  transfers between devices with their start and end apart: 19, of which 5 were waited for; matrix products, arithmetic and copies ran while one was open for 6% of the time, Pallas kernels for 29%

profile of v2, /device:TPU:1, one launch (start us, length us, event | category | flops | bytes accessed | tf_op | source)
XLA Modules:
  0.0 362.3 jit_solution(16340593269832152253)
XLA Ops:
  2.8 7.6 %all-to-all-start = ((s32[16,1,2]{2,1,0:T(1,128)}), s32[16,1,2]{2,1,0:T(1,128)S(1)}, u32[]{:S(2)}, u32[]{:S(2)}) async-start(s32[16,1,2]{2,1,0:T(1,128)} %bitcast.2), calls=%async_computation | async-start | bytes 16384 | tf_op jit(solution)/shard_map/all_to_all | solution.py:454
  10.4 4.7 %pack.5 = bf16[32,48,1536]{2,1,0:T(8,128)(2,1)} custom-call(s32[32]{0:T(128)S(1)} %get-tuple-element.38.pick_ref, bf16[8,48,9216]{2,1,0:T(8,128)(2,1)} %bitcast.44), custom_call_target="tpu_custom_call" | custom-call | bytes 9437184 | tf_op jit(solution)/shard_map/pack/pallas_call | solution.py:47
  16.8 4.9 %all-to-all-start.3 = ((bf16[16,2,48,1536]{3,2,1,0:T(8,128)(2,1)}), bf16[16,2,48,1536]{3,2,1,0:T(8,128)(2,1)}, u32[]{:S(2)}, u32[]{:S(2)}) async-start(bf16[16,2,48,1536]{3,2,1,0:T(8,128)(2,1)} %bitcast.49), calls=%async_computation.3 | async-start | bytes 9437184 | tf_op jit(solution)/shard_map/all_to_all | solution.py:446
  21.7 4.7 %pack.4 = bf16[32,48,1536]{2,1,0:T(8,128)(2,1)} custom-call(s32[32]{0:T(128)S(1)} %get-tuple-element.38.pick_ref, bf16[8,48,9216]{2,1,0:T(8,128)(2,1)} %bitcast.45), custom_call_target="tpu_custom_call" | custom-call | bytes 9437184 | tf_op jit(solution)/shard_map/pack/pallas_call | solution.py:47
  26.5 55.2 %all-to-all-done.3 = bf16[16,2,48,1536]{3,2,1,0:T(8,128)(2,1)} async-done(((bf16[16,2,48,1536]{3,2,1,0:T(8,128)(2,1)}), bf16[16,2,48,1536]{3,2,1,0:T(8,128)(2,1)}, u32[]{:S(2)}, u32[]{:S(2)}) %all-to-all-start.3) | async-done | bytes 4718624 | tf_op jit(solution)/shard_map/all_to_all | solution.py:446
  81.7 12.9 %all-to-all-start.2 = ((bf16[16,2,48,1536]{3,2,1,0:T(8,128)(2,1)}), bf16[16,2,48,1536]{3,2,1,0:T(8,128)(2,1)}, u32[]{:S(2)}, u32[]{:S(2)}) async-start(bf16[16,2,48,1536]{3,2,1,0:T(8,128)(2,1)} %bitcast.48), calls=%async_computation.2 | async-start | bytes 9437184 | tf_op jit(solution)/shard_map/all_to_all | solution.py:446
  100.0 4.7 %pack.3 = bf16[32,48,1536]{2,1,0:T(8,128)(2,1)} custom-call(s32[32]{0:T(128)S(1)} %get-tuple-element.38.pick_ref, bf16[8,48,9216]{2,1,0:T(8,128)(2,1)} %bitcast.46), custom_call_target="tpu_custom_call" | custom-call | bytes 9437184 | tf_op jit(solution)/shard_map/pack/pallas_call | solution.py:47
  105.7 45.3 %all-to-all-done.2 = bf16[16,2,48,1536]{3,2,1,0:T(8,128)(2,1)} async-done(((bf16[16,2,48,1536]{3,2,1,0:T(8,128)(2,1)}), bf16[16,2,48,1536]{3,2,1,0:T(8,128)(2,1)}, u32[]{:S(2)}, u32[]{:S(2)}) %all-to-all-start.2) | async-done | bytes 4718624 | tf_op jit(solution)/shard_map/all_to_all | solution.py:446
  151.0 6.1 %all-to-all-start.1 = ((bf16[16,2,48,1536]{3,2,1,0:T(8,128)(2,1)}), bf16[16,2,48,1536]{3,2,1,0:T(8,128)(2,1)}, u32[]{:S(2)}, u32[]{:S(2)}) async-start(bf16[16,2,48,1536]{3,2,1,0:T(8,128)(2,1)} %bitcast.47), calls=%async_computation.1 | async-start | bytes 9437184 | tf_op jit(solution)/shard_map/all_to_all | solution.py:446
  158.0 11.2 %collective-permute-start.2 = (f32[96,50]{1,0:T(8,128)S(1)}, f32[96,50]{1,0:T(8,128)S(1)}, u32[]{:S(2)}, u32[]{:S(2)}) collective-permute-start(f32[96,50]{1,0:T(8,128)S(1)} %slice.201), channel_id=1, source_target_pairs={{0,1},{1,2},{2,3},{3,4},{4,5},{5,6},{6,7},{8,9},{9,10},{10,11},{11... | collective-permute-start | bytes 57608 | tf_op jit(solution)/shard_map/ppermute | solution.py:373
  184.9 18.0 %head.5 = (f32[32,120,256]{2,1,0:T(8,128)}, bf16[16,120,128]{2,1,0:T(8,128)(2,1)S(1)}, bf16[120,128]{1,0:T(8,128)(2,1)S(1)}) custom-call(s32[33]{0:T(128)S(1)} %pad_add_fusion.10.code_ref, bf16[32,48,1536]{2,1,0:T(8,128)(2,1)} %bitcast.19.recv_ref, bf16[48,48]{1,0:T(8,128)(2,1)S(1)} %copy-done, f32[48,128]{1,0:T(8,128)S(1)} %broadcast_in_dim.97.bias_ref, ...), custom_call_target="tpu_custom_call" | custom-call | flops 300000000 | bytes 8333333 | tf_op jit(solution)/shard_map/head/pallas_call | solution.py:153
  202.8 6.1 %collective-permute-start.6 = (bf16[16,120,128]{2,1,0:T(8,128)(2,1)S(1)}, bf16[16,120,128]{2,1,0:T(8,128)(2,1)S(1)}, u32[]{:S(2)}, u32[]{:S(2)}) collective-permute-start(bf16[16,120,128]{2,1,0:T(8,128)(2,1)S(1)} %get-tuple-element.19), channel_id=1, source_target_pairs={{0,1},{1,2},{2,3},{3,4},{4,5},{5,6},{6,7},{8,9},{9,10},{10,11},{11... | collective-permute-start | bytes 1474568 | tf_op jit(solution)/shard_map/ppermute | solution.py:373
  209.0 18.1 %head.4 = (f32[32,120,256]{2,1,0:T(8,128)}, bf16[16,120,128]{2,1,0:T(8,128)(2,1)S(1)}, bf16[120,128]{1,0:T(8,128)(2,1)S(1)}) custom-call(s32[33]{0:T(128)S(1)} %pad_add_fusion.10.code_ref, bf16[32,48,1536]{2,1,0:T(8,128)(2,1)} %bitcast.17.recv_ref, bf16[48,48]{1,0:T(8,128)(2,1)S(1)} %copy-done, f32[48,128]{1,0:T(8,128)S(1)} %broadcast_in_dim.97.bias_ref, ...), custom_call_target="tpu_custom_call" | custom-call | flops 300000000 | bytes 8333333 | tf_op jit(solution)/shard_map/head/pallas_call | solution.py:153
  227.0 6.4 %collective-permute-start.4 = (bf16[16,120,128]{2,1,0:T(8,128)(2,1)S(1)}, bf16[16,120,128]{2,1,0:T(8,128)(2,1)S(1)}, u32[]{:S(2)}, u32[]{:S(2)}) collective-permute-start(bf16[16,120,128]{2,1,0:T(8,128)(2,1)S(1)} %get-tuple-element.16), channel_id=1, source_target_pairs={{0,1},{1,2},{2,3},{3,4},{4,5},{5,6},{6,7},{8,9},{9,10},{10,11},{11... | collective-permute-start | bytes 1474568 | tf_op jit(solution)/shard_map/ppermute | solution.py:373
  237.4 18.1 %head.3 = (f32[32,120,256]{2,1,0:T(8,128)}, bf16[16,120,128]{2,1,0:T(8,128)(2,1)S(1)}, bf16[120,128]{1,0:T(8,128)(2,1)S(1)}) custom-call(s32[33]{0:T(128)S(1)} %pad_add_fusion.10.code_ref, bf16[32,48,1536]{2,1,0:T(8,128)(2,1)} %bitcast.7.recv_ref, bf16[48,48]{1,0:T(8,128)(2,1)S(1)} %copy-done, f32[48,128]{1,0:T(8,128)S(1)} %broadcast_in_dim.97.bias_ref, ...), custom_call_target="tpu_custom_call" | custom-call | flops 300000000 | bytes 8333333 | tf_op jit(solution)/shard_map/head/pallas_call | solution.py:153
  255.4 8.2 %collective-permute-start = (bf16[16,120,128]{2,1,0:T(8,128)(2,1)S(1)}, bf16[16,120,128]{2,1,0:T(8,128)(2,1)S(1)}, u32[]{:S(2)}, u32[]{:S(2)}) collective-permute-start(bf16[16,120,128]{2,1,0:T(8,128)(2,1)S(1)} %get-tuple-element.13), channel_id=1, source_target_pairs={{0,1},{1,2},{2,3},{3,4},{4,5},{5,6},{6,7},{8,9},{9,10},{10,11},{11... | collective-permute-start | bytes 1474568 | tf_op jit(solution)/shard_map/ppermute | solution.py:373
  265.6 4.1 %blend.5.prob_ref = bf16[32,120,256]{2,1,0:T(8,128)(2,1)S(1)} custom-call(f32[32,120,256]{2,1,0:T(8,128)} %get-tuple-element.18.own_ref, bf16[16,120,128]{2,1,0:T(8,128)(2,1)S(1)} %collective-permute-done.6.up_ref, bf16[120,128]{1,0:T(8,128)(2,1)S(1)} %collective-permute-done.7.down_ref, f32[32,256]{1,0:T(8,128)S(1)} %pad_maximum_fusion.5.inv_ref), custom_call_target="tpu_custom_call" | custom-call | flops 3932160 | bytes 6881280 | tf_op jit(solution)/shard_map/blend/pallas_call | solution.py:202
  285.3 4.1 %blend.3.prob_ref = bf16[32,120,256]{2,1,0:T(8,128)(2,1)S(1)} custom-call(f32[32,120,256]{2,1,0:T(8,128)} %get-tuple-element.12.own_ref, bf16[16,120,128]{2,1,0:T(8,128)(2,1)S(1)} %collective-permute-done.up_ref, bf16[120,128]{1,0:T(8,128)(2,1)S(1)} %collective-permute-done.1.down_ref, f32[32,256]{1,0:T(8,128)S(1)} %concatenate.64.inv_ref), custom_call_target="tpu_custom_call" | custom-call | flops 3932160 | bytes 6881280 | tf_op jit(solution)/shard_map/blend/pallas_call | solution.py:202
  291.7 8.7 %copy.54 = bf16[118,96,192]{0,2,1:T(8,128)(2,1)} copy(bf16[118,96,192]{2,1,0:T(8,128)(2,1)} %emit.5) | data formatting | bytes 8699904
  301.8 9.6 %dice.5 = f32[2,120,128]{2,1,0:T(8,128)S(1)} custom-call(bf16[40,120,256]{2,1,0:T(8,128)(2,1)S(1)} %pad_maximum_fusion.prob_ref, s32[38,256]{1,0:T(8,128)S(1)} %slice.231.label_ref), custom_call_target="tpu_custom_call" | custom-call | flops 36864000 | bytes 2457600 | tf_op jit(solution)/shard_map/dice/pallas_call | solution.py:298
  311.6 8.0 %dice.3 = f32[2,120,128]{2,1,0:T(8,128)S(1)} custom-call(bf16[34,120,256]{2,1,0:T(8,128)(2,1)S(1)} %pad_maximum_fusion.1.prob_ref, s32[32,256]{1,0:T(8,128)S(1)} %get-tuple-element.52.label_ref), custom_call_target="tpu_custom_call" | custom-call | flops 31334400 | bytes 2088960 | tf_op jit(solution)/shard_map/dice/pallas_call | solution.py:298
  320.0 8.0 %dice.4 = f32[2,120,128]{2,1,0:T(8,128)S(1)} custom-call(bf16[34,120,256]{2,1,0:T(8,128)(2,1)S(1)} %pad_maximum_fusion.2.prob_ref, s32[32,256]{1,0:T(8,128)S(1)} %get-tuple-element.53.label_ref), custom_call_target="tpu_custom_call" | custom-call | flops 31334400 | bytes 2088960 | tf_op jit(solution)/shard_map/dice/pallas_call | solution.py:298
  328.8 23.1 %all-to-all-start.4 = ((f32[128,2,120]{2,1,0:T(2,128)}), f32[128,2,120]{2,1,0:T(2,128)S(1)}, u32[]{:S(2)}, u32[]{:S(2)}) async-start(f32[128,2,120]{2,1,0:T(2,128)} %broadcast_in_dim.105), calls=%async_computation.4 | async-start | bytes 262144 | tf_op jit(solution)/shard_map/all_to_all | solution.py:536
  352.5 9.2 %all-to-all-done.4 = f32[128,2,120]{2,1,0:T(2,128)S(1)} async-done(((f32[128,2,120]{2,1,0:T(2,128)}), f32[128,2,120]{2,1,0:T(2,128)S(1)}, u32[]{:S(2)}, u32[]{:S(2)}) %all-to-all-start.4) | async-done | bytes 122912 | tf_op jit(solution)/shard_map/all_to_all | solution.py:536
  (127 shorter events, 53.3 us)
Async XLA Ops:
  2.8 14.0 %all-to-all-start = ((s32[16,1,2]{2,1,0:T(1,128)}), s32[16,1,2]{2,1,0:T(1,128)S(1)}, u32[]{:S(2)}, u32[]{:S(2)}) async-start(s32[16,1,2]{2,1,0:T(1,128)} %bitcast.2), calls=%async_computation | async-start | bytes 16384 | tf_op jit(solution)/shard_map/all_to_all | solution.py:454
  16.8 64.9 %all-to-all-start.3 = ((bf16[16,2,48,1536]{3,2,1,0:T(8,128)(2,1)}), bf16[16,2,48,1536]{3,2,1,0:T(8,128)(2,1)}, u32[]{:S(2)}, u32[]{:S(2)}) async-start(bf16[16,2,48,1536]{3,2,1,0:T(8,128)(2,1)} %bitcast.49), calls=%async_computation.3 | async-start | bytes 9437184 | tf_op jit(solution)/shard_map/all_to_all | solution.py:446
  81.7 12.9 %copy-start.4 = (s32[96,192]{1,0:T(8,128)S(1)}, s32[96,192]{1,0:T(8,128)}, u32[]{:S(2)}) copy-start(s32[96,192]{1,0:T(8,128)} %param.11) | copy-start | bytes 221188
  81.7 69.3 %all-to-all-start.2 = ((bf16[16,2,48,1536]{3,2,1,0:T(8,128)(2,1)}), bf16[16,2,48,1536]{3,2,1,0:T(8,128)(2,1)}, u32[]{:S(2)}, u32[]{:S(2)}) async-start(bf16[16,2,48,1536]{3,2,1,0:T(8,128)(2,1)} %bitcast.48), calls=%async_computation.2 | async-start | bytes 9437184 | tf_op jit(solution)/shard_map/all_to_all | solution.py:446
  94.7 79.5 %collective-permute-start.10 = (s32[2,192]{1,0:T(2,128)S(1)}, s32[2,192]{1,0:T(2,128)S(1)}, u32[]{:S(2)}, u32[]{:S(2)}) collective-permute-start(s32[2,192]{1,0:T(2,128)S(1)} %get-tuple-element.57), channel_id=1, source_target_pairs={{8,0},{16,8},{24,16},{32,24},{40,32},{48,40},{56,48},{64,56},{72,6... | collective-permute-start | bytes 4616 | tf_op jit(solution)/shard_map/ppermute | solution.py:373
  96.0 78.1 %collective-permute-start.9 = (s32[2,192]{1,0:T(2,128)S(1)}, s32[2,192]{1,0:T(2,128)S(1)}, u32[]{:S(2)}, u32[]{:S(2)}) collective-permute-start(s32[2,192]{1,0:T(2,128)S(1)} %get-tuple-element.56), channel_id=1, source_target_pairs={{0,8},{8,16},{16,24},{24,32},{32,40},{40,48},{48,56},{56,64},{64,7... | collective-permute-start | bytes 4616 | tf_op jit(solution)/shard_map/ppermute | solution.py:373
  151.0 86.4 %all-to-all-start.1 = ((bf16[16,2,48,1536]{3,2,1,0:T(8,128)(2,1)}), bf16[16,2,48,1536]{3,2,1,0:T(8,128)(2,1)}, u32[]{:S(2)}, u32[]{:S(2)}) async-start(bf16[16,2,48,1536]{3,2,1,0:T(8,128)(2,1)} %bitcast.47), calls=%async_computation.1 | async-start | bytes 9437184 | tf_op jit(solution)/shard_map/all_to_all | solution.py:446
  157.2 27.6 %copy-start.6 = (f32[48]{0:T(128)S(1)}, f32[48]{0:T(128)}, u32[]{:S(2)}) copy-start(f32[48]{0:T(128)} %param.13) | copy-start | bytes 580
  157.5 27.3 %copy-start = (bf16[48,48]{1,0:T(8,128)(2,1)S(1)}, bf16[48,48]{1,0:T(8,128)(2,1)}, u32[]{:S(2)}) copy-start(bf16[48,48]{1,0:T(8,128)(2,1)} %mlp_ref.5) | copy-start | bytes 13828
  158.0 26.4 %collective-permute-start.2 = (f32[96,50]{1,0:T(8,128)S(1)}, f32[96,50]{1,0:T(8,128)S(1)}, u32[]{:S(2)}, u32[]{:S(2)}) collective-permute-start(f32[96,50]{1,0:T(8,128)S(1)} %slice.201), channel_id=1, source_target_pairs={{0,1},{1,2},{2,3},{3,4},{4,5},{5,6},{6,7},{8,9},{9,10},{10,11},{11... | collective-permute-start | bytes 57608 | tf_op jit(solution)/shard_map/ppermute | solution.py:373
  169.2 10.6 %collective-permute-start.3 = (f32[96,2]{1,0:T(8,128)S(1)}, f32[96,2]{1,0:T(8,128)S(1)}, u32[]{:S(2)}, u32[]{:S(2)}) collective-permute-start(f32[96,2]{1,0:T(8,128)S(1)} %slice.207), channel_id=1, source_target_pairs={{1,0},{2,1},{3,2},{4,3},{5,4},{6,5},{7,6},{9,8},{10,9},{11,10},{12... | collective-permute-start | bytes 2312 | tf_op jit(solution)/shard_map/ppermute | solution.py:373
  174.2 5.7 %collective-permute-start.11 = (s32[100,2]{1,0:T(8,128)S(1)}, s32[100,2]{1,0:T(8,128)S(1)}, u32[]{:S(2)}, u32[]{:S(2)}) collective-permute-start(s32[100,2]{1,0:T(8,128)S(1)} %get-tuple-element.54), channel_id=1, source_target_pairs={{0,1},{1,2},{2,3},{3,4},{4,5},{5,6},{6,7},{8,9},{9,10},{10,11},{11... | collective-permute-start | bytes 2408 | tf_op jit(solution)/shard_map/ppermute | solution.py:373
  177.9 5.9 %collective-permute-start.12 = (s32[100,2]{1,0:T(8,128)S(1)}, s32[100,2]{1,0:T(8,128)S(1)}, u32[]{:S(2)}, u32[]{:S(2)}) collective-permute-start(s32[100,2]{1,0:T(8,128)S(1)} %get-tuple-element.55), channel_id=1, source_target_pairs={{1,0},{2,1},{3,2},{4,3},{5,4},{6,5},{7,6},{9,8},{10,9},{11,10},{12... | collective-permute-start | bytes 2408 | tf_op jit(solution)/shard_map/ppermute | solution.py:373
  202.8 62.8 %collective-permute-start.6 = (bf16[16,120,128]{2,1,0:T(8,128)(2,1)S(1)}, bf16[16,120,128]{2,1,0:T(8,128)(2,1)S(1)}, u32[]{:S(2)}, u32[]{:S(2)}) collective-permute-start(bf16[16,120,128]{2,1,0:T(8,128)(2,1)S(1)} %get-tuple-element.19), channel_id=1, source_target_pairs={{0,1},{1,2},{2,3},{3,4},{4,5},{5,6},{6,7},{8,9},{9,10},{10,11},{11... | collective-permute-start | bytes 1474568 | tf_op jit(solution)/shard_map/ppermute | solution.py:373
  227.0 43.8 %collective-permute-start.4 = (bf16[16,120,128]{2,1,0:T(8,128)(2,1)S(1)}, bf16[16,120,128]{2,1,0:T(8,128)(2,1)S(1)}, u32[]{:S(2)}, u32[]{:S(2)}) collective-permute-start(bf16[16,120,128]{2,1,0:T(8,128)(2,1)S(1)} %get-tuple-element.16), channel_id=1, source_target_pairs={{0,1},{1,2},{2,3},{3,4},{4,5},{5,6},{6,7},{8,9},{9,10},{10,11},{11... | collective-permute-start | bytes 1474568 | tf_op jit(solution)/shard_map/ppermute | solution.py:373
  233.5 30.2 %collective-permute-start.7 = (bf16[120,128]{1,0:T(8,128)(2,1)S(1)}, bf16[120,128]{1,0:T(8,128)(2,1)S(1)}, u32[]{:S(2)}, u32[]{:S(2)}) collective-permute-start(bf16[120,128]{1,0:T(8,128)(2,1)S(1)} %get-tuple-element.20), channel_id=1, source_target_pairs={{1,0},{2,1},{3,2},{4,3},{5,4},{6,5},{7,6},{9,8},{10,9},{11,10},{12... | collective-permute-start | bytes 92168 | tf_op jit(solution)/shard_map/ppermute | solution.py:373
  235.4 35.4 %collective-permute-start.5 = (bf16[120,128]{1,0:T(8,128)(2,1)S(1)}, bf16[120,128]{1,0:T(8,128)(2,1)S(1)}, u32[]{:S(2)}, u32[]{:S(2)}) collective-permute-start(bf16[120,128]{1,0:T(8,128)(2,1)S(1)} %get-tuple-element.17), channel_id=1, source_target_pairs={{1,0},{2,1},{3,2},{4,3},{5,4},{6,5},{7,6},{9,8},{10,9},{11,10},{12... | collective-permute-start | bytes 92168 | tf_op jit(solution)/shard_map/ppermute | solution.py:373
  255.4 29.8 %collective-permute-start = (bf16[16,120,128]{2,1,0:T(8,128)(2,1)S(1)}, bf16[16,120,128]{2,1,0:T(8,128)(2,1)S(1)}, u32[]{:S(2)}, u32[]{:S(2)}) collective-permute-start(bf16[16,120,128]{2,1,0:T(8,128)(2,1)S(1)} %get-tuple-element.13), channel_id=1, source_target_pairs={{0,1},{1,2},{2,3},{3,4},{4,5},{5,6},{6,7},{8,9},{9,10},{10,11},{11... | collective-permute-start | bytes 1474568 | tf_op jit(solution)/shard_map/ppermute | solution.py:373
  263.7 21.6 %collective-permute-start.1 = (bf16[120,128]{1,0:T(8,128)(2,1)S(1)}, bf16[120,128]{1,0:T(8,128)(2,1)S(1)}, u32[]{:S(2)}, u32[]{:S(2)}) collective-permute-start(bf16[120,128]{1,0:T(8,128)(2,1)S(1)} %get-tuple-element.14), channel_id=1, source_target_pairs={{1,0},{2,1},{3,2},{4,3},{5,4},{6,5},{7,6},{9,8},{10,9},{11,10},{12... | collective-permute-start | bytes 92168 | tf_op jit(solution)/shard_map/ppermute | solution.py:373
  278.0 33.4 %collective-permute-start.8 = (bf16[2,120,256]{2,1,0:T(8,128)(2,1)}, bf16[2,120,256]{2,1,0:T(8,128)(2,1)S(1)}, u32[]{:S(2)}, u32[]{:S(2)}) collective-permute-start(bf16[2,120,256]{2,1,0:T(8,128)(2,1)} %get-tuple-element.40), channel_id=1, source_target_pairs={{0,8},{8,16},{16,24},{24,32},{32,40},{40,48},{48,56},{56,64},{64,7... | collective-permute-start | bytes 368648 | tf_op jit(solution)/shard_map/ppermute | solution.py:373
  279.3 40.4 %collective-permute-start.13 = (bf16[2,120,256]{2,1,0:T(8,128)(2,1)}, bf16[2,120,256]{2,1,0:T(8,128)(2,1)S(1)}, u32[]{:S(2)}, u32[]{:S(2)}) collective-permute-start(bf16[2,120,256]{2,1,0:T(8,128)(2,1)} %get-tuple-element.41), channel_id=1, source_target_pairs={{8,0},{16,8},{24,16},{32,24},{40,32},{48,40},{56,48},{64,56},{72,6... | collective-permute-start | bytes 368648 | tf_op jit(solution)/shard_map/ppermute | solution.py:373
  301.7 9.6 %copy-start.1 = (bf16[16,120,256]{2,1,0:T(8,128)(2,1)S(1)}, bf16[16,120,256]{2,1,0:T(8,128)(2,1)}, u32[]{:S(2)}) copy-start(bf16[16,120,256]{2,1,0:T(8,128)(2,1)} %get-tuple-element.42) | copy-start | bytes 2949124
  301.7 9.6 %copy-start.3 = (bf16[16,120,256]{2,1,0:T(8,128)(2,1)S(1)}, bf16[16,120,256]{2,1,0:T(8,128)(2,1)}, u32[]{:S(2)}) copy-start(bf16[16,120,256]{2,1,0:T(8,128)(2,1)} %get-tuple-element.44) | copy-start | bytes 2949124
  328.8 32.8 %all-to-all-start.4 = ((f32[128,2,120]{2,1,0:T(2,128)}), f32[128,2,120]{2,1,0:T(2,128)S(1)}, u32[]{:S(2)}, u32[]{:S(2)}) async-start(f32[128,2,120]{2,1,0:T(2,128)} %broadcast_in_dim.105), calls=%async_computation.4 | async-start | bytes 262144 | tf_op jit(solution)/shard_map/all_to_all | solution.py:536
  (3 other events, 26.2 us)

commit v3 on v2

--- a/solution.py
+++ b/solution.py
@@ -16,7 +16,8 @@
 VMEM_LIMIT = 50 * 1024 * 1024
 
 
-def pack_kernel(first, rows, pick_ref, feats_ref, out_ref, sems):
+def pack_kernel(first, rows, pick_ref, feats_ref, *refs):
+    out_ref, sems = refs[-2:]
     width = rows * PATCH
 
     def copy_of(column):
@@ -41,13 +42,14 @@
             copy_of(column).wait()
 
 
-def pack(feats, pick, first, rows):
+def pack(feats, pick, first, rows, *after):
     columns = pick.shape[0]
     width = rows * PATCH
     return pl.pallas_call(
         functools.partial(pack_kernel, first, rows),
         out_shape=jax.ShapeDtypeStruct((columns, feats.shape[1], width), feats.dtype),
-        in_specs=[pl.BlockSpec(memory_space=pltpu.SMEM), pl.BlockSpec(memory_space=pl.ANY)],
+        in_specs=[pl.BlockSpec(memory_space=pltpu.SMEM)]
+        + [pl.BlockSpec(memory_space=pl.ANY)] * (1 + len(after)),
         out_specs=pl.BlockSpec(memory_space=pltpu.VMEM),
         scratch_shapes=[pltpu.SemaphoreType.DMA((columns,))],
         compiler_params=pltpu.CompilerParams(vmem_limit_bytes=VMEM_LIMIT),
@@ -55,7 +57,7 @@
             flops=0, bytes_accessed=columns * width * feats.shape[1] * 4, transcendentals=0
         ),
         name="pack",
-    )(pick, feats)
+    )(pick, feats, *after)
 
 
 def spread_rows(tiles, lane):
@@ -315,38 +317,35 @@
 
 def emit_kernel(low, high, prob_ref, *refs):
     out_ref, turned_ref, sems = refs[-3:]
-    rows, padded, _ = prob_ref.shape
-    classes, _, span_y = out_ref.shape
+    rows = prob_ref.shape[0]
+    _, span_y, classes = out_ref.shape
     half = rows // 2
 
-    @pl.loop(0, padded // 8)
-    def _(index):
-        group = pl.multiple_of(index * 8, 8)
-        for at in range(0, rows, 8):
-            for i in range(2):
-                lanes = slice(i * TILE, min((i + 1) * TILE, span_y))
-                block = prob_ref[at : at + 8, pl.ds(group, 8), i * TILE : (i + 1) * TILE]
-                block = jnp.transpose(block.astype(jnp.float32), (1, 0, 2))
-                turned_ref[pl.ds(group, 8), at : at + 8, lanes] = block[
-                    :, :, : lanes.stop - lanes.start
+    def copy_of(i, at):
+        return pltpu.make_async_copy(
+            turned_ref.at[pl.ds(i * half, half)], out_ref.at[pl.ds(at, half)], sems.at[i]
+        )
+
+    for i, at in enumerate((low, high)):
+
+        @pl.loop(0, half)
+        def _(index):
+            row = i * half + index
+            for j in range(2):
+                block = prob_ref[row, :, j * TILE : (j + 1) * TILE].astype(jnp.float32)
+                block = jnp.transpose(block, (1, 0))
+                stop = min((j + 1) * TILE, span_y)
+                turned_ref[row, j * TILE : stop, :] = block[
+                    : stop - j * TILE, :classes
                 ].astype(jnp.bfloat16)
 
-    copies = [
-        pltpu.make_async_copy(
-            turned_ref.at[pl.ds(0, classes), pl.ds(i * half, half), :],
-            out_ref.at[:, pl.ds(at, half), :],
-            sems.at[i],
-        )
-        for i, at in enumerate((low, high))
-    ]
-    for copy in copies:
-        copy.start()
-    for copy in copies:
-        copy.wait()
+        copy_of(i, at).start()
+    for i, at in enumerate((low, high)):
+        copy_of(i, at).wait()
 
 
 def emit(prob, low, high, shape, out=None):
-    rows, padded, _ = prob.shape
+    rows = prob.shape[0]
     anywhere = pl.BlockSpec(memory_space=pl.ANY)
     before = () if out is None else (out,)
     return pl.pallas_call(
@@ -356,7 +355,7 @@
         out_specs=anywhere,
         input_output_aliases={1: 0} if before else {},
         scratch_shapes=[
-            pltpu.VMEM((padded, rows, shape[2]), prob.dtype),
+            pltpu.VMEM((rows,) + shape[1:], prob.dtype),
             pltpu.SemaphoreType.DMA((2,)),
         ],
         compiler_params=pltpu.CompilerParams(vmem_limit_bytes=VMEM_LIMIT),
@@ -441,13 +440,13 @@
         jnp.where(hit, (2 * slot_ids[:, None] + halves[None, :])[:, :, None], -1), axis=(0, 1)
     )
 
-    payloads = [pack(feats, pick, first, rows) for first, rows in CHUNKS]
-    received = [
-        lax.all_to_all(
-            payload.reshape(wide, 2, feat, payload.shape[2]), "wide", 0, 0, tiled=True
-        ).reshape(2 * wide, feat, payload.shape[2])
-        for payload in payloads
-    ]
+    def exchange(chunk, *after):
+        payload = pack(feats, pick, *CHUNKS[chunk], *after)
+        shape = payload.shape
+        payload = payload.reshape((wide, 2) + shape[1:])
+        return lax.all_to_all(payload, "wide", 0, 0, tiled=True).reshape(shape)
+
+    received = [exchange(0), exchange(1)]
 
     kind = (patch_ids[0, 0] % rows_q - ROWS * here_narrow)[:, None] * 2 + halves[None, :]
     tag = jnp.max(jnp.where(hit, kind[:, :, None], -1), axis=(0, 1)).reshape(wide, 2)
@@ -507,16 +506,18 @@
     bias_tile = jnp.broadcast_to(mlp_bias[:, None], (feat, TILE))
     probs = []
     blended = None
-    for (first, rows), recv in zip(CHUNKS, received):
+    for chunk, (first, rows) in enumerate(CHUNKS):
         own, up, down = head_of(
-            recv, codes, mlp_weight, bias_tile, head_weight, table, first, rows, classes
-        )
+            received[chunk], codes, mlp_weight, bias_tile, head_weight, table, first, rows, classes
+        )
+        if chunk + 2 < len(CHUNKS):
+            received.append(exchange(chunk + 2, down))
         up = shifted(up, "narrow", 1)
         down = shifted(down, "narrow", -1)
         prob = blend_of(own, up, down, rows_of(inverse, first, rows))
         probs.append(prob)
         blended = emit(
-            prob, first, span_x - first - rows, (classes, span_x, span_y), blended
+            prob, first, span_x - first - rows, (span_x, span_y, classes), blended
         )
     edge_rows = CHUNKS[0][1]
     before = shifted(probs[0][2 * edge_rows - 2 :], "wide", 1)
@@ -536,7 +537,7 @@
     whole = jnp.sum(lax.all_to_all(whole, ("wide", "narrow"), 0, 0, tiled=True), axis=0)
     dice = ((whole[0] + 1.0) / (whole[1] + 1.0))[:classes]
     slab_sums = (sums[:, :classes] / jnp.float32(span_x)).reshape(1, 1, 2, classes)
-    return (blended, dice, slab_sums)
+    return (blended.transpose(2, 0, 1), dice, slab_sums)
 
 
 def solution(mesh):

time: 367 us -> 329 us (0.90)
  waiting for transfers between devices: 115 us -> 95 us
  starting transfers between devices: 108 us -> 92.8 us
  Pallas kernels: 113 us -> 123 us
  local copies, waits for them, and re-layouts: 17.1 us -> 7.18 us
    all_to_all x3, waiting for transfers between devices: 101 us -> 80.3 us  [exchange(): return lax.all_to_all(payload, 'wide', 0, 0, tiled=True).reshape(shape)]
    ppermute x14, starting transfers between devices: 53 us -> 39.8 us  [shifted(): return lax.ppermute(block, axis, pairs)]
    unnamed x18 -> x19, local copies, waits for them, and re-layouts: 8.85 us -> 0.16 us
    pallas_call x3, Pallas kernels: 6.97 us -> 12.5 us  [emit(): pl.pallas_call(functools.partial(emit_kernel, low, high), out_shape=jax.S...]
    pallas_call x3, Pallas kernels: 54.1 us -> 58.9 us  [head_of(): pl.pallas_call(functools.partial(head_kernel, first, rows, classes), out_...]
    all_to_all x1, waiting for transfers between devices: 9.18 us -> 5 us  [on_device(): lax.all_to_all(whole, ('wide', 'narrow'), 0, 0, tiled=True)]
    ppermute x14, waiting for transfers between devices: 3.86 us -> 7.9 us  [shifted(): return lax.ppermute(block, axis, pairs)]
  transfers between devices with their start and end apart: 19 -> 19, of which waited for: 5 -> 6; matrix products, arithmetic and copies ran while one was open for 6% -> 3% of each run, Pallas kernels for 29% -> 34%
where the time goes in v3:
time: 329 us; the launch traced here: 326 us
  Pallas kernels  123 us (37%)
  waiting for transfers between devices  95 us (29%)
  starting transfers between devices  92.8 us (28%)
  local copies, waits for them, and re-layouts  7.18 us (2%)
  other arithmetic  6.08 us (2%)
    all_to_all x3, waiting for transfers between devices, exchange(): return lax.all_to_all(payload, 'wide', 0, 0, tiled=True).reshape(shape)  80.3 us
    pallas_call x3, Pallas kernels, head_of(): pl.pallas_call(functools.partial(head_kernel, first, rows, classes), out_...  58.9 us
    ppermute x14, starting transfers between devices, shifted(): return lax.ppermute(block, axis, pairs)  39.8 us
    pallas_call x3, Pallas kernels, dice_of(): pl.pallas_call(dice_kernel, out_shape=jax.ShapeDtypeStruct((2, padded, TI...  25.7 us
    all_to_all x3, starting transfers between devices, exchange(): return lax.all_to_all(payload, 'wide', 0, 0, tiled=True).reshape(shape)  23.6 us
    all_to_all x1, starting transfers between devices, on_device(): lax.all_to_all(whole, ('wide', 'narrow'), 0, 0, tiled=True)  21.9 us
    pallas_call x3, Pallas kernels, pack(): pl.pallas_call(functools.partial(pack_kernel, first, rows), out_shape=jax...  13.8 us
    pallas_call x3, Pallas kernels, emit(): pl.pallas_call(functools.partial(emit_kernel, low, high), out_shape=jax.S...  12.5 us
  transfers between devices with their start and end apart: 19, of which 6 were waited for; matrix products, arithmetic and copies ran while one was open for 3% of the time, Pallas kernels for 34%

profile of v3, /device:TPU:1, one launch (start us, length us, event | category | flops | bytes accessed | tf_op | source)
XLA Modules:
  0.0 326.2 jit_solution(12370642887377658004)
XLA Ops:
  2.8 7.6 %all-to-all-start = ((s32[16,1,2]{2,1,0:T(1,128)}), s32[16,1,2]{2,1,0:T(1,128)S(1)}, u32[]{:S(2)}, u32[]{:S(2)}) async-start(s32[16,1,2]{2,1,0:T(1,128)} %bitcast.2), calls=%async_computation | async-start | bytes 16384 | tf_op jit(solution)/shard_map/all_to_all | solution.py:453
  10.4 4.6 %pack.3 = bf16[32,48,1536]{2,1,0:T(8,128)(2,1)} custom-call(s32[32]{0:T(128)S(1)} %get-tuple-element.23.pick_ref, bf16[8,48,9216]{2,1,0:T(8,128)(2,1)} %bitcast.45), custom_call_target="tpu_custom_call" | custom-call | bytes 9437184 | tf_op jit(solution)/shard_map/pack/pallas_call | solution.py:48
  16.8 5.0 %all-to-all-start.1 = ((bf16[16,2,48,1536]{3,2,1,0:T(8,128)(2,1)}), bf16[16,2,48,1536]{3,2,1,0:T(8,128)(2,1)}, u32[]{:S(2)}, u32[]{:S(2)}) async-start(bf16[16,2,48,1536]{3,2,1,0:T(8,128)(2,1)} %bitcast.51), calls=%async_computation.1 | async-start | bytes 9437184 | tf_op jit(solution)/shard_map/all_to_all | solution.py:447
  21.8 4.6 %pack.5 = bf16[32,48,1536]{2,1,0:T(8,128)(2,1)} custom-call(s32[32]{0:T(128)S(1)} %get-tuple-element.23.pick_ref, bf16[8,48,9216]{2,1,0:T(8,128)(2,1)} %bitcast.46), custom_call_target="tpu_custom_call" | custom-call | bytes 9437184 | tf_op jit(solution)/shard_map/pack/pallas_call | solution.py:48
  26.4 57.8 %all-to-all-done.1 = bf16[16,2,48,1536]{3,2,1,0:T(8,128)(2,1)} async-done(((bf16[16,2,48,1536]{3,2,1,0:T(8,128)(2,1)}), bf16[16,2,48,1536]{3,2,1,0:T(8,128)(2,1)}, u32[]{:S(2)}, u32[]{:S(2)}) %all-to-all-start.1) | async-done | bytes 4718624 | tf_op jit(solution)/shard_map/all_to_all | solution.py:447
  84.1 12.4 %all-to-all-start.3 = ((bf16[16,2,48,1536]{3,2,1,0:T(8,128)(2,1)}), bf16[16,2,48,1536]{3,2,1,0:T(8,128)(2,1)}, u32[]{:S(2)}, u32[]{:S(2)}) async-start(bf16[16,2,48,1536]{3,2,1,0:T(8,128)(2,1)} %bitcast.50), calls=%async_computation.3 | async-start | bytes 9437184 | tf_op jit(solution)/shard_map/all_to_all | solution.py:447
  105.9 19.6 %head.3 = (f32[32,120,256]{2,1,0:T(8,128)}, bf16[16,120,128]{2,1,0:T(8,128)(2,1)S(1)}, bf16[120,128]{1,0:T(8,128)(2,1)S(1)}) custom-call(s32[33]{0:T(128)S(1)} %pad_add_fusion.10.code_ref, bf16[32,48,1536]{2,1,0:T(8,128)(2,1)} %bitcast.7.recv_ref, bf16[48,48]{1,0:T(8,128)(2,1)S(1)} %copy-done, f32[48,128]{1,0:T(8,128)S(1)} %broadcast_in_dim.97.bias_ref, ...), custom_call_target="tpu_custom_call" | custom-call | flops 300000000 | bytes 8333333 | tf_op jit(solution)/shard_map/head/pallas_call | solution.py:155
  125.5 4.6 %pack.4 = bf16[32,48,1536]{2,1,0:T(8,128)(2,1)} custom-call(s32[32]{0:T(128)S(1)} %get-tuple-element.23.pick_ref, bf16[8,48,9216]{2,1,0:T(8,128)(2,1)} %bitcast.47, bf16[120,128]{1,0:T(8,128)(2,1)S(1)} %get-tuple-element.12.refs_0_), custom_call_target="tpu_custom_call" | custom-call | bytes 9437184 | tf_op jit(solution)/shard_map/pack/pallas_call | solution.py:48
  130.2 22.6 %all-to-all-done.3 = bf16[16,2,48,1536]{3,2,1,0:T(8,128)(2,1)} async-done(((bf16[16,2,48,1536]{3,2,1,0:T(8,128)(2,1)}), bf16[16,2,48,1536]{3,2,1,0:T(8,128)(2,1)}, u32[]{:S(2)}, u32[]{:S(2)}) %all-to-all-start.3) | async-done | bytes 4718624 | tf_op jit(solution)/shard_map/all_to_all | solution.py:447
  152.7 6.2 %all-to-all-start.2 = ((bf16[16,2,48,1536]{3,2,1,0:T(8,128)(2,1)}), bf16[16,2,48,1536]{3,2,1,0:T(8,128)(2,1)}, u32[]{:S(2)}, u32[]{:S(2)}) async-start(bf16[16,2,48,1536]{3,2,1,0:T(8,128)(2,1)} %bitcast.49), calls=%async_computation.2 | async-start | bytes 9437184 | tf_op jit(solution)/shard_map/all_to_all | solution.py:447
  159.9 5.8 %collective-permute-start.2 = (f32[96,50]{1,0:T(8,128)S(1)}, f32[96,50]{1,0:T(8,128)S(1)}, u32[]{:S(2)}, u32[]{:S(2)}) collective-permute-start(f32[96,50]{1,0:T(8,128)S(1)} %slice.201), channel_id=1, source_target_pairs={{0,1},{1,2},{2,3},{3,4},{4,5},{5,6},{6,7},{8,9},{9,10},{10,11},{11... | collective-permute-start | bytes 57608 | tf_op jit(solution)/shard_map/ppermute | solution.py:372
  173.4 6.1 %collective-permute-done.12 = s32[100,2]{1,0:T(8,128)S(1)} collective-permute-done((s32[100,2]{1,0:T(8,128)S(1)}, s32[100,2]{1,0:T(8,128)S(1)}, u32[]{:S(2)}, u32[]{:S(2)}) %collective-permute-start.12) | collective-permute-done | bytes 832 | tf_op jit(solution)/shard_map/ppermute | solution.py:372
  182.7 19.5 %head.5 = (f32[32,120,256]{2,1,0:T(8,128)}, bf16[16,120,128]{2,1,0:T(8,128)(2,1)S(1)}, bf16[120,128]{1,0:T(8,128)(2,1)S(1)}) custom-call(s32[33]{0:T(128)S(1)} %pad_add_fusion.10.code_ref, bf16[32,48,1536]{2,1,0:T(8,128)(2,1)} %bitcast.19.recv_ref, bf16[48,48]{1,0:T(8,128)(2,1)S(1)} %copy-done, f32[48,128]{1,0:T(8,128)S(1)} %broadcast_in_dim.97.bias_ref, ...), custom_call_target="tpu_custom_call" | custom-call | flops 300000000 | bytes 8333333 | tf_op jit(solution)/shard_map/head/pallas_call | solution.py:155
  202.2 4.4 %collective-permute-start.4 = (bf16[16,120,128]{2,1,0:T(8,128)(2,1)S(1)}, bf16[16,120,128]{2,1,0:T(8,128)(2,1)S(1)}, u32[]{:S(2)}, u32[]{:S(2)}) collective-permute-start(bf16[16,120,128]{2,1,0:T(8,128)(2,1)S(1)} %get-tuple-element.17), channel_id=1, source_target_pairs={{0,1},{1,2},{2,3},{3,4},{4,5},{5,6},{6,7},{8,9},{9,10},{10,11},{11... | collective-permute-start | bytes 1474568 | tf_op jit(solution)/shard_map/ppermute | solution.py:372
  216.4 4.4 %collective-permute-start.8 = (bf16[2,120,256]{2,1,0:T(8,128)(2,1)S(1)}, bf16[2,120,256]{2,1,0:T(8,128)(2,1)S(1)}, u32[]{:S(2)}, u32[]{:S(2)}) collective-permute-start(bf16[2,120,256]{2,1,0:T(8,128)(2,1)S(1)} %get-tuple-element.25), channel_id=1, source_target_pairs={{0,8},{8,16},{16,24},{24,32},{32,40},{40,48},{48,56},{56,64},{64,7... | collective-permute-start | bytes 368648 | tf_op jit(solution)/shard_map/ppermute | solution.py:372
  222.1 4.2 %emit.3.refs_0_ = bf16[96,192,118]{2,1,0:T(8,128)(2,1)} custom-call(bf16[32,120,256]{2,1,0:T(8,128)(2,1)S(1)} %blend.5.prob_ref), custom_call_target="tpu_custom_call" | custom-call | flops 3932160 | bytes 3932160 | tf_op jit(solution)/shard_map/emit/pallas_call | solution.py:351
  230.3 4.2 %emit.4.refs_0_ = bf16[96,192,118]{2,1,0:T(8,128)(2,1)} custom-call(bf16[32,120,256]{2,1,0:T(8,128)(2,1)S(1)} %blend.4.prob_ref, bf16[96,192,118]{2,1,0:T(8,128)(2,1)} %emit.3.refs_0_), custom_call_target="tpu_custom_call", output_to_operand_aliasing={{}: (1, {})} | custom-call | flops 3932160 | bytes 3932160 | tf_op jit(solution)/shard_map/emit/pallas_call | solution.py:351
  237.4 19.8 %head.4 = (f32[32,120,256]{2,1,0:T(8,128)}, bf16[16,120,128]{2,1,0:T(8,128)(2,1)S(1)}, bf16[120,128]{1,0:T(8,128)(2,1)S(1)}) custom-call(s32[33]{0:T(128)S(1)} %pad_add_fusion.10.code_ref, bf16[32,48,1536]{2,1,0:T(8,128)(2,1)} %bitcast.12.recv_ref, bf16[48,48]{1,0:T(8,128)(2,1)S(1)} %copy-done, f32[48,128]{1,0:T(8,128)S(1)} %broadcast_in_dim.97.bias_ref, ...), custom_call_target="tpu_custom_call" | custom-call | flops 300000000 | bytes 8333333 | tf_op jit(solution)/shard_map/head/pallas_call | solution.py:155
  263.0 8.0 %dice.3 = f32[2,120,128]{2,1,0:T(8,128)S(1)} custom-call(bf16[34,120,256]{2,1,0:T(8,128)(2,1)S(1)} %pad_maximum_fusion.1.prob_ref, s32[32,256]{1,0:T(8,128)S(1)} %get-tuple-element.37.label_ref), custom_call_target="tpu_custom_call" | custom-call | flops 31334400 | bytes 2088960 | tf_op jit(solution)/shard_map/dice/pallas_call | solution.py:300
  271.1 8.0 %dice.4 = f32[2,120,128]{2,1,0:T(8,128)S(1)} custom-call(bf16[34,120,256]{2,1,0:T(8,128)(2,1)S(1)} %pad_maximum_fusion.2.prob_ref, s32[32,256]{1,0:T(8,128)S(1)} %get-tuple-element.38.label_ref), custom_call_target="tpu_custom_call" | custom-call | flops 31334400 | bytes 2088960 | tf_op jit(solution)/shard_map/dice/pallas_call | solution.py:300
  283.6 9.6 %dice.5 = f32[2,120,128]{2,1,0:T(8,128)S(1)} custom-call(bf16[40,120,256]{2,1,0:T(8,128)(2,1)S(1)} %pad_maximum_fusion.prob_ref, s32[38,256]{1,0:T(8,128)S(1)} %slice.231.label_ref), custom_call_target="tpu_custom_call" | custom-call | flops 36864000 | bytes 2457600 | tf_op jit(solution)/shard_map/dice/pallas_call | solution.py:300
  294.0 21.9 %all-to-all-start.4 = ((f32[128,2,120]{2,1,0:T(2,128)}), f32[128,2,120]{2,1,0:T(2,128)S(1)}, u32[]{:S(2)}, u32[]{:S(2)}) async-start(f32[128,2,120]{2,1,0:T(2,128)} %broadcast_in_dim.105), calls=%async_computation.4 | async-start | bytes 262144 | tf_op jit(solution)/shard_map/all_to_all | solution.py:537
  315.8 4.2 %emit.5 = bf16[96,192,118]{2,1,0:T(8,128)(2,1)} custom-call(bf16[32,120,256]{2,1,0:T(8,128)(2,1)S(1)} %blend.3.prob_ref, bf16[96,192,118]{2,1,0:T(8,128)(2,1)} %emit.4.refs_0_), custom_call_target="tpu_custom_call", output_to_operand_aliasing={{}: (1, {})} | custom-call | flops 3932160 | bytes 3932160 | tf_op jit(solution)/shard_map/emit/pallas_call | solution.py:351
  320.6 5.0 %all-to-all-done.4 = f32[128,2,120]{2,1,0:T(2,128)S(1)} async-done(((f32[128,2,120]{2,1,0:T(2,128)}), f32[128,2,120]{2,1,0:T(2,128)S(1)}, u32[]{:S(2)}, u32[]{:S(2)}) %all-to-all-start.4) | async-done | bytes 122912 | tf_op jit(solution)/shard_map/all_to_all | solution.py:537
  (128 shorter events, 54.3 us)
Async XLA Ops:
  2.8 14.0 %all-to-all-start = ((s32[16,1,2]{2,1,0:T(1,128)}), s32[16,1,2]{2,1,0:T(1,128)S(1)}, u32[]{:S(2)}, u32[]{:S(2)}) async-start(s32[16,1,2]{2,1,0:T(1,128)} %bitcast.2), calls=%async_computation | async-start | bytes 16384 | tf_op jit(solution)/shard_map/all_to_all | solution.py:453
  16.8 67.3 %all-to-all-start.1 = ((bf16[16,2,48,1536]{3,2,1,0:T(8,128)(2,1)}), bf16[16,2,48,1536]{3,2,1,0:T(8,128)(2,1)}, u32[]{:S(2)}, u32[]{:S(2)}) async-start(bf16[16,2,48,1536]{3,2,1,0:T(8,128)(2,1)} %bitcast.51), calls=%async_computation.1 | async-start | bytes 9437184 | tf_op jit(solution)/shard_map/all_to_all | solution.py:447
  84.1 18.2 %copy-start.6 = (bf16[118,48]{0,1:T(8,128)(2,1)S(1)}, bf16[118,48]{0,1:T(8,128)(2,1)}, u32[]{:S(2)}) copy-start(bf16[118,48]{0,1:T(8,128)(2,1)} %param.14) | copy-start | bytes 33988
  84.1 21.7 %copy-start.7 = (f32[48]{0:T(128)S(1)}, f32[48]{0:T(128)}, u32[]{:S(2)}) copy-start(f32[48]{0:T(128)} %param.13) | copy-start | bytes 580
  84.1 21.8 %copy-start = (bf16[48,48]{1,0:T(8,128)(2,1)S(1)}, bf16[48,48]{1,0:T(8,128)(2,1)}, u32[]{:S(2)}) copy-start(bf16[48,48]{1,0:T(8,128)(2,1)} %mlp_ref.5) | copy-start | bytes 13828
  84.1 68.6 %all-to-all-start.3 = ((bf16[16,2,48,1536]{3,2,1,0:T(8,128)(2,1)}), bf16[16,2,48,1536]{3,2,1,0:T(8,128)(2,1)}, u32[]{:S(2)}, u32[]{:S(2)}) async-start(bf16[16,2,48,1536]{3,2,1,0:T(8,128)(2,1)} %bitcast.50), calls=%async_computation.3 | async-start | bytes 9437184 | tf_op jit(solution)/shard_map/all_to_all | solution.py:447
  96.5 71.3 %collective-permute-start.10 = (s32[2,192]{1,0:T(2,128)S(1)}, s32[2,192]{1,0:T(2,128)S(1)}, u32[]{:S(2)}, u32[]{:S(2)}) collective-permute-start(s32[2,192]{1,0:T(2,128)S(1)} %get-tuple-element.42), channel_id=1, source_target_pairs={{8,0},{16,8},{24,16},{32,24},{40,32},{48,40},{56,48},{64,56},{72,6... | collective-permute-start | bytes 4616 | tf_op jit(solution)/shard_map/ppermute | solution.py:372
  97.8 70.1 %collective-permute-start.9 = (s32[2,192]{1,0:T(2,128)S(1)}, s32[2,192]{1,0:T(2,128)S(1)}, u32[]{:S(2)}, u32[]{:S(2)}) collective-permute-start(s32[2,192]{1,0:T(2,128)S(1)} %get-tuple-element.41), channel_id=1, source_target_pairs={{0,8},{8,16},{16,24},{24,32},{32,40},{40,48},{48,56},{56,64},{64,7... | collective-permute-start | bytes 4616 | tf_op jit(solution)/shard_map/ppermute | solution.py:372
  152.7 84.7 %all-to-all-start.2 = ((bf16[16,2,48,1536]{3,2,1,0:T(8,128)(2,1)}), bf16[16,2,48,1536]{3,2,1,0:T(8,128)(2,1)}, u32[]{:S(2)}, u32[]{:S(2)}) async-start(bf16[16,2,48,1536]{3,2,1,0:T(8,128)(2,1)} %bitcast.49), calls=%async_computation.2 | async-start | bytes 9437184 | tf_op jit(solution)/shard_map/all_to_all | solution.py:447
  159.9 20.3 %collective-permute-start.2 = (f32[96,50]{1,0:T(8,128)S(1)}, f32[96,50]{1,0:T(8,128)S(1)}, u32[]{:S(2)}, u32[]{:S(2)}) collective-permute-start(f32[96,50]{1,0:T(8,128)S(1)} %slice.201), channel_id=1, source_target_pairs={{0,1},{1,2},{2,3},{3,4},{4,5},{5,6},{6,7},{8,9},{9,10},{10,11},{11... | collective-permute-start | bytes 57608 | tf_op jit(solution)/shard_map/ppermute | solution.py:372
  165.7 7.6 %collective-permute-start.3 = (f32[96,2]{1,0:T(8,128)S(1)}, f32[96,2]{1,0:T(8,128)S(1)}, u32[]{:S(2)}, u32[]{:S(2)}) collective-permute-start(f32[96,2]{1,0:T(8,128)S(1)} %slice.207), channel_id=1, source_target_pairs={{1,0},{2,1},{3,2},{4,3},{5,4},{6,5},{7,6},{9,8},{10,9},{11,10},{12... | collective-permute-start | bytes 2312 | tf_op jit(solution)/shard_map/ppermute | solution.py:372
  168.0 5.4 %collective-permute-start.11 = (s32[100,2]{1,0:T(8,128)S(1)}, s32[100,2]{1,0:T(8,128)S(1)}, u32[]{:S(2)}, u32[]{:S(2)}) collective-permute-start(s32[100,2]{1,0:T(8,128)S(1)} %get-tuple-element.39), channel_id=1, source_target_pairs={{0,1},{1,2},{2,3},{3,4},{4,5},{5,6},{6,7},{8,9},{9,10},{10,11},{11... | collective-permute-start | bytes 2408 | tf_op jit(solution)/shard_map/ppermute | solution.py:372
  171.4 8.2 %collective-permute-start.12 = (s32[100,2]{1,0:T(8,128)S(1)}, s32[100,2]{1,0:T(8,128)S(1)}, u32[]{:S(2)}, u32[]{:S(2)}) collective-permute-start(s32[100,2]{1,0:T(8,128)S(1)} %get-tuple-element.40), channel_id=1, source_target_pairs={{1,0},{2,1},{3,2},{4,3},{5,4},{6,5},{7,6},{9,8},{10,9},{11,10},{12... | collective-permute-start | bytes 2408 | tf_op jit(solution)/shard_map/ppermute | solution.py:372
  180.5 31.8 %collective-permute-start.6 = (bf16[16,120,128]{2,1,0:T(8,128)(2,1)S(1)}, bf16[16,120,128]{2,1,0:T(8,128)(2,1)S(1)}, u32[]{:S(2)}, u32[]{:S(2)}) collective-permute-start(bf16[16,120,128]{2,1,0:T(8,128)(2,1)S(1)} %get-tuple-element.20), channel_id=1, source_target_pairs={{0,1},{1,2},{2,3},{3,4},{4,5},{5,6},{6,7},{8,9},{9,10},{10,11},{11... | collective-permute-start | bytes 1474568 | tf_op jit(solution)/shard_map/ppermute | solution.py:372
  202.2 24.0 %collective-permute-start.4 = (bf16[16,120,128]{2,1,0:T(8,128)(2,1)S(1)}, bf16[16,120,128]{2,1,0:T(8,128)(2,1)S(1)}, u32[]{:S(2)}, u32[]{:S(2)}) collective-permute-start(bf16[16,120,128]{2,1,0:T(8,128)(2,1)S(1)} %get-tuple-element.17), channel_id=1, source_target_pairs={{0,1},{1,2},{2,3},{3,4},{4,5},{5,6},{6,7},{8,9},{9,10},{10,11},{11... | collective-permute-start | bytes 1474568 | tf_op jit(solution)/shard_map/ppermute | solution.py:372
  206.6 5.6 %collective-permute-start.7 = (bf16[120,128]{1,0:T(8,128)(2,1)S(1)}, bf16[120,128]{1,0:T(8,128)(2,1)S(1)}, u32[]{:S(2)}, u32[]{:S(2)}) collective-permute-start(bf16[120,128]{1,0:T(8,128)(2,1)S(1)} %get-tuple-element.12.refs_0_), channel_id=1, source_target_pairs={{1,0},{2,1},{3,2},{4,3},{5,4},{6,5},{7,6},{9,8},{10,9},{11,10},{12... | collective-permute-start | bytes 92168 | tf_op jit(solution)/shard_map/ppermute | solution.py:372
  208.6 17.6 %collective-permute-start.5 = (bf16[120,128]{1,0:T(8,128)(2,1)S(1)}, bf16[120,128]{1,0:T(8,128)(2,1)S(1)}, u32[]{:S(2)}, u32[]{:S(2)}) collective-permute-start(bf16[120,128]{1,0:T(8,128)(2,1)S(1)} %get-tuple-element.18), channel_id=1, source_target_pairs={{1,0},{2,1},{3,2},{4,3},{5,4},{6,5},{7,6},{9,8},{10,9},{11,10},{12... | collective-permute-start | bytes 92168 | tf_op jit(solution)/shard_map/ppermute | solution.py:372
  216.4 44.0 %collective-permute-start.8 = (bf16[2,120,256]{2,1,0:T(8,128)(2,1)S(1)}, bf16[2,120,256]{2,1,0:T(8,128)(2,1)S(1)}, u32[]{:S(2)}, u32[]{:S(2)}) collective-permute-start(bf16[2,120,256]{2,1,0:T(8,128)(2,1)S(1)} %get-tuple-element.25), channel_id=1, source_target_pairs={{0,8},{8,16},{16,24},{24,32},{32,40},{40,48},{48,56},{56,64},{64,7... | collective-permute-start | bytes 368648 | tf_op jit(solution)/shard_map/ppermute | solution.py:372
  220.8 42.0 %collective-permute-start.13 = (bf16[2,120,256]{2,1,0:T(8,128)(2,1)S(1)}, bf16[2,120,256]{2,1,0:T(8,128)(2,1)S(1)}, u32[]{:S(2)}, u32[]{:S(2)}) collective-permute-start(bf16[2,120,256]{2,1,0:T(8,128)(2,1)S(1)} %get-tuple-element.26), channel_id=1, source_target_pairs={{8,0},{16,8},{24,16},{32,24},{40,32},{48,40},{56,48},{64,56},{72,6... | collective-permute-start | bytes 368648 | tf_op jit(solution)/shard_map/ppermute | solution.py:372
  237.4 23.0 %copy-start.3 = (bf16[16,120,256]{2,1,0:T(8,128)(2,1)S(1)}, bf16[16,120,256]{2,1,0:T(8,128)(2,1)}, u32[]{:S(2)}) copy-start(bf16[16,120,256]{2,1,0:T(8,128)(2,1)} %get-tuple-element.27) | copy-start | bytes 2949124
  237.4 23.0 %copy-start.4 = (bf16[16,120,256]{2,1,0:T(8,128)(2,1)S(1)}, bf16[16,120,256]{2,1,0:T(8,128)(2,1)}, u32[]{:S(2)}) copy-start(bf16[16,120,256]{2,1,0:T(8,128)(2,1)} %get-tuple-element.29) | copy-start | bytes 2949124
  257.2 21.9 %collective-permute-start = (bf16[16,120,128]{2,1,0:T(8,128)(2,1)S(1)}, bf16[16,120,128]{2,1,0:T(8,128)(2,1)S(1)}, u32[]{:S(2)}, u32[]{:S(2)}) collective-permute-start(bf16[16,120,128]{2,1,0:T(8,128)(2,1)S(1)} %get-tuple-element.14), channel_id=1, source_target_pairs={{0,1},{1,2},{2,3},{3,4},{4,5},{5,6},{6,7},{8,9},{9,10},{10,11},{11... | collective-permute-start | bytes 1474568 | tf_op jit(solution)/shard_map/ppermute | solution.py:372
  260.7 18.5 %collective-permute-start.1 = (bf16[120,128]{1,0:T(8,128)(2,1)S(1)}, bf16[120,128]{1,0:T(8,128)(2,1)S(1)}, u32[]{:S(2)}, u32[]{:S(2)}) collective-permute-start(bf16[120,128]{1,0:T(8,128)(2,1)S(1)} %get-tuple-element.15), channel_id=1, source_target_pairs={{1,0},{2,1},{3,2},{4,3},{5,4},{6,5},{7,6},{9,8},{10,9},{11,10},{12... | collective-permute-start | bytes 92168 | tf_op jit(solution)/shard_map/ppermute | solution.py:372
  294.0 31.6 %all-to-all-start.4 = ((f32[128,2,120]{2,1,0:T(2,128)}), f32[128,2,120]{2,1,0:T(2,128)S(1)}, u32[]{:S(2)}, u32[]{:S(2)}) async-start(f32[128,2,120]{2,1,0:T(2,128)} %broadcast_in_dim.105), calls=%async_computation.4 | async-start | bytes 262144 | tf_op jit(solution)/shard_map/all_to_all | solution.py:537
  (4 other events, 34.7 us)

commit v4 on v3

--- a/solution.py
+++ b/solution.py
@@ -72,7 +72,7 @@
 
 def head_kernel(
     first, rows, classes, code_ref, recv_ref, mlp_ref, bias_ref, head_ref, gauss_ref,
-    own_ref, up_ref, down_ref, acc_ref, edge_ref, act_ref,
+    own_ref, up_ref, down_ref, acc_ref, edge_ref, act0_ref, act1_ref, logit0_ref, logit1_ref,
 ):
     feat = recv_ref.shape[1]
     padded = head_ref.shape[0]
@@ -81,7 +81,8 @@
     real = lax.broadcasted_iota(jnp.int32, (padded, TILE), 0) < classes
     mlp = mlp_ref[...]
     head = head_ref[...]
-    act_ref[feat:, :] = jnp.ones((act_ref.shape[0] - feat, act_ref.shape[1]), jnp.bfloat16)
+    for act_ref in (act0_ref, act1_ref):
+        act_ref[feat:, :] = jnp.ones((act_ref.shape[0] - feat, rows * TILE), jnp.bfloat16)
 
     @pl.loop(0, ROWS)
     def _(which):
@@ -91,14 +92,10 @@
 
     edge_ref[...] = jnp.zeros_like(edge_ref)
 
-    @pl.loop(0, code_ref[2 * 16])
-    def _(item):
-        code = code_ref[item]
-        slot = code // 8
-        which = (code // 2) % 4
-        side = slot % 2
-        start = (code % 2) * QUAD + jnp.where(side == 0, first, QUAD - first - rows)
-        flat = recv_ref[slot]
+    count = code_ref[code_ref.shape[0] - 1]
+
+    def raise_logits(item, act_ref, logit_ref):
+        flat = recv_ref[code_ref[jnp.minimum(item, count - 1)] // 8]
         hidden = jnp.dot(mlp, flat, preferred_element_type=jnp.float32)
         for group in range(rows // 4):
             tiles = []
@@ -111,15 +108,33 @@
             for i, tile in enumerate(spread_rows(tiles, lane_feat)):
                 at = (group * 4 + i) * TILE
                 act_ref[0:feat, at : at + TILE] = tile.astype(jnp.bfloat16)
-        logits = jnp.dot(head, act_ref[...], preferred_element_type=jnp.float32)
+        logit_ref[...] = jnp.dot(head, act_ref[...], preferred_element_type=jnp.float32)
+
+    def add_up(item, logit_ref):
+        code = code_ref[jnp.minimum(item, count - 1)]
+        which = (code // 2) % 4
+        side = (code // 8) % 2
+        start = (code % 2) * QUAD + jnp.where(side == 0, first, QUAD - first - rows)
+        start = jnp.where(item < count, start, PATCH)
         for i in range(rows):
-            part = logits[:, i * TILE : (i + 1) * TILE]
+            part = logit_ref[:, i * TILE : (i + 1) * TILE]
             top = jnp.max(part, axis=0, keepdims=True)
             raised = jnp.where(real, jnp.exp(part - top), 0.0)
             scale = gauss_ref[pl.ds(start + i, 1), :] / jnp.sum(raised, axis=0, keepdims=True)
             acc_ref[which, side * rows + i] += (
                 (raised * scale).astype(jnp.bfloat16).astype(jnp.float32)
             )
+
+    @pl.when(count > 0)
+    def _():
+        raise_logits(0, act0_ref, logit0_ref)
+
+        @pl.loop(0, (count + 1) // 2)
+        def _(pair):
+            raise_logits(2 * pair + 1, act1_ref, logit1_ref)
+            add_up(2 * pair, logit0_ref)
+            raise_logits(2 * pair + 2, act0_ref, logit0_ref)
+            add_up(2 * pair + 1, logit1_ref)
 
     def merged(row):
         a0, a1, a2, a3 = [acc_ref[which, row] for which in range(ROWS)]
@@ -165,6 +180,9 @@
             pltpu.VMEM((ROWS, 2 * rows, padded, TILE), jnp.float32),
             pltpu.VMEM((padded, TILE), jnp.float32),
             pltpu.VMEM((head_weight.shape[1], rows * TILE), jnp.bfloat16),
+            pltpu.VMEM((head_weight.shape[1], rows * TILE), jnp.bfloat16),
+            pltpu.VMEM((padded, rows * TILE), jnp.float32),
+            pltpu.VMEM((padded, rows * TILE), jnp.float32),
         ],
         compiler_params=pltpu.CompilerParams(vmem_limit_bytes=VMEM_LIMIT),
         cost_estimate=pl.CostEstimate(
@@ -315,55 +333,57 @@
     )(prob, label)
 
 
-def emit_kernel(low, high, prob_ref, *refs):
+def emit_kernel(chunks, *refs):
+    prob_refs = refs[: len(chunks)]
     out_ref, turned_ref, sems = refs[-3:]
-    rows = prob_ref.shape[0]
     _, span_y, classes = out_ref.shape
-    half = rows // 2
-
-    def copy_of(i, at):
-        return pltpu.make_async_copy(
-            turned_ref.at[pl.ds(i * half, half)], out_ref.at[pl.ds(at, half)], sems.at[i]
-        )
-
-    for i, at in enumerate((low, high)):
-
-        @pl.loop(0, half)
-        def _(index):
-            row = i * half + index
-            for j in range(2):
-                block = prob_ref[row, :, j * TILE : (j + 1) * TILE].astype(jnp.float32)
-                block = jnp.transpose(block, (1, 0))
-                stop = min((j + 1) * TILE, span_y)
-                turned_ref[row, j * TILE : stop, :] = block[
-                    : stop - j * TILE, :classes
-                ].astype(jnp.bfloat16)
-
-        copy_of(i, at).start()
-    for i, at in enumerate((low, high)):
-        copy_of(i, at).wait()
-
-
-def emit(prob, low, high, shape, out=None):
-    rows = prob.shape[0]
+    span_x = out_ref.shape[0]
+
+    copies = []
+    base = 0
+    for prob_ref, (first, rows) in zip(prob_refs, chunks):
+        for i, at in enumerate((first, span_x - first - rows)):
+
+            @pl.loop(0, rows)
+            def _(index):
+                for j in range(2):
+                    block = prob_ref[i * rows + index, :, j * TILE : (j + 1) * TILE]
+                    block = jnp.transpose(block.astype(jnp.float32), (1, 0))
+                    stop = min((j + 1) * TILE, span_y)
+                    turned_ref[base + index, j * TILE : stop, :] = block[
+                        : stop - j * TILE, :classes
+                    ].astype(jnp.bfloat16)
+
+            copy = pltpu.make_async_copy(
+                turned_ref.at[pl.ds(base, rows)], out_ref.at[pl.ds(at, rows)], sems.at[len(copies)]
+            )
+            copy.start()
+            copies.append(copy)
+            base += rows
+    for copy in copies:
+        copy.wait()
+
+
+def emit(probs, chunks, shape, *before):
     anywhere = pl.BlockSpec(memory_space=pl.ANY)
-    before = () if out is None else (out,)
+    rows = sum(prob.shape[0] for prob in probs)
+    size = sum(prob.size for prob in probs)
     return pl.pallas_call(
-        functools.partial(emit_kernel, low, high),
-        out_shape=jax.ShapeDtypeStruct(shape, prob.dtype),
-        in_specs=[pl.BlockSpec(memory_space=pltpu.VMEM)] + [anywhere] * len(before),
+        functools.partial(emit_kernel, chunks),
+        out_shape=jax.ShapeDtypeStruct(shape, probs[0].dtype),
+        in_specs=[pl.BlockSpec(memory_space=pltpu.VMEM)] * len(probs) + [anywhere] * len(before),
         out_specs=anywhere,
-        input_output_aliases={1: 0} if before else {},
+        input_output_aliases={len(probs): 0} if before else {},
         scratch_shapes=[
-            pltpu.VMEM((rows,) + shape[1:], prob.dtype),
-            pltpu.SemaphoreType.DMA((2,)),
+            pltpu.VMEM((rows,) + shape[1:], probs[0].dtype),
+            pltpu.SemaphoreType.DMA((2 * len(chunks),)),
         ],
         compiler_params=pltpu.CompilerParams(vmem_limit_bytes=VMEM_LIMIT),
         cost_estimate=pl.CostEstimate(
-            flops=prob.size * 4, bytes_accessed=prob.size * 4, transcendentals=0
+            flops=size * 4, bytes_accessed=size * 4, transcendentals=0
         ),
         name="emit",
-    )(prob, *before)
+    )(*probs, *before)
 
 
 def shifted(block, axis, by):
@@ -372,14 +392,6 @@
     return lax.ppermute(block, axis, pairs)
 
 
-def padded_2(block, sides, width):
-    for axis, dim in sides:
-        low = shifted(lax.slice_in_dim(block, block.shape[dim] - width, None, axis=dim), axis, 1)
-        high = shifted(lax.slice_in_dim(block, 0, width, axis=dim), axis, -1)
-        block = jnp.concatenate([low, block, high], axis=dim)
-    return block
-
-
 def gauss_line():
     position = jnp.arange(PATCH, dtype=jnp.float32) - (PATCH - 1) / 2.0
     sigma = 0.125 * PATCH
@@ -389,7 +401,7 @@
 def gauss_table():
     line = gauss_line()
     table = jnp.exp(-(line[:, None] + line[None, :]))
-    return jnp.pad(table, ((0, 0), (0, TILE - PATCH)))
+    return jnp.pad(table, ((0, QUAD), (0, TILE - PATCH)))
 
 
 def three_parts(values):
@@ -450,7 +462,21 @@
 
     kind = (patch_ids[0, 0] % rows_q - ROWS * here_narrow)[:, None] * 2 + halves[None, :]
     tag = jnp.max(jnp.where(hit, kind[:, :, None], -1), axis=(0, 1)).reshape(wide, 2)
-    tag = lax.all_to_all(tag, "wide", 0, 0, tiled=True).reshape(-1)
+    marked = labels + 1
+    others = jnp.arange(wide, dtype=jnp.int32)[:, None]
+    edges = jnp.where(others == here_wide + 1, marked[span_x - 2 :].reshape(1, -1), 0)
+    edges = jnp.where(others == here_wide - 1, marked[:2].reshape(1, -1), edges)
+    notes = lax.all_to_all(
+        jnp.concatenate([tag, edges], axis=1), "wide", 0, 0, tiled=True
+    )
+    tag = notes[:, :2].reshape(-1)
+
+    def rows_from(device):
+        return jnp.sum(jnp.where(others == device, notes[:, 2:], 0), axis=0).reshape(2, span_y)
+
+    label_wide = jnp.concatenate(
+        [rows_from(here_wide - 1), marked, rows_from(here_wide + 1)], axis=0
+    )
     valid = tag >= 0
     order = jnp.cumsum(valid.astype(jnp.int32)) - 1
     code = jnp.where(valid, columns * 8 + tag, 0)
@@ -463,27 +489,50 @@
     )
 
     table = gauss_table()
-    line = table[:, :PATCH]
+    square = table[:PATCH, :PATCH].reshape(2, QUAD, PATCH)
     kinds = jnp.arange(2 * ROWS, dtype=jnp.int32)
-    counts = jnp.sum(
-        (tag.reshape(wide, 2, 1) == kinds).astype(jnp.float32), axis=0
-    ).reshape(2, ROWS, 2)
-    square = line.reshape(2, QUAD, PATCH)
-    by_row = jnp.sum(
-        counts[:, :, :, None, None] * square[None, None], axis=2
-    )
-    by_row = by_row.transpose(1, 0, 2, 3).reshape(ROWS, span_x, PATCH)
+    counts = jnp.sum((tag.reshape(wide, 2, 1) == kinds).astype(jnp.float32), axis=0)
+
+    def beside(columns, by):
+        block = jnp.concatenate(
+            [columns.astype(jnp.float32), counts.reshape(2 * ROWS, 2)], axis=0
+        )
+        return shifted(block, "narrow", by)
+
+    def parts_of(block):
+        return block[:-2 * ROWS].astype(jnp.int32), block[-2 * ROWS :].reshape(2, 2 * ROWS)
+
+    blocks = beside(label_wide[:, span_y - 2 :], 1), beside(label_wide[:, :2], -1)
+    head_weight = head_matrix(out_weight, out_bias)
+    bias_tile = jnp.broadcast_to(mlp_bias[:, None], (feat, TILE))
+
+    def head_at(chunk):
+        return head_of(
+            received[chunk], codes, mlp_weight, bias_tile, head_weight, table, *CHUNKS[chunk], classes
+        )
+
+    heads = [head_at(0)]
+    received.append(exchange(2, heads[0][2]))
+    heads.append(head_at(1))
+    _, low_block, high_block = lax.optimization_barrier((heads[1][2],) + blocks)
+    label_low, counts_low = parts_of(low_block)
+    label_high, counts_high = parts_of(high_block)
+
+    def plane_of(counts, row):
+        pairs = counts.reshape(2, ROWS, 2)[:, row, :, None, None]
+        return jnp.sum(pairs * square[None], axis=1).reshape(span_x, PATCH)
+
     norm = sum(
-        jnp.pad(by_row[i], ((0, 0), (QUAD * i, QUAD * (ROWS - 1 - i)))) for i in range(ROWS)
-    )
-    came_low = shifted(norm[:, span_y - 2 :], "narrow", 1)
-    came_high = shifted(norm[:, :2], "narrow", -1)
+        jnp.pad(plane_of(counts, i), ((0, 0), (QUAD * i, QUAD * (ROWS - 1 - i))))
+        for i in range(ROWS)
+    )
+    came = plane_of(counts_low, 3)
     norm = jnp.concatenate(
         [
-            came_low[:, :2],
-            norm[:, :QUAD] + came_low[:, 2:],
+            came[:, 46:48] + plane_of(counts_low, 2)[:, 94:96],
+            norm[:, :QUAD] + came[:, 48:],
             norm[:, QUAD:span_y],
-            norm[:, span_y : span_y + 2] + came_high,
+            norm[:, span_y : span_y + 2] + plane_of(counts_high, 0)[:, :2],
         ],
         axis=1,
     )
@@ -491,7 +540,7 @@
     inside = (across >= 0) & (across < narrow * span_y)
     inverse = ring_of(jnp.where(inside[None, :], 1.0 / (norm + 0.001), 0.0))
 
-    label_wide = padded_2(labels + 1, (("wide", 0), ("narrow", 1)), 2)
+    label_wide = jnp.concatenate([label_low, label_wide, label_high], axis=1)
     centre = label_wide[1:-1, 1:-1]
     same = (
         (label_wide[:-2, 1:-1] == centre)
@@ -502,23 +551,13 @@
     boundary = jnp.where(same, 0, centre)
     boundary = ring_of(jnp.pad(boundary, ((0, 0), (1, 1))))
 
-    head_weight = head_matrix(out_weight, out_bias)
-    bias_tile = jnp.broadcast_to(mlp_bias[:, None], (feat, TILE))
     probs = []
-    blended = None
     for chunk, (first, rows) in enumerate(CHUNKS):
-        own, up, down = head_of(
-            received[chunk], codes, mlp_weight, bias_tile, head_weight, table, first, rows, classes
-        )
-        if chunk + 2 < len(CHUNKS):
-            received.append(exchange(chunk + 2, down))
+        own, up, down = heads[chunk] if chunk < 2 else head_at(chunk)
         up = shifted(up, "narrow", 1)
         down = shifted(down, "narrow", -1)
         prob = blend_of(own, up, down, rows_of(inverse, first, rows))
         probs.append(prob)
-        blended = emit(
-            prob, first, span_x - first - rows, (span_x, span_y, classes), blended
-        )
     edge_rows = CHUNKS[0][1]
     before = shifted(probs[0][2 * edge_rows - 2 :], "wide", 1)
     after = shifted(probs[0][:2], "wide", -1)
@@ -533,6 +572,9 @@
         + dice_of(high, boundary[span_x - last + 2 :])
         + dice_of(middle, boundary[last - 2 : span_x - last + 4])
     )[:, :, 0]
+    shape = (span_x, span_y, classes)
+    blended = emit(probs[:1], CHUNKS[:1], shape)
+    blended = emit(probs[1:], CHUNKS[1:], shape, blended)
     whole = jnp.broadcast_to(sums[None], (wide * narrow,) + sums.shape)
     whole = jnp.sum(lax.all_to_all(whole, ("wide", "narrow"), 0, 0, tiled=True), axis=0)
     dice = ((whole[0] + 1.0) / (whole[1] + 1.0))[:classes]

time: 329 us -> 310 us (0.942)
  waiting for transfers between devices: 95 us -> 84.6 us
  Pallas kernels: 123 us -> 113 us
    pallas_call x3, Pallas kernels: 58.9 us -> 49.7 us  [head_of(): pl.pallas_call(functools.partial(head_kernel, first, rows, classes), out_...]
    ppermute x14 -> x10, waiting for transfers between devices: 7.9 us -> 3.04 us  [shifted(): return lax.ppermute(block, axis, pairs)]
    all_to_all x1, waiting for transfers between devices: 5 us -> 0.16 us  [on_device(): lax.all_to_all(whole, ('wide', 'narrow'), 0, 0, tiled=True)]
    pallas_call x3 -> x2, Pallas kernels: 12.5 us -> 11.6 us  [emit(): pl.pallas_call(functools.partial(emit_kernel, chunks), out_shape=jax.Shap...]
    ppermute x14 -> x10, starting transfers between devices: 39.8 us -> 40.3 us  [shifted(): return lax.ppermute(block, axis, pairs)]
  transfers between devices with their start and end apart: 19 -> 15, of which waited for: 6 -> 5; matrix products, arithmetic and copies ran while one was open for 3% -> 3% of each run, Pallas kernels for 34% -> 32%
where the time goes in v4:
time: 310 us
  Pallas kernels  113 us (36%)
  starting transfers between devices  93.9 us (30%)
  waiting for transfers between devices  84.6 us (27%)
  local copies, waits for them, and re-layouts  9.77 us (3%)
  other arithmetic  6.77 us (2%)
    all_to_all x3, waiting for transfers between devices, exchange(): return lax.all_to_all(payload, 'wide', 0, 0, tiled=True).reshape(shape)  79.6 us
    pallas_call x3, Pallas kernels, head_of(): pl.pallas_call(functools.partial(head_kernel, first, rows, classes), out_...  49.7 us
    ppermute x10, starting transfers between devices, shifted(): return lax.ppermute(block, axis, pairs)  40.3 us
    pallas_call x3, Pallas kernels, dice_of(): pl.pallas_call(dice_kernel, out_shape=jax.ShapeDtypeStruct((2, padded, TI...  25.8 us
    all_to_all x3, starting transfers between devices, exchange(): return lax.all_to_all(payload, 'wide', 0, 0, tiled=True).reshape(shape)  25.3 us
    all_to_all x1, starting transfers between devices, on_device(): lax.all_to_all(whole, ('wide', 'narrow'), 0, 0, tiled=True)  20.7 us
    pallas_call x3, Pallas kernels, pack(): pl.pallas_call(functools.partial(pack_kernel, first, rows), out_shape=jax...  14 us
    pallas_call x3, Pallas kernels, blend_of(): pl.pallas_call(blend_kernel, out_shape=jax.ShapeDtypeStruct(own.shape, jn...  12.2 us
  transfers between devices with their start and end apart: 15, of which 5 were waited for; matrix products, arithmetic and copies ran while one was open for 3% of the time, Pallas kernels for 32%

profile of v4, /device:TPU:1, one launch (start us, length us, event | category | flops | bytes accessed | tf_op | source)
XLA Modules:
  0.0 310.5 jit_solution(17847020232772524503)
XLA Ops:
  4.1 7.6 %all-to-all-start = ((s32[16,1,386]{2,1,0:T(1,128)}), s32[16,1,386]{2,1,0:T(1,128)S(1)}, u32[]{:S(2)}, u32[]{:S(2)}) async-start(s32[16,1,386]{2,1,0:T(1,128)} %all_to_all.20), calls=%async_computation | async-start | bytes 65536 | tf_op jit(solution)/shard_map/all_to_all | solution.py:469
  11.7 4.7 %pack.4 = bf16[32,48,1536]{2,1,0:T(8,128)(2,1)} custom-call(s32[32]{0:T(128)S(1)} %get-tuple-element.34.pick_ref, bf16[8,48,9216]{2,1,0:T(8,128)(2,1)} %bitcast.61), custom_call_target="tpu_custom_call" | custom-call | bytes 9437184 | tf_op jit(solution)/shard_map/pack/pallas_call | solution.py:48
  18.1 5.1 %all-to-all-start.2 = ((bf16[16,2,48,1536]{3,2,1,0:T(8,128)(2,1)}), bf16[16,2,48,1536]{3,2,1,0:T(8,128)(2,1)}, u32[]{:S(2)}, u32[]{:S(2)}) async-start(bf16[16,2,48,1536]{3,2,1,0:T(8,128)(2,1)} %bitcast.67), calls=%async_computation.2 | async-start | bytes 9437184 | tf_op jit(solution)/shard_map/all_to_all | solution.py:459
  23.2 4.7 %pack.3 = bf16[32,48,1536]{2,1,0:T(8,128)(2,1)} custom-call(s32[32]{0:T(128)S(1)} %get-tuple-element.34.pick_ref, bf16[8,48,9216]{2,1,0:T(8,128)(2,1)} %bitcast.62), custom_call_target="tpu_custom_call" | custom-call | bytes 9437184 | tf_op jit(solution)/shard_map/pack/pallas_call | solution.py:48
  27.9 60.1 %all-to-all-done.2 = bf16[16,2,48,1536]{3,2,1,0:T(8,128)(2,1)} async-done(((bf16[16,2,48,1536]{3,2,1,0:T(8,128)(2,1)}), bf16[16,2,48,1536]{3,2,1,0:T(8,128)(2,1)}, u32[]{:S(2)}, u32[]{:S(2)}) %all-to-all-start.2) | async-done | bytes 4718624 | tf_op jit(solution)/shard_map/all_to_all | solution.py:459
  88.0 10.8 %all-to-all-start.1 = ((bf16[16,2,48,1536]{3,2,1,0:T(8,128)(2,1)}), bf16[16,2,48,1536]{3,2,1,0:T(8,128)(2,1)}, u32[]{:S(2)}, u32[]{:S(2)}) async-start(bf16[16,2,48,1536]{3,2,1,0:T(8,128)(2,1)} %bitcast.66), calls=%async_computation.1 | async-start | bytes 9437184 | tf_op jit(solution)/shard_map/all_to_all | solution.py:459
  101.5 6.6 %collective-permute-start.2 = (f32[108,2]{1,0:T(8,128)S(1)}, f32[108,2]{1,0:T(8,128)S(1)}, u32[]{:S(2)}, u32[]{:S(2)}) collective-permute-start(f32[108,2]{1,0:T(8,128)S(1)} %get-tuple-element.63), channel_id=1, source_target_pairs={{0,1},{1,2},{2,3},{3,4},{4,5},{5,6},{6,7},{8,9},{9,10},{10,11},{11... | collective-permute-start | bytes 2600 | tf_op jit(solution)/shard_map/ppermute | solution.py:392
  111.2 16.5 %head.4 = (f32[32,120,256]{2,1,0:T(8,128)}, bf16[16,120,128]{2,1,0:T(8,128)(2,1)S(1)}, bf16[120,128]{1,0:T(8,128)(2,1)S(1)}) custom-call(s32[33]{0:T(128)S(1)} %pad_add_fusion.11.code_ref, bf16[32,48,1536]{2,1,0:T(8,128)(2,1)} %bitcast.26.recv_ref, bf16[48,48]{1,0:T(8,128)(2,1)S(1)} %copy-done.2, f32[48,128]{1,0:T(8,128)S(1)} %broadcast_in_dim.157.bias_ref, ...), custom_call_target="tpu_custom_call" | custom-call | flops 300000000 | bytes 8333333 | tf_op jit(solution)/shard_map/head/pallas_call | solution.py:170
  127.7 4.7 %pack.5 = bf16[32,48,1536]{2,1,0:T(8,128)(2,1)} custom-call(s32[32]{0:T(128)S(1)} %get-tuple-element.34.pick_ref, bf16[8,48,9216]{2,1,0:T(8,128)(2,1)} %bitcast.63, bf16[120,128]{1,0:T(8,128)(2,1)S(1)} %get-tuple-element.19.refs_0_), custom_call_target="tpu_custom_call" | custom-call | bytes 9437184 | tf_op jit(solution)/shard_map/pack/pallas_call | solution.py:48
  132.4 19.5 %all-to-all-done.1 = bf16[16,2,48,1536]{3,2,1,0:T(8,128)(2,1)} async-done(((bf16[16,2,48,1536]{3,2,1,0:T(8,128)(2,1)}), bf16[16,2,48,1536]{3,2,1,0:T(8,128)(2,1)}, u32[]{:S(2)}, u32[]{:S(2)}) %all-to-all-start.1) | async-done | bytes 4718624 | tf_op jit(solution)/shard_map/all_to_all | solution.py:459
  151.9 9.4 %all-to-all-start.3 = ((bf16[16,2,48,1536]{3,2,1,0:T(8,128)(2,1)}), bf16[16,2,48,1536]{3,2,1,0:T(8,128)(2,1)}, u32[]{:S(2)}, u32[]{:S(2)}) async-start(bf16[16,2,48,1536]{3,2,1,0:T(8,128)(2,1)} %bitcast.65), calls=%async_computation.3 | async-start | bytes 9437184 | tf_op jit(solution)/shard_map/all_to_all | solution.py:459
  161.3 16.5 %head.3 = (f32[32,120,256]{2,1,0:T(8,128)}, bf16[16,120,128]{2,1,0:T(8,128)(2,1)S(1)}, bf16[120,128]{1,0:T(8,128)(2,1)S(1)}) custom-call(s32[33]{0:T(128)S(1)} %pad_add_fusion.11.code_ref, bf16[32,48,1536]{2,1,0:T(8,128)(2,1)} %bitcast.5.recv_ref, bf16[48,48]{1,0:T(8,128)(2,1)S(1)} %copy-done.2, f32[48,128]{1,0:T(8,128)S(1)} %broadcast_in_dim.157.bias_ref, ...), custom_call_target="tpu_custom_call" | custom-call | flops 300000000 | bytes 8333333 | tf_op jit(solution)/shard_map/head/pallas_call | solution.py:170
  178.8 10.4 %collective-permute-start.7 = (bf16[120,128]{1,0:T(8,128)(2,1)S(1)}, bf16[120,128]{1,0:T(8,128)(2,1)S(1)}, u32[]{:S(2)}, u32[]{:S(2)}) collective-permute-start(bf16[120,128]{1,0:T(8,128)(2,1)S(1)} %get-tuple-element.19.refs_0_), channel_id=1, source_target_pairs={{1,0},{2,1},{3,2},{4,3},{5,4},{6,5},{7,6},{9,8},{10,9},{11,10},{12... | collective-permute-start | bytes 92168 | tf_op jit(solution)/shard_map/ppermute | solution.py:392
  200.5 4.1 %blend.5.refs_0_ = bf16[32,120,256]{2,1,0:T(8,128)(2,1)S(1)} custom-call(f32[32,120,256]{2,1,0:T(8,128)} %get-tuple-element.23.own_ref, bf16[16,120,128]{2,1,0:T(8,128)(2,1)S(1)} %collective-permute-done.6.up_ref, bf16[120,128]{1,0:T(8,128)(2,1)S(1)} %collective-permute-done.7.down_ref, f32[32,256]{1,0:T(8,128)S(1)} %pad_maximum_fusion.7.inv_ref), custom_call_target="tpu_custom_call" | custom-call | flops 3932160 | bytes 6881280 | tf_op jit(solution)/shard_map/blend/pallas_call | solution.py:222
  209.3 4.2 %emit.2.refs_2_ = bf16[96,192,118]{2,1,0:T(8,128)(2,1)} custom-call(bf16[32,120,256]{2,1,0:T(8,128)(2,1)S(1)} %blend.5.refs_0_), custom_call_target="tpu_custom_call" | custom-call | flops 3932160 | bytes 3932160 | tf_op jit(solution)/shard_map/emit/pallas_call | solution.py:371
  213.5 4.1 %blend.3.refs_0_ = bf16[32,120,256]{2,1,0:T(8,128)(2,1)S(1)} custom-call(f32[32,120,256]{2,1,0:T(8,128)} %get-tuple-element.14.own_ref, bf16[16,120,128]{2,1,0:T(8,128)(2,1)S(1)} %collective-permute-done.up_ref, bf16[120,128]{1,0:T(8,128)(2,1)S(1)} %collective-permute-done.1.down_ref, f32[32,256]{1,0:T(8,128)S(1)} %pad_maximum_fusion.6.inv_ref), custom_call_target="tpu_custom_call" | custom-call | flops 3932160 | bytes 6881280 | tf_op jit(solution)/shard_map/blend/pallas_call | solution.py:222
  220.5 16.6 %head.5 = (f32[32,120,256]{2,1,0:T(8,128)}, bf16[16,120,128]{2,1,0:T(8,128)(2,1)S(1)}, bf16[120,128]{1,0:T(8,128)(2,1)S(1)}) custom-call(s32[33]{0:T(128)S(1)} %pad_add_fusion.11.code_ref, bf16[32,48,1536]{2,1,0:T(8,128)(2,1)} %bitcast.28.recv_ref, bf16[48,48]{1,0:T(8,128)(2,1)S(1)} %copy-done.2, f32[48,128]{1,0:T(8,128)S(1)} %broadcast_in_dim.157.bias_ref, ...), custom_call_target="tpu_custom_call" | custom-call | flops 300000000 | bytes 8333333 | tf_op jit(solution)/shard_map/head/pallas_call | solution.py:170
  240.2 6.6 %collective-permute-start.5 = (bf16[120,128]{1,0:T(8,128)(2,1)S(1)}, bf16[120,128]{1,0:T(8,128)(2,1)S(1)}, u32[]{:S(2)}, u32[]{:S(2)}) collective-permute-start(bf16[120,128]{1,0:T(8,128)(2,1)S(1)} %get-tuple-element.22), channel_id=1, source_target_pairs={{1,0},{2,1},{3,2},{4,3},{5,4},{6,5},{7,6},{9,8},{10,9},{11,10},{12... | collective-permute-start | bytes 92168 | tf_op jit(solution)/shard_map/ppermute | solution.py:392
  247.1 8.1 %dice.3 = f32[2,120,128]{2,1,0:T(8,128)S(1)} custom-call(bf16[34,120,256]{2,1,0:T(8,128)(2,1)S(1)} %pad_maximum_fusion.1.prob_ref, s32[32,256]{1,0:T(8,128)S(1)} %get-tuple-element.44.label_ref), custom_call_target="tpu_custom_call" | custom-call | flops 31334400 | bytes 2088960 | tf_op jit(solution)/shard_map/dice/pallas_call | solution.py:318
  255.1 8.1 %dice.4 = f32[2,120,128]{2,1,0:T(8,128)S(1)} custom-call(bf16[34,120,256]{2,1,0:T(8,128)(2,1)S(1)} %pad_maximum_fusion.2.prob_ref, s32[32,256]{1,0:T(8,128)S(1)} %get-tuple-element.45.label_ref), custom_call_target="tpu_custom_call" | custom-call | flops 31334400 | bytes 2088960 | tf_op jit(solution)/shard_map/dice/pallas_call | solution.py:318
  263.2 4.1 %blend.4.refs_1_ = bf16[32,120,256]{2,1,0:T(8,128)(2,1)S(1)} custom-call(f32[32,120,256]{2,1,0:T(8,128)} %get-tuple-element.20.own_ref, bf16[16,120,128]{2,1,0:T(8,128)(2,1)S(1)} %collective-permute-done.4.up_ref, bf16[120,128]{1,0:T(8,128)(2,1)S(1)} %collective-permute-done.5.down_ref, f32[32,256]{1,0:T(8,128)S(1)} %concatenate.76.inv_ref), custom_call_target="tpu_custom_call" | custom-call | flops 3932160 | bytes 6881280 | tf_op jit(solution)/shard_map/blend/pallas_call | solution.py:222
  268.9 9.6 %dice.5 = f32[2,120,128]{2,1,0:T(8,128)S(1)} custom-call(bf16[40,120,256]{2,1,0:T(8,128)(2,1)S(1)} %pad_maximum_fusion.prob_ref, s32[38,256]{1,0:T(8,128)S(1)} %slice.269.label_ref), custom_call_target="tpu_custom_call" | custom-call | flops 36864000 | bytes 2457600 | tf_op jit(solution)/shard_map/dice/pallas_call | solution.py:318
  279.3 20.7 %all-to-all-start.4 = ((f32[128,2,120]{2,1,0:T(2,128)}), f32[128,2,120]{2,1,0:T(2,128)S(1)}, u32[]{:S(2)}, u32[]{:S(2)}) async-start(f32[128,2,120]{2,1,0:T(2,128)} %broadcast_in_dim.165), calls=%async_computation.4 | async-start | bytes 262144 | tf_op jit(solution)/shard_map/all_to_all | solution.py:579
  301.6 7.5 %emit.3 = bf16[96,192,118]{2,1,0:T(8,128)(2,1)} custom-call(bf16[32,120,256]{2,1,0:T(8,128)(2,1)S(1)} %blend.3.refs_0_, bf16[32,120,256]{2,1,0:T(8,128)(2,1)S(1)} %copy-done.1, bf16[96,192,118]{2,1,0:T(8,128)(2,1)} %emit.2.refs_2_), custom_call_target="tpu_custom_call", output_to_operand_aliasing={{}: (2, {})} | custom-call | flops 7864320 | bytes 7864320 | tf_op jit(solution)/shard_map/emit/pallas_call | solution.py:371
  (137 shorter events, 38.3 us)
Async XLA Ops:
  4.1 14.1 %all-to-all-start = ((s32[16,1,386]{2,1,0:T(1,128)}), s32[16,1,386]{2,1,0:T(1,128)S(1)}, u32[]{:S(2)}, u32[]{:S(2)}) async-start(s32[16,1,386]{2,1,0:T(1,128)} %all_to_all.20), calls=%async_computation | async-start | bytes 65536 | tf_op jit(solution)/shard_map/all_to_all | solution.py:469
  18.1 69.9 %all-to-all-start.2 = ((bf16[16,2,48,1536]{3,2,1,0:T(8,128)(2,1)}), bf16[16,2,48,1536]{3,2,1,0:T(8,128)(2,1)}, u32[]{:S(2)}, u32[]{:S(2)}) async-start(bf16[16,2,48,1536]{3,2,1,0:T(8,128)(2,1)} %bitcast.67), calls=%async_computation.2 | async-start | bytes 9437184 | tf_op jit(solution)/shard_map/all_to_all | solution.py:459
  88.0 10.9 %copy-start.9 = (f32[118]{0:T(128)S(1)}, f32[118]{0:T(128)}, u32[]{:S(2)}) copy-start(f32[118]{0:T(128)} %param.15) | copy-start | bytes 1420
  88.0 11.3 %copy-start.7 = (bf16[118,48]{0,1:T(8,128)(2,1)S(1)}, bf16[118,48]{0,1:T(8,128)(2,1)}, u32[]{:S(2)}) copy-start(bf16[118,48]{0,1:T(8,128)(2,1)} %param.14) | copy-start | bytes 33988
  88.0 23.1 %copy-start.8 = (f32[48]{0:T(128)S(1)}, f32[48]{0:T(128)}, u32[]{:S(2)}) copy-start(f32[48]{0:T(128)} %param.13) | copy-start | bytes 580
  88.0 23.2 %copy-start.2 = (bf16[48,48]{1,0:T(8,128)(2,1)S(1)}, bf16[48,48]{1,0:T(8,128)(2,1)}, u32[]{:S(2)}) copy-start(bf16[48,48]{1,0:T(8,128)(2,1)} %mlp_ref.5) | copy-start | bytes 13828
  88.0 63.9 %all-to-all-start.1 = ((bf16[16,2,48,1536]{3,2,1,0:T(8,128)(2,1)}), bf16[16,2,48,1536]{3,2,1,0:T(8,128)(2,1)}, u32[]{:S(2)}, u32[]{:S(2)}) async-start(bf16[16,2,48,1536]{3,2,1,0:T(8,128)(2,1)} %bitcast.66), calls=%async_computation.1 | async-start | bytes 9437184 | tf_op jit(solution)/shard_map/all_to_all | solution.py:459
  101.5 76.3 %collective-permute-start.2 = (f32[108,2]{1,0:T(8,128)S(1)}, f32[108,2]{1,0:T(8,128)S(1)}, u32[]{:S(2)}, u32[]{:S(2)}) collective-permute-start(f32[108,2]{1,0:T(8,128)S(1)} %get-tuple-element.63), channel_id=1, source_target_pairs={{0,1},{1,2},{2,3},{3,4},{4,5},{5,6},{6,7},{8,9},{9,10},{10,11},{11... | collective-permute-start | bytes 2600 | tf_op jit(solution)/shard_map/ppermute | solution.py:392
  108.1 69.8 %collective-permute-start.3 = (f32[108,2]{1,0:T(8,128)S(1)}, f32[108,2]{1,0:T(8,128)S(1)}, u32[]{:S(2)}, u32[]{:S(2)}) collective-permute-start(f32[108,2]{1,0:T(8,128)S(1)} %get-tuple-element.62), channel_id=1, source_target_pairs={{1,0},{2,1},{3,2},{4,3},{5,4},{6,5},{7,6},{9,8},{10,9},{11,10},{12... | collective-permute-start | bytes 2600 | tf_op jit(solution)/shard_map/ppermute | solution.py:392
  151.9 68.5 %all-to-all-start.3 = ((bf16[16,2,48,1536]{3,2,1,0:T(8,128)(2,1)}), bf16[16,2,48,1536]{3,2,1,0:T(8,128)(2,1)}, u32[]{:S(2)}, u32[]{:S(2)}) async-start(bf16[16,2,48,1536]{3,2,1,0:T(8,128)(2,1)} %bitcast.65), calls=%async_computation.3 | async-start | bytes 9437184 | tf_op jit(solution)/shard_map/all_to_all | solution.py:459
  178.8 18.7 %collective-permute-start.7 = (bf16[120,128]{1,0:T(8,128)(2,1)S(1)}, bf16[120,128]{1,0:T(8,128)(2,1)S(1)}, u32[]{:S(2)}, u32[]{:S(2)}) collective-permute-start(bf16[120,128]{1,0:T(8,128)(2,1)S(1)} %get-tuple-element.19.refs_0_), channel_id=1, source_target_pairs={{1,0},{2,1},{3,2},{4,3},{5,4},{6,5},{7,6},{9,8},{10,9},{11,10},{12... | collective-permute-start | bytes 92168 | tf_op jit(solution)/shard_map/ppermute | solution.py:392
  189.2 24.3 %collective-permute-start.1 = (bf16[120,128]{1,0:T(8,128)(2,1)S(1)}, bf16[120,128]{1,0:T(8,128)(2,1)S(1)}, u32[]{:S(2)}, u32[]{:S(2)}) collective-permute-start(bf16[120,128]{1,0:T(8,128)(2,1)S(1)} %get-tuple-element.16), channel_id=1, source_target_pairs={{1,0},{2,1},{3,2},{4,3},{5,4},{6,5},{7,6},{9,8},{10,9},{11,10},{12... | collective-permute-start | bytes 92168 | tf_op jit(solution)/shard_map/ppermute | solution.py:392
  191.1 9.4 %collective-permute-start.6 = (bf16[16,120,128]{2,1,0:T(8,128)(2,1)S(1)}, bf16[16,120,128]{2,1,0:T(8,128)(2,1)S(1)}, u32[]{:S(2)}, u32[]{:S(2)}) collective-permute-start(bf16[16,120,128]{2,1,0:T(8,128)(2,1)S(1)} %get-tuple-element.24), channel_id=1, source_target_pairs={{0,1},{1,2},{2,3},{3,4},{4,5},{5,6},{6,7},{8,9},{9,10},{10,11},{11... | collective-permute-start | bytes 1474568 | tf_op jit(solution)/shard_map/ppermute | solution.py:392
  194.8 18.7 %collective-permute-start = (bf16[16,120,128]{2,1,0:T(8,128)(2,1)S(1)}, bf16[16,120,128]{2,1,0:T(8,128)(2,1)S(1)}, u32[]{:S(2)}, u32[]{:S(2)}) collective-permute-start(bf16[16,120,128]{2,1,0:T(8,128)(2,1)S(1)} %get-tuple-element.15), channel_id=1, source_target_pairs={{0,1},{1,2},{2,3},{3,4},{4,5},{5,6},{6,7},{8,9},{9,10},{10,11},{11... | collective-permute-start | bytes 1474568 | tf_op jit(solution)/shard_map/ppermute | solution.py:392
  204.6 35.3 %collective-permute-start.8 = (bf16[2,120,256]{2,1,0:T(8,128)(2,1)S(1)}, bf16[2,120,256]{2,1,0:T(8,128)(2,1)S(1)}, u32[]{:S(2)}, u32[]{:S(2)}) collective-permute-start(bf16[2,120,256]{2,1,0:T(8,128)(2,1)S(1)} %get-tuple-element.36), channel_id=1, source_target_pairs={{0,8},{8,16},{16,24},{24,32},{32,40},{40,48},{48,56},{56,64},{64,7... | collective-permute-start | bytes 368648 | tf_op jit(solution)/shard_map/ppermute | solution.py:392
  208.0 38.8 %collective-permute-start.9 = (bf16[2,120,256]{2,1,0:T(8,128)(2,1)S(1)}, bf16[2,120,256]{2,1,0:T(8,128)(2,1)S(1)}, u32[]{:S(2)}, u32[]{:S(2)}) collective-permute-start(bf16[2,120,256]{2,1,0:T(8,128)(2,1)S(1)} %get-tuple-element.37), channel_id=1, source_target_pairs={{8,0},{16,8},{24,16},{32,24},{40,32},{48,40},{56,48},{64,56},{72,6... | collective-permute-start | bytes 368648 | tf_op jit(solution)/shard_map/ppermute | solution.py:392
  220.4 19.5 %copy-start.5 = (bf16[16,120,256]{2,1,0:T(8,128)(2,1)S(1)}, bf16[16,120,256]{2,1,0:T(8,128)(2,1)}, u32[]{:S(2)}) copy-start(bf16[16,120,256]{2,1,0:T(8,128)(2,1)} %get-tuple-element.38) | copy-start | bytes 2949124
  220.5 19.5 %copy-start.6 = (bf16[16,120,256]{2,1,0:T(8,128)(2,1)S(1)}, bf16[16,120,256]{2,1,0:T(8,128)(2,1)}, u32[]{:S(2)}) copy-start(bf16[16,120,256]{2,1,0:T(8,128)(2,1)} %get-tuple-element.40) | copy-start | bytes 2949124
  237.1 26.1 %collective-permute-start.4 = (bf16[16,120,128]{2,1,0:T(8,128)(2,1)S(1)}, bf16[16,120,128]{2,1,0:T(8,128)(2,1)S(1)}, u32[]{:S(2)}, u32[]{:S(2)}) collective-permute-start(bf16[16,120,128]{2,1,0:T(8,128)(2,1)S(1)} %get-tuple-element.21), channel_id=1, source_target_pairs={{0,1},{1,2},{2,3},{3,4},{4,5},{5,6},{6,7},{8,9},{9,10},{10,11},{11... | collective-permute-start | bytes 1474568 | tf_op jit(solution)/shard_map/ppermute | solution.py:392
  239.9 6.8 %copy-start.3 = (bf16[16,120,256]{2,1,0:T(8,128)(2,1)S(1)}, bf16[16,120,256]{2,1,0:T(8,128)(2,1)}, u32[]{:S(2)}) copy-start(bf16[16,120,256]{2,1,0:T(8,128)(2,1)} %get-tuple-element.39) | copy-start | bytes 2949124
  239.9 6.8 %copy-start.4 = (bf16[16,120,256]{2,1,0:T(8,128)(2,1)S(1)}, bf16[16,120,256]{2,1,0:T(8,128)(2,1)}, u32[]{:S(2)}) copy-start(bf16[16,120,256]{2,1,0:T(8,128)(2,1)} %get-tuple-element.41) | copy-start | bytes 2949124
  240.2 23.0 %collective-permute-start.5 = (bf16[120,128]{1,0:T(8,128)(2,1)S(1)}, bf16[120,128]{1,0:T(8,128)(2,1)S(1)}, u32[]{:S(2)}, u32[]{:S(2)}) collective-permute-start(bf16[120,128]{1,0:T(8,128)(2,1)S(1)} %get-tuple-element.22), channel_id=1, source_target_pairs={{1,0},{2,1},{3,2},{4,3},{5,4},{6,5},{7,6},{9,8},{10,9},{11,10},{12... | collective-permute-start | bytes 92168 | tf_op jit(solution)/shard_map/ppermute | solution.py:392
  279.3 30.4 %all-to-all-start.4 = ((f32[128,2,120]{2,1,0:T(2,128)}), f32[128,2,120]{2,1,0:T(2,128)S(1)}, u32[]{:S(2)}, u32[]{:S(2)}) async-start(f32[128,2,120]{2,1,0:T(2,128)} %broadcast_in_dim.165), calls=%async_computation.4 | async-start | bytes 262144 | tf_op jit(solution)/shard_map/all_to_all | solution.py:579
  300.0 1.5 copy-start.1
  (1 other events, 1.3 us)

commit v5 on v4

--- a/solution.py
+++ b/solution.py
@@ -12,7 +12,7 @@
 TILE = 128
 RING = 256
 ROWS = 4
-CHUNKS = ((0, 16), (16, 16), (32, 16))
+CHUNKS = ((0, 12), (12, 20), (32, 16))
 VMEM_LIMIT = 50 * 1024 * 1024
 
 
@@ -73,6 +73,7 @@
 def head_kernel(
     first, rows, classes, code_ref, recv_ref, mlp_ref, bias_ref, head_ref, gauss_ref,
     own_ref, up_ref, down_ref, acc_ref, edge_ref, act0_ref, act1_ref, logit0_ref, logit1_ref,
+    half_ref, half_sems, merged_ref, merged_sems,
 ):
     feat = recv_ref.shape[1]
     padded = head_ref.shape[0]
@@ -81,6 +82,22 @@
     real = lax.broadcasted_iota(jnp.int32, (padded, TILE), 0) < classes
     mlp = mlp_ref[...]
     head = head_ref[...]
+    count = code_ref[code_ref.shape[0] - 1]
+
+    def half_copy(item):
+        return pltpu.make_async_copy(
+            recv_ref.at[code_ref[item] // 8], half_ref.at[item], half_sems.at[item]
+        )
+
+    def arrived(item):
+        @pl.when(item < count)
+        def _():
+            half_copy(item).wait()
+
+    @pl.loop(0, count)
+    def _(item):
+        half_copy(item).start()
+
     for act_ref in (act0_ref, act1_ref):
         act_ref[feat:, :] = jnp.ones((act_ref.shape[0] - feat, rows * TILE), jnp.bfloat16)
 
@@ -92,10 +109,8 @@
 
     edge_ref[...] = jnp.zeros_like(edge_ref)
 
-    count = code_ref[code_ref.shape[0] - 1]
-
     def raise_logits(item, act_ref, logit_ref):
-        flat = recv_ref[code_ref[jnp.minimum(item, count - 1)] // 8]
+        flat = half_ref[jnp.minimum(item, count - 1)]
         hidden = jnp.dot(mlp, flat, preferred_element_type=jnp.float32)
         for group in range(rows // 4):
             tiles = []
@@ -127,10 +142,13 @@
 
     @pl.when(count > 0)
     def _():
+        arrived(0)
         raise_logits(0, act0_ref, logit0_ref)
 
         @pl.loop(0, (count + 1) // 2)
         def _(pair):
+            arrived(2 * pair + 1)
+            arrived(2 * pair + 2)
             raise_logits(2 * pair + 1, act1_ref, logit1_ref)
             add_up(2 * pair, logit0_ref)
             raise_logits(2 * pair + 2, act0_ref, logit0_ref)
@@ -146,20 +164,31 @@
             + jnp.where(lane < 96, a2, 0.0)
             + pltpu.roll(a3, 16, 1)
         )
-        own_ref[row, :, 0:TILE] = low
-        own_ref[row, :, TILE:RING] = high
+        merged_ref[row, :, 0:TILE] = low
+        merged_ref[row, :, TILE:RING] = high
         edge_ref[...] = jnp.where(
             (lane == 2 * row) | (lane == 2 * row + 1), pltpu.roll(low, 2 * row, 1), edge_ref[...]
         )
         return high
+
+    def own_copy(pair):
+        place = pl.ds(2 * pair, 2)
+        return pltpu.make_async_copy(
+            merged_ref.at[place], own_ref.at[place], merged_sems.at[pair]
+        )
 
     @pl.loop(0, rows)
     def _(pair):
         even = merged(2 * pair)
         odd = merged(2 * pair + 1)
+        own_copy(pair).start()
         up_ref[pair] = jnp.where(lane < 64, pltpu.roll(even, 66, 1), pltpu.roll(odd, 2, 1)).astype(
             jnp.bfloat16
         )
+
+    @pl.loop(0, rows)
+    def _(pair):
+        own_copy(pair).wait()
 
     down_ref[...] = edge_ref[...].astype(jnp.bfloat16)
 
@@ -174,8 +203,11 @@
             jax.ShapeDtypeStruct((rows, padded, TILE), jnp.bfloat16),
             jax.ShapeDtypeStruct((padded, TILE), jnp.bfloat16),
         ),
-        in_specs=[pl.BlockSpec(memory_space=pltpu.SMEM)] + [whole] * 5,
-        out_specs=(whole, whole, whole),
+        in_specs=[
+            pl.BlockSpec(memory_space=pltpu.SMEM), pl.BlockSpec(memory_space=pl.ANY)
+        ]
+        + [whole] * 4,
+        out_specs=(pl.BlockSpec(memory_space=pl.ANY), whole, whole),
         scratch_shapes=[
             pltpu.VMEM((ROWS, 2 * rows, padded, TILE), jnp.float32),
             pltpu.VMEM((padded, TILE), jnp.float32),
@@ -183,6 +215,10 @@
             pltpu.VMEM((head_weight.shape[1], rows * TILE), jnp.bfloat16),
             pltpu.VMEM((padded, rows * TILE), jnp.float32),
             pltpu.VMEM((padded, rows * TILE), jnp.float32),
+            pltpu.VMEM(recv.shape, recv.dtype),
+            pltpu.SemaphoreType.DMA(recv.shape[:1]),
+            pltpu.VMEM((2 * rows, padded, RING), jnp.float32),
+            pltpu.SemaphoreType.DMA((rows,)),
         ],
         compiler_params=pltpu.CompilerParams(vmem_limit_bytes=VMEM_LIMIT),
         cost_estimate=pl.CostEstimate(
@@ -199,31 +235,35 @@
     first = lax.broadcasted_iota(jnp.int32, (padded, TILE), 0) == 0
     extra = jnp.where(first, 0.001, 0.0)
     down = down_ref[...].astype(jnp.float32)
-
-    def one(row, came, shift):
-        came = pltpu.roll(came, shift, 1)
+    base = pl.program_id(0) * rows
+
+    for row in range(rows):
+        came = up_ref[row // 2].astype(jnp.float32)
+        came = pltpu.roll(came, 126 if row % 2 == 0 else 62, 1)
         low = own_ref[row, :, 0:TILE] + jnp.where(lane < 48, came, 0.0)
         high = own_ref[row, :, TILE:RING] + jnp.where(lane >= 126, came, 0.0)
-        after = pltpu.roll(down, lax.rem(192 - 2 * row, TILE), 1)
+        after = pltpu.roll(down, lax.rem(192 - 2 * (base + row), TILE), 1)
         high = high + jnp.where((lane == 64) | (lane == 65), after, 0.0)
-        scale = inv_ref[pl.ds(row, 1), :]
+        scale = inv_ref[pl.ds(base + row, 1), :]
         prob_ref[row, :, 0:TILE] = ((low + extra) * scale[:, 0:TILE]).astype(jnp.bfloat16)
         prob_ref[row, :, TILE:RING] = ((high + extra) * scale[:, TILE:RING]).astype(jnp.bfloat16)
 
-    @pl.loop(0, rows // 2)
-    def _(pair):
-        came = up_ref[pair].astype(jnp.float32)
-        one(2 * pair, came, 126)
-        one(2 * pair + 1, came, 62)
-
 
 def blend_of(own, up, down, inv):
+    rows, padded, _ = own.shape
     whole = pl.BlockSpec(memory_space=pltpu.VMEM)
+    step = 8
     return pl.pallas_call(
         blend_kernel,
+        grid=(rows // step,),
         out_shape=jax.ShapeDtypeStruct(own.shape, jnp.bfloat16),
-        in_specs=[whole] * 4,
-        out_specs=whole,
+        in_specs=[
+            pl.BlockSpec((step, padded, RING), lambda i: (i, 0, 0)),
+            pl.BlockSpec((step // 2, padded, TILE), lambda i: (i, 0, 0)),
+            whole,
+            whole,
+        ],
+        out_specs=pl.BlockSpec((step, padded, RING), lambda i: (i, 0, 0)),
         compiler_params=pltpu.CompilerParams(vmem_limit_bytes=VMEM_LIMIT),
         cost_estimate=pl.CostEstimate(
             flops=own.size * 4, bytes_accessed=own.size * 7, transcendentals=0
@@ -242,27 +282,27 @@
 def dice_kernel(prob_ref, label_ref, sums_ref, edge_ref, numer_ref, denom_ref):
     padded = prob_ref.shape[1]
     rows = prob_ref.shape[0] - 4
-    lane = lax.broadcasted_iota(jnp.int32, (8, TILE), 1)
-    klass = lax.broadcasted_iota(jnp.int32, (8, TILE), 0) + 1
-    owned = (lane < TILE, lane < 64)
+    groups = [(at, min(16, padded - at)) for at in range(0, padded, 16)]
 
     def tiles_of(ref, row, group):
-        return [
-            ref[row, group : group + 8, i * TILE : (i + 1) * TILE].astype(jnp.float32)
-            for i in range(2)
-        ]
+        at, size = group
+        return [ref[row, at : at + size, i * TILE : (i + 1) * TILE] for i in range(2)]
+
+    def lanes(size):
+        return lax.broadcasted_iota(jnp.int32, (size, TILE), 1)
 
     @pl.loop(0, rows + 2)
     def _(row):
-        for group in range(0, padded, 8):
+        for group in groups:
+            at, size = group
             centre = tiles_of(prob_ref, row + 1, group)
             before, after = tiles_of(prob_ref, row, group), tiles_of(prob_ref, row + 2, group)
-            left, right = turn(centre, True, lane), turn(centre, False, lane)
+            left, right = turn(centre, True, lanes(size)), turn(centre, False, lanes(size))
             for i in range(2):
                 low = jnp.minimum(
                     jnp.minimum(before[i], after[i]), jnp.minimum(left[i], right[i])
                 )
-                edge_ref[row, group : group + 8, i * TILE : (i + 1) * TILE] = centre[
+                edge_ref[row, at : at + size, i * TILE : (i + 1) * TILE] = centre[
                     i
                 ] - jnp.minimum(centre[i], low)
 
@@ -273,36 +313,46 @@
     def _(row):
         def labels_of(at):
             line = label_ref[pl.ds(at, 1), :]
-            return [
-                jnp.broadcast_to(line[:, i * TILE : (i + 1) * TILE], (8, TILE)) for i in range(2)
-            ]
+            return [line[:, i * TILE : (i + 1) * TILE] for i in range(2)]
 
         middle = labels_of(row + 1)
-        near = (labels_of(row), labels_of(row + 2), turn(middle, True, lane), turn(middle, False, lane))
-        for group in range(0, padded, 8):
+        line = lanes(1)
+        near = (labels_of(row), labels_of(row + 2), turn(middle, True, line), turn(middle, False, line))
+        near = [[other[i].astype(jnp.bfloat16) for i in range(2)] for other in near]
+        middle = [middle[i].astype(jnp.bfloat16) for i in range(2)]
+        for group in groups:
+            at, size = group
+            klass = (
+                lax.broadcasted_iota(jnp.int32, (size, TILE), 0) + (1 + at)
+            ).astype(jnp.float32).astype(jnp.bfloat16)
+            lane = lanes(size)
+            zero = jnp.zeros((size, TILE), jnp.bfloat16)
             centre = tiles_of(edge_ref, row + 1, group)
             before, after = tiles_of(edge_ref, row, group), tiles_of(edge_ref, row + 2, group)
             left, right = turn(centre, True, lane), turn(centre, False, lane)
-            numer = numer_ref[group : group + 8, :]
-            denom = denom_ref[group : group + 8, :]
+            numer = numer_ref[at : at + size, :]
+            denom = denom_ref[at : at + size, :]
             for i in range(2):
                 wide = jnp.maximum(
                     jnp.maximum(centre[i], jnp.maximum(before[i], after[i])),
                     jnp.maximum(left[i], right[i]),
                 )
-                here = middle[i] == klass + group
+                here = middle[i] == klass
                 about = here
                 for other in near:
-                    about = about | (other[i] == klass + group)
-                value = jnp.where(about, centre[i], 0.0) + jnp.where(here, wide, 0.0)
-                total = centre[i] + jnp.where(here, 1.0, 0.0)
+                    about = about | (other[i] == klass)
+                value = jnp.where(about, centre[i], zero).astype(jnp.float32)
+                value = value + jnp.where(here, wide, zero).astype(jnp.float32)
+                total = centre[i].astype(jnp.float32) + jnp.where(here, zero + 1, zero).astype(
+                    jnp.float32
+                )
                 if i == 1:
-                    value = jnp.where(owned[i], value, 0.0)
-                    total = jnp.where(owned[i], total, 0.0)
+                    value = jnp.where(lane < 64, value, 0.0)
+                    total = jnp.where(lane < 64, total, 0.0)
                 numer = numer + value
                 denom = denom + total
-            numer_ref[group : group + 8, :] = numer
-            denom_ref[group : group + 8, :] = denom
+            numer_ref[at : at + size, :] = numer
+            denom_ref[at : at + size, :] = denom
 
     sums_ref[0] = jnp.broadcast_to(
         jnp.sum(numer_ref[...], axis=1, keepdims=True), (padded, TILE)
@@ -321,7 +371,7 @@
         in_specs=[whole] * 2,
         out_specs=whole,
         scratch_shapes=[
-            pltpu.VMEM((rows - 2, padded, RING), jnp.float32),
+            pltpu.VMEM((rows - 2, padded, RING), jnp.bfloat16),
             pltpu.VMEM((padded, TILE), jnp.float32),
             pltpu.VMEM((padded, TILE), jnp.float32),
         ],
@@ -511,9 +561,11 @@
             received[chunk], codes, mlp_weight, bias_tile, head_weight, table, *CHUNKS[chunk], classes
         )
 
-    heads = [head_at(0)]
-    received.append(exchange(2, heads[0][2]))
-    heads.append(head_at(1))
+    heads = []
+    for chunk in range(len(CHUNKS) - 1):
+        heads.append(head_at(chunk))
+        if chunk + 2 < len(CHUNKS):
+            received.append(exchange(chunk + 2, heads[chunk][2]))
     _, low_block, high_block = lax.optimization_barrier((heads[1][2],) + blocks)
     label_low, counts_low = parts_of(low_block)
     label_high, counts_high = parts_of(high_block)
@@ -553,7 +605,7 @@
 
     probs = []
     for chunk, (first, rows) in enumerate(CHUNKS):
-        own, up, down = heads[chunk] if chunk < 2 else head_at(chunk)
+        own, up, down = heads[chunk] if chunk + 1 < len(CHUNKS) else head_at(chunk)
         up = shifted(up, "narrow", 1)
         down = shifted(down, "narrow", -1)
         prob = blend_of(own, up, down, rows_of(inverse, first, rows))
@@ -573,8 +625,8 @@
         + dice_of(middle, boundary[last - 2 : span_x - last + 4])
     )[:, :, 0]
     shape = (span_x, span_y, classes)
-    blended = emit(probs[:1], CHUNKS[:1], shape)
-    blended = emit(probs[1:], CHUNKS[1:], shape, blended)
+    blended = emit(probs[:-2], CHUNKS[:-2], shape)
+    blended = emit(probs[-2:], CHUNKS[-2:], shape, blended)
     whole = jnp.broadcast_to(sums[None], (wide * narrow,) + sums.shape)
     whole = jnp.sum(lax.all_to_all(whole, ("wide", "narrow"), 0, 0, tiled=True), axis=0)
     dice = ((whole[0] + 1.0) / (whole[1] + 1.0))[:classes]

time: 310 us -> 291 us (0.939)
  waiting for transfers between devices: 84.6 us -> 68.2 us
    all_to_all x3, waiting for transfers between devices: 79.6 us -> 65.3 us  [exchange(): return lax.all_to_all(payload, 'wide', 0, 0, tiled=True).reshape(shape)]
    ppermute x10, starting transfers between devices: 40.3 us -> 50.7 us  [shifted(): return lax.ppermute(block, axis, pairs)]
    all_to_all x3, starting transfers between devices: 25.3 us -> 18 us  [exchange(): return lax.all_to_all(payload, 'wide', 0, 0, tiled=True).reshape(shape)]
  transfers between devices with their start and end apart: 15 -> 15, of which waited for: 5 -> 4; matrix products, arithmetic and copies ran while one was open for 3% -> 4% of each run, Pallas kernels for 32% -> 33%
where the time goes in v5:
time: 291 us; the launch traced here: 292 us
  Pallas kernels  110 us (38%)
  starting transfers between devices  95.4 us (33%)
  waiting for transfers between devices  68.2 us (23%)
  other arithmetic  8.71 us (3%)
  local copies, waits for them, and re-layouts  7.76 us (3%)
    all_to_all x3, waiting for transfers between devices, exchange(): return lax.all_to_all(payload, 'wide', 0, 0, tiled=True).reshape(shape)  65.3 us
    ppermute x10, starting transfers between devices, shifted(): return lax.ppermute(block, axis, pairs)  50.7 us
    pallas_call x3, Pallas kernels, head_of(): pl.pallas_call(functools.partial(head_kernel, first, rows, classes), out_...  47.7 us
    pallas_call x3, Pallas kernels, dice_of(): pl.pallas_call(dice_kernel, out_shape=jax.ShapeDtypeStruct((2, padded, TI...  24.3 us
    all_to_all x1, starting transfers between devices, on_device(): lax.all_to_all(whole, ('wide', 'narrow'), 0, 0, tiled=True)  19.1 us
    all_to_all x3, starting transfers between devices, exchange(): return lax.all_to_all(payload, 'wide', 0, 0, tiled=True).reshape(shape)  18 us
    pallas_call x3, Pallas kernels, pack(): pl.pallas_call(functools.partial(pack_kernel, first, rows), out_shape=jax...  13.7 us
    pallas_call x2, Pallas kernels, emit(): pl.pallas_call(functools.partial(emit_kernel, chunks), out_shape=jax.Shap...  13.3 us
  transfers between devices with their start and end apart: 15, of which 4 were waited for; matrix products, arithmetic and copies ran while one was open for 4% of the time, Pallas kernels for 33%

profile of v5, /device:TPU:1, one launch (start us, length us, event | category | flops | bytes accessed | tf_op | source)
XLA Modules:
  0.0 291.9 jit_solution(3044499168412883498)
XLA Ops:
  4.1 7.6 %all-to-all-start = ((s32[16,1,386]{2,1,0:T(1,128)}), s32[16,1,386]{2,1,0:T(1,128)S(1)}, u32[]{:S(2)}, u32[]{:S(2)}) async-start(s32[16,1,386]{2,1,0:T(1,128)} %all_to_all.20), calls=%async_computation | async-start | bytes 65536 | tf_op jit(solution)/shard_map/all_to_all | solution.py:519
  11.6 4.1 %pack.4 = bf16[32,48,1152]{2,1,0:T(8,128)(2,1)} custom-call(s32[32]{0:T(128)S(1)} %get-tuple-element.34.pick_ref, bf16[8,48,9216]{2,1,0:T(8,128)(2,1)} %bitcast.61), custom_call_target="tpu_custom_call" | custom-call | bytes 7077888 | tf_op jit(solution)/shard_map/pack/pallas_call | solution.py:48
  18.1 4.5 %all-to-all-start.2 = ((bf16[16,2,48,1152]{3,2,1,0:T(8,128)(2,1)}), bf16[16,2,48,1152]{3,2,1,0:T(8,128)(2,1)}, u32[]{:S(2)}, u32[]{:S(2)}) async-start(bf16[16,2,48,1152]{3,2,1,0:T(8,128)(2,1)} %bitcast.25), calls=%async_computation.2 | async-start | bytes 7077888 | tf_op jit(solution)/shard_map/all_to_all | solution.py:509
  22.6 5.1 %pack.3 = bf16[32,48,1920]{2,1,0:T(8,128)(2,1)} custom-call(s32[32]{0:T(128)S(1)} %get-tuple-element.34.pick_ref, bf16[8,48,9216]{2,1,0:T(8,128)(2,1)} %bitcast.62), custom_call_target="tpu_custom_call" | custom-call | bytes 11796480 | tf_op jit(solution)/shard_map/pack/pallas_call | solution.py:48
  27.7 38.6 %all-to-all-done.2 = bf16[16,2,48,1152]{3,2,1,0:T(8,128)(2,1)} async-done(((bf16[16,2,48,1152]{3,2,1,0:T(8,128)(2,1)}), bf16[16,2,48,1152]{3,2,1,0:T(8,128)(2,1)}, u32[]{:S(2)}, u32[]{:S(2)}) %all-to-all-start.2) | async-done | bytes 3538976 | tf_op jit(solution)/shard_map/all_to_all | solution.py:509
  66.3 4.8 %all-to-all-start.1 = ((bf16[16,2,48,1920]{3,2,1,0:T(8,128)(2,1)}), bf16[16,2,48,1920]{3,2,1,0:T(8,128)(2,1)}, u32[]{:S(2)}, u32[]{:S(2)}) async-start(bf16[16,2,48,1920]{3,2,1,0:T(8,128)(2,1)} %bitcast.64), calls=%async_computation.1 | async-start | bytes 11796480 | tf_op jit(solution)/shard_map/all_to_all | solution.py:509
  73.7 8.4 %collective-permute-start.2 = (f32[108,2]{1,0:T(8,128)S(1)}, f32[108,2]{1,0:T(8,128)S(1)}, u32[]{:S(2)}, u32[]{:S(2)}) collective-permute-start(f32[108,2]{1,0:T(8,128)S(1)} %get-tuple-element.63), channel_id=1, source_target_pairs={{0,1},{1,2},{2,3},{3,4},{4,5},{5,6},{6,7},{8,9},{9,10},{10,11},{11... | collective-permute-start | bytes 2600 | tf_op jit(solution)/shard_map/ppermute | solution.py:442
  85.2 15.8 %head.4 = (f32[24,120,256]{2,1,0:T(8,128)S(1)}, bf16[12,120,128]{2,1,0:T(8,128)(2,1)S(1)}, bf16[120,128]{1,0:T(8,128)(2,1)S(1)}) custom-call(s32[33]{0:T(128)S(1)} %pad_add_fusion.11.code_ref, bf16[32,48,1152]{2,1,0:T(8,128)(2,1)} %bitcast.26.recv_ref, bf16[48,48]{1,0:T(8,128)(2,1)S(1)} %copy-done.2, f32[48,128]{1,0:T(8,128)S(1)} %broadcast_in_dim.157.bias_ref, ...), custom_call_target="tpu_custom_call" | custom-call | flops 225000000 | bytes 6250000 | tf_op jit(solution)/shard_map/head/pallas_call | solution.py:199
  103.0 4.5 %pack.5 = bf16[32,48,1536]{2,1,0:T(8,128)(2,1)} custom-call(s32[32]{0:T(128)S(1)} %get-tuple-element.34.pick_ref, bf16[8,48,9216]{2,1,0:T(8,128)(2,1)} %bitcast.63, bf16[120,128]{1,0:T(8,128)(2,1)S(1)} %get-tuple-element.19.refs_0_), custom_call_target="tpu_custom_call" | custom-call | bytes 9437184 | tf_op jit(solution)/shard_map/pack/pallas_call | solution.py:48
  107.5 5.0 %collective-permute-start.6 = (bf16[12,120,128]{2,1,0:T(8,128)(2,1)S(1)}, bf16[12,120,128]{2,1,0:T(8,128)(2,1)S(1)}, u32[]{:S(2)}, u32[]{:S(2)}) collective-permute-start(bf16[12,120,128]{2,1,0:T(8,128)(2,1)S(1)} %get-tuple-element.24), channel_id=1, source_target_pairs={{0,1},{1,2},{2,3},{3,4},{4,5},{5,6},{6,7},{8,9},{9,10},{10,11},{11... | collective-permute-start | bytes 1105928 | tf_op jit(solution)/shard_map/ppermute | solution.py:442
  112.5 26.7 %all-to-all-done.1 = bf16[16,2,48,1920]{3,2,1,0:T(8,128)(2,1)} async-done(((bf16[16,2,48,1920]{3,2,1,0:T(8,128)(2,1)}), bf16[16,2,48,1920]{3,2,1,0:T(8,128)(2,1)}, u32[]{:S(2)}, u32[]{:S(2)}) %all-to-all-start.1) | async-done | bytes 5898272 | tf_op jit(solution)/shard_map/all_to_all | solution.py:509
  139.2 8.7 %all-to-all-start.3 = ((bf16[16,2,48,1536]{3,2,1,0:T(8,128)(2,1)}), bf16[16,2,48,1536]{3,2,1,0:T(8,128)(2,1)}, u32[]{:S(2)}, u32[]{:S(2)}) async-start(bf16[16,2,48,1536]{3,2,1,0:T(8,128)(2,1)} %bitcast.65), calls=%async_computation.3 | async-start | bytes 9437184 | tf_op jit(solution)/shard_map/all_to_all | solution.py:509
  147.9 17.2 %head.3 = (f32[40,120,256]{2,1,0:T(8,128)}, bf16[20,120,128]{2,1,0:T(8,128)(2,1)S(1)}, bf16[120,128]{1,0:T(8,128)(2,1)S(1)}) custom-call(s32[33]{0:T(128)S(1)} %pad_add_fusion.11.code_ref, bf16[32,48,1920]{2,1,0:T(8,128)(2,1)} %bitcast.5.recv_ref, bf16[48,48]{1,0:T(8,128)(2,1)S(1)} %copy-done.2, f32[48,128]{1,0:T(8,128)S(1)} %broadcast_in_dim.157.bias_ref, ...), custom_call_target="tpu_custom_call" | custom-call | flops 375000000 | bytes 10416666 | tf_op jit(solution)/shard_map/head/pallas_call | solution.py:199
  166.1 6.5 %collective-permute-start.1 = (bf16[120,128]{1,0:T(8,128)(2,1)S(1)}, bf16[120,128]{1,0:T(8,128)(2,1)S(1)}, u32[]{:S(2)}, u32[]{:S(2)}) collective-permute-start(bf16[120,128]{1,0:T(8,128)(2,1)S(1)} %get-tuple-element.16), channel_id=1, source_target_pairs={{1,0},{2,1},{3,2},{4,3},{5,4},{6,5},{7,6},{9,8},{10,9},{11,10},{12... | collective-permute-start | bytes 92168 | tf_op jit(solution)/shard_map/ppermute | solution.py:442
  176.5 5.8 %collective-permute-start.8 = (bf16[2,120,256]{2,1,0:T(8,128)(2,1)}, bf16[2,120,256]{2,1,0:T(8,128)(2,1)}, u32[]{:S(2)}, u32[]{:S(2)}) collective-permute-start(bf16[2,120,256]{2,1,0:T(8,128)(2,1)} %get-tuple-element.40), channel_id=1, source_target_pairs={{0,8},{8,16},{16,24},{24,32},{32,40},{40,48},{48,56},{56,64},{64,7... | collective-permute-start | bytes 368648 | tf_op jit(solution)/shard_map/ppermute | solution.py:442
  182.3 5.3 %collective-permute-start = (bf16[20,120,128]{2,1,0:T(8,128)(2,1)S(1)}, bf16[20,120,128]{2,1,0:T(8,128)(2,1)S(1)}, u32[]{:S(2)}, u32[]{:S(2)}) collective-permute-start(bf16[20,120,128]{2,1,0:T(8,128)(2,1)S(1)} %get-tuple-element.15), channel_id=1, source_target_pairs={{0,1},{1,2},{2,3},{3,4},{4,5},{5,6},{6,7},{8,9},{9,10},{10,11},{11... | collective-permute-start | bytes 1843208 | tf_op jit(solution)/shard_map/ppermute | solution.py:442
  194.7 4.5 %blend.3.refs_0_ = bf16[40,120,256]{2,1,0:T(8,128)(2,1)S(1)} custom-call(f32[40,120,256]{2,1,0:T(8,128)} %get-tuple-element.14.own_ref, bf16[20,120,128]{2,1,0:T(8,128)(2,1)S(1)} %collective-permute-done.up_ref, bf16[120,128]{1,0:T(8,128)(2,1)S(1)} %collective-permute-done.1.down_ref, f32[40,256]{1,0:T(8,128)S(1)} %pad_maximum_fusion.6.inv_ref), custom_call_target="tpu_custom_call" | custom-call | flops 4915200 | bytes 8601600 | tf_op jit(solution)/shard_map/blend/pallas_call | solution.py:256
  200.9 14.6 %head.5 = (f32[32,120,256]{2,1,0:T(8,128)}, bf16[16,120,128]{2,1,0:T(8,128)(2,1)S(1)}, bf16[120,128]{1,0:T(8,128)(2,1)S(1)}) custom-call(s32[33]{0:T(128)S(1)} %pad_add_fusion.11.code_ref, bf16[32,48,1536]{2,1,0:T(8,128)(2,1)} %bitcast.28.recv_ref, bf16[48,48]{1,0:T(8,128)(2,1)S(1)} %copy-done.2, f32[48,128]{1,0:T(8,128)S(1)} %broadcast_in_dim.157.bias_ref, ...), custom_call_target="tpu_custom_call" | custom-call | flops 300000000 | bytes 8333333 | tf_op jit(solution)/shard_map/head/pallas_call | solution.py:199
  215.6 12.7 %collective-permute-start.4 = (bf16[16,120,128]{2,1,0:T(8,128)(2,1)S(1)}, bf16[16,120,128]{2,1,0:T(8,128)(2,1)S(1)}, u32[]{:S(2)}, u32[]{:S(2)}) collective-permute-start(bf16[16,120,128]{2,1,0:T(8,128)(2,1)S(1)} %get-tuple-element.21), channel_id=1, source_target_pairs={{0,1},{1,2},{2,3},{3,4},{4,5},{5,6},{6,7},{8,9},{9,10},{10,11},{11... | collective-permute-start | bytes 1474568 | tf_op jit(solution)/shard_map/ppermute | solution.py:442
  232.8 7.6 %dice.3 = f32[2,120,128]{2,1,0:T(8,128)S(1)} custom-call(bf16[34,120,256]{2,1,0:T(8,128)(2,1)S(1)} %pad_maximum_fusion.1.prob_ref, s32[32,256]{1,0:T(8,128)S(1)} %get-tuple-element.44.label_ref), custom_call_target="tpu_custom_call" | custom-call | flops 31334400 | bytes 2088960 | tf_op jit(solution)/shard_map/dice/pallas_call | solution.py:368
  240.4 7.6 %dice.4 = f32[2,120,128]{2,1,0:T(8,128)S(1)} custom-call(bf16[34,120,256]{2,1,0:T(8,128)(2,1)S(1)} %pad_maximum_fusion.2.prob_ref, s32[32,256]{1,0:T(8,128)S(1)} %get-tuple-element.45.label_ref), custom_call_target="tpu_custom_call" | custom-call | flops 31334400 | bytes 2088960 | tf_op jit(solution)/shard_map/dice/pallas_call | solution.py:368
  251.7 9.1 %dice.5 = f32[2,120,128]{2,1,0:T(8,128)S(1)} custom-call(bf16[40,120,256]{2,1,0:T(8,128)(2,1)S(1)} %pad_maximum_fusion.prob_ref, s32[38,256]{1,0:T(8,128)S(1)} %slice.269.label_ref), custom_call_target="tpu_custom_call" | custom-call | flops 36864000 | bytes 2457600 | tf_op jit(solution)/shard_map/dice/pallas_call | solution.py:368
  261.6 19.1 %all-to-all-start.4 = ((f32[128,2,120]{2,1,0:T(2,128)}), f32[128,2,120]{2,1,0:T(2,128)S(1)}, u32[]{:S(2)}, u32[]{:S(2)}) async-start(f32[128,2,120]{2,1,0:T(2,128)} %broadcast_in_dim.165), calls=%async_computation.4 | async-start | bytes 262144 | tf_op jit(solution)/shard_map/all_to_all | solution.py:631
  280.7 10.0 %emit.3 = bf16[96,192,118]{2,1,0:T(8,128)(2,1)} custom-call(bf16[40,120,256]{2,1,0:T(8,128)(2,1)} %copy-done, bf16[32,120,256]{2,1,0:T(8,128)(2,1)S(1)} %blend.4.refs_1_, bf16[96,192,118]{2,1,0:T(8,128)(2,1)} %emit.2.refs_2_), custom_call_target="tpu_custom_call", output_to_operand_aliasing={{}: (2, {})} | custom-call | flops 8847360 | bytes 8847360 | tf_op jit(solution)/shard_map/emit/pallas_call | solution.py:421
  (138 shorter events, 36.1 us)
Async XLA Ops:
  4.1 14.1 %all-to-all-start = ((s32[16,1,386]{2,1,0:T(1,128)}), s32[16,1,386]{2,1,0:T(1,128)S(1)}, u32[]{:S(2)}, u32[]{:S(2)}) async-start(s32[16,1,386]{2,1,0:T(1,128)} %all_to_all.20), calls=%async_computation | async-start | bytes 65536 | tf_op jit(solution)/shard_map/all_to_all | solution.py:519
  18.1 48.2 %all-to-all-start.2 = ((bf16[16,2,48,1152]{3,2,1,0:T(8,128)(2,1)}), bf16[16,2,48,1152]{3,2,1,0:T(8,128)(2,1)}, u32[]{:S(2)}, u32[]{:S(2)}) async-start(bf16[16,2,48,1152]{3,2,1,0:T(8,128)(2,1)} %bitcast.25), calls=%async_computation.2 | async-start | bytes 7077888 | tf_op jit(solution)/shard_map/all_to_all | solution.py:509
  66.3 4.8 %copy-start.9 = (f32[118]{0:T(128)S(1)}, f32[118]{0:T(128)}, u32[]{:S(2)}) copy-start(f32[118]{0:T(128)} %param.15) | copy-start | bytes 1420
  66.3 5.2 %copy-start.7 = (bf16[118,48]{0,1:T(8,128)(2,1)S(1)}, bf16[118,48]{0,1:T(8,128)(2,1)}, u32[]{:S(2)}) copy-start(bf16[118,48]{0,1:T(8,128)(2,1)} %param.14) | copy-start | bytes 33988
  66.3 18.8 %copy-start.8 = (f32[48]{0:T(128)S(1)}, f32[48]{0:T(128)}, u32[]{:S(2)}) copy-start(f32[48]{0:T(128)} %param.13) | copy-start | bytes 580
  66.3 18.9 %copy-start.2 = (bf16[48,48]{1,0:T(8,128)(2,1)S(1)}, bf16[48,48]{1,0:T(8,128)(2,1)}, u32[]{:S(2)}) copy-start(bf16[48,48]{1,0:T(8,128)(2,1)} %mlp_ref.5) | copy-start | bytes 13828
  66.3 72.8 %all-to-all-start.1 = ((bf16[16,2,48,1920]{3,2,1,0:T(8,128)(2,1)}), bf16[16,2,48,1920]{3,2,1,0:T(8,128)(2,1)}, u32[]{:S(2)}, u32[]{:S(2)}) async-start(bf16[16,2,48,1920]{3,2,1,0:T(8,128)(2,1)} %bitcast.64), calls=%async_computation.1 | async-start | bytes 11796480 | tf_op jit(solution)/shard_map/all_to_all | solution.py:509
  73.7 91.4 %collective-permute-start.2 = (f32[108,2]{1,0:T(8,128)S(1)}, f32[108,2]{1,0:T(8,128)S(1)}, u32[]{:S(2)}, u32[]{:S(2)}) collective-permute-start(f32[108,2]{1,0:T(8,128)S(1)} %get-tuple-element.63), channel_id=1, source_target_pairs={{0,1},{1,2},{2,3},{3,4},{4,5},{5,6},{6,7},{8,9},{9,10},{10,11},{11... | collective-permute-start | bytes 2600 | tf_op jit(solution)/shard_map/ppermute | solution.py:442
  82.1 83.1 %collective-permute-start.3 = (f32[108,2]{1,0:T(8,128)S(1)}, f32[108,2]{1,0:T(8,128)S(1)}, u32[]{:S(2)}, u32[]{:S(2)}) collective-permute-start(f32[108,2]{1,0:T(8,128)S(1)} %get-tuple-element.62), channel_id=1, source_target_pairs={{1,0},{2,1},{3,2},{4,3},{5,4},{6,5},{7,6},{9,8},{10,9},{11,10},{12... | collective-permute-start | bytes 2600 | tf_op jit(solution)/shard_map/ppermute | solution.py:442
  101.0 6.5 %copy-start.1 = (f32[24,120,256]{2,1,0:T(8,128)}, f32[24,120,256]{2,1,0:T(8,128)S(1)}, u32[]{:S(2)}) copy-start(f32[24,120,256]{2,1,0:T(8,128)S(1)} %get-tuple-element.23.own_ref) | copy-start | bytes 8847364
  101.0 71.7 %collective-permute-start.7 = (bf16[120,128]{1,0:T(8,128)(2,1)S(1)}, bf16[120,128]{1,0:T(8,128)(2,1)S(1)}, u32[]{:S(2)}, u32[]{:S(2)}) collective-permute-start(bf16[120,128]{1,0:T(8,128)(2,1)S(1)} %get-tuple-element.19.refs_0_), channel_id=1, source_target_pairs={{1,0},{2,1},{3,2},{4,3},{5,4},{6,5},{7,6},{9,8},{10,9},{11,10},{12... | collective-permute-start | bytes 92168 | tf_op jit(solution)/shard_map/ppermute | solution.py:442
  107.5 65.2 %collective-permute-start.6 = (bf16[12,120,128]{2,1,0:T(8,128)(2,1)S(1)}, bf16[12,120,128]{2,1,0:T(8,128)(2,1)S(1)}, u32[]{:S(2)}, u32[]{:S(2)}) collective-permute-start(bf16[12,120,128]{2,1,0:T(8,128)(2,1)S(1)} %get-tuple-element.24), channel_id=1, source_target_pairs={{0,1},{1,2},{2,3},{3,4},{4,5},{5,6},{6,7},{8,9},{9,10},{10,11},{11... | collective-permute-start | bytes 1105928 | tf_op jit(solution)/shard_map/ppermute | solution.py:442
  139.2 61.7 %all-to-all-start.3 = ((bf16[16,2,48,1536]{3,2,1,0:T(8,128)(2,1)}), bf16[16,2,48,1536]{3,2,1,0:T(8,128)(2,1)}, u32[]{:S(2)}, u32[]{:S(2)}) async-start(bf16[16,2,48,1536]{3,2,1,0:T(8,128)(2,1)} %bitcast.65), calls=%async_computation.3 | async-start | bytes 9437184 | tf_op jit(solution)/shard_map/all_to_all | solution.py:509
  166.1 28.0 %collective-permute-start.1 = (bf16[120,128]{1,0:T(8,128)(2,1)S(1)}, bf16[120,128]{1,0:T(8,128)(2,1)S(1)}, u32[]{:S(2)}, u32[]{:S(2)}) collective-permute-start(bf16[120,128]{1,0:T(8,128)(2,1)S(1)} %get-tuple-element.16), channel_id=1, source_target_pairs={{1,0},{2,1},{3,2},{4,3},{5,4},{6,5},{7,6},{9,8},{10,9},{11,10},{12... | collective-permute-start | bytes 92168 | tf_op jit(solution)/shard_map/ppermute | solution.py:442
  176.5 51.9 %collective-permute-start.8 = (bf16[2,120,256]{2,1,0:T(8,128)(2,1)}, bf16[2,120,256]{2,1,0:T(8,128)(2,1)}, u32[]{:S(2)}, u32[]{:S(2)}) collective-permute-start(bf16[2,120,256]{2,1,0:T(8,128)(2,1)} %get-tuple-element.40), channel_id=1, source_target_pairs={{0,8},{8,16},{16,24},{24,32},{32,40},{40,48},{48,56},{56,64},{64,7... | collective-permute-start | bytes 368648 | tf_op jit(solution)/shard_map/ppermute | solution.py:442
  182.3 12.4 %collective-permute-start = (bf16[20,120,128]{2,1,0:T(8,128)(2,1)S(1)}, bf16[20,120,128]{2,1,0:T(8,128)(2,1)S(1)}, u32[]{:S(2)}, u32[]{:S(2)}) collective-permute-start(bf16[20,120,128]{2,1,0:T(8,128)(2,1)S(1)} %get-tuple-element.15), channel_id=1, source_target_pairs={{0,1},{1,2},{2,3},{3,4},{4,5},{5,6},{6,7},{8,9},{9,10},{10,11},{11... | collective-permute-start | bytes 1843208 | tf_op jit(solution)/shard_map/ppermute | solution.py:442
  187.6 43.9 %collective-permute-start.9 = (bf16[2,120,256]{2,1,0:T(8,128)(2,1)}, bf16[2,120,256]{2,1,0:T(8,128)(2,1)}, u32[]{:S(2)}, u32[]{:S(2)}) collective-permute-start(bf16[2,120,256]{2,1,0:T(8,128)(2,1)} %get-tuple-element.41), channel_id=1, source_target_pairs={{8,0},{16,8},{24,16},{32,24},{40,32},{48,40},{56,48},{64,56},{72,6... | collective-permute-start | bytes 368648 | tf_op jit(solution)/shard_map/ppermute | solution.py:442
  199.2 29.1 %copy-start = (bf16[40,120,256]{2,1,0:T(8,128)(2,1)}, bf16[40,120,256]{2,1,0:T(8,128)(2,1)S(1)}, u32[]{:S(2)}) copy-start(bf16[40,120,256]{2,1,0:T(8,128)(2,1)S(1)} %blend.3.refs_0_) | copy-start | bytes 7372804
  200.9 27.4 %copy-start.4 = (bf16[20,120,256]{2,1,0:T(8,128)(2,1)S(1)}, bf16[20,120,256]{2,1,0:T(8,128)(2,1)}, u32[]{:S(2)}) copy-start(bf16[20,120,256]{2,1,0:T(8,128)(2,1)} %get-tuple-element.36) | copy-start | bytes 3686404
  200.9 27.4 %copy-start.6 = (bf16[12,120,256]{2,1,0:T(8,128)(2,1)S(1)}, bf16[12,120,256]{2,1,0:T(8,128)(2,1)}, u32[]{:S(2)}) copy-start(bf16[12,120,256]{2,1,0:T(8,128)(2,1)} %get-tuple-element.42) | copy-start | bytes 2211844
  215.6 32.5 %collective-permute-start.4 = (bf16[16,120,128]{2,1,0:T(8,128)(2,1)S(1)}, bf16[16,120,128]{2,1,0:T(8,128)(2,1)S(1)}, u32[]{:S(2)}, u32[]{:S(2)}) collective-permute-start(bf16[16,120,128]{2,1,0:T(8,128)(2,1)S(1)} %get-tuple-element.21), channel_id=1, source_target_pairs={{0,1},{1,2},{2,3},{3,4},{4,5},{5,6},{6,7},{8,9},{9,10},{10,11},{11... | collective-permute-start | bytes 1474568 | tf_op jit(solution)/shard_map/ppermute | solution.py:442
  228.4 3.2 %copy-start.3 = (bf16[20,120,256]{2,1,0:T(8,128)(2,1)S(1)}, bf16[20,120,256]{2,1,0:T(8,128)(2,1)}, u32[]{:S(2)}) copy-start(bf16[20,120,256]{2,1,0:T(8,128)(2,1)} %get-tuple-element.37) | copy-start | bytes 3686404
  229.6 18.4 %collective-permute-start.5 = (bf16[120,128]{1,0:T(8,128)(2,1)S(1)}, bf16[120,128]{1,0:T(8,128)(2,1)S(1)}, u32[]{:S(2)}, u32[]{:S(2)}) collective-permute-start(bf16[120,128]{1,0:T(8,128)(2,1)S(1)} %get-tuple-element.22), channel_id=1, source_target_pairs={{1,0},{2,1},{3,2},{4,3},{5,4},{6,5},{7,6},{9,8},{10,9},{11,10},{12... | collective-permute-start | bytes 92168 | tf_op jit(solution)/shard_map/ppermute | solution.py:442
  261.6 29.7 %all-to-all-start.4 = ((f32[128,2,120]{2,1,0:T(2,128)}), f32[128,2,120]{2,1,0:T(2,128)S(1)}, u32[]{:S(2)}, u32[]{:S(2)}) async-start(f32[128,2,120]{2,1,0:T(2,128)} %broadcast_in_dim.165), calls=%async_computation.4 | async-start | bytes 262144 | tf_op jit(solution)/shard_map/all_to_all | solution.py:631
  (1 other events, 3.2 us)

commit v6 on v5

--- a/solution.py
+++ b/solution.py
@@ -60,16 +60,6 @@
     )(pick, feats, *after)
 
 
-def spread_rows(tiles, lane):
-    one, two, three = tiles
-    return (
-        one,
-        jnp.where(lane < 32, pltpu.roll(one, 32, 1), pltpu.roll(two, 32, 1)),
-        jnp.where(lane < 64, pltpu.roll(two, 64, 1), pltpu.roll(three, 64, 1)),
-        pltpu.roll(three, 96, 1),
-    )
-
-
 def head_kernel(
     first, rows, classes, code_ref, recv_ref, mlp_ref, bias_ref, head_ref, gauss_ref,
     own_ref, up_ref, down_ref, acc_ref, edge_ref, act0_ref, act1_ref, logit0_ref, logit1_ref,
@@ -77,7 +67,6 @@
 ):
     feat = recv_ref.shape[1]
     padded = head_ref.shape[0]
-    lane_feat = lax.broadcasted_iota(jnp.int32, (feat, TILE), 1)
     lane = lax.broadcasted_iota(jnp.int32, (padded, TILE), 1)
     real = lax.broadcasted_iota(jnp.int32, (padded, TILE), 0) < classes
     mlp = mlp_ref[...]
@@ -99,30 +88,25 @@
         half_copy(item).start()
 
     for act_ref in (act0_ref, act1_ref):
-        act_ref[feat:, :] = jnp.ones((act_ref.shape[0] - feat, rows * TILE), jnp.bfloat16)
+        act_ref[feat:, :] = jnp.ones((act_ref.shape[0] - feat, rows * PATCH), jnp.bfloat16)
 
     @pl.loop(0, ROWS)
     def _(which):
-        @pl.loop(0, 2 * rows)
-        def _(row):
-            acc_ref[which, row] = jnp.zeros((padded, TILE), jnp.float32)
+        @pl.loop(0, rows // 2)
+        def _(group):
+            acc_ref[which, group] = jnp.zeros((padded, 4 * PATCH), jnp.float32)
 
     edge_ref[...] = jnp.zeros_like(edge_ref)
 
     def raise_logits(item, act_ref, logit_ref):
         flat = half_ref[jnp.minimum(item, count - 1)]
         hidden = jnp.dot(mlp, flat, preferred_element_type=jnp.float32)
-        for group in range(rows // 4):
-            tiles = []
-            for i in range(3):
-                part = slice((group * 3 + i) * TILE, (group * 3 + i + 1) * TILE)
-                tiles.append(
-                    flat[:, part].astype(jnp.float32)
-                    + jnp.maximum(hidden[:, part] + bias_ref[...], 0.0)
-                )
-            for i, tile in enumerate(spread_rows(tiles, lane_feat)):
-                at = (group * 4 + i) * TILE
-                act_ref[0:feat, at : at + TILE] = tile.astype(jnp.bfloat16)
+        for i in range(rows * PATCH // TILE):
+            part = slice(i * TILE, (i + 1) * TILE)
+            act_ref[0:feat, part] = (
+                flat[:, part].astype(jnp.float32)
+                + jnp.maximum(hidden[:, part] + bias_ref[...], 0.0)
+            ).astype(jnp.bfloat16)
         logit_ref[...] = jnp.dot(head, act_ref[...], preferred_element_type=jnp.float32)
 
     def add_up(item, logit_ref):
@@ -131,12 +115,15 @@
         side = (code // 8) % 2
         start = (code % 2) * QUAD + jnp.where(side == 0, first, QUAD - first - rows)
         start = jnp.where(item < count, start, PATCH)
-        for i in range(rows):
+        for i in range(rows * PATCH // TILE):
             part = logit_ref[:, i * TILE : (i + 1) * TILE]
             top = jnp.max(part, axis=0, keepdims=True)
             raised = jnp.where(real, jnp.exp(part - top), 0.0)
-            scale = gauss_ref[pl.ds(start + i, 1), :] / jnp.sum(raised, axis=0, keepdims=True)
-            acc_ref[which, side * rows + i] += (
+            group, lanes = i // 3, slice(i % 3 * TILE, (i % 3 + 1) * TILE)
+            scale = gauss_ref[start // 4 + group, i % 3] / jnp.sum(
+                raised, axis=0, keepdims=True
+            )
+            acc_ref[which, side * (rows // 4) + group, :, lanes] += (
                 (raised * scale).astype(jnp.bfloat16).astype(jnp.float32)
             )
 
@@ -154,16 +141,26 @@
             raise_logits(2 * pair + 2, act0_ref, logit0_ref)
             add_up(2 * pair + 1, logit1_ref)
 
-    def merged(row):
-        a0, a1, a2, a3 = [acc_ref[which, row] for which in range(ROWS)]
-        a1 = pltpu.roll(a1, 48, 1)
-        a2 = pltpu.roll(a2, 96, 1)
-        low = a0 + jnp.where(lane >= 48, a1, 0.0) + jnp.where(lane >= 96, a2, 0.0)
-        high = (
-            jnp.where(lane < 48, a1, 0.0)
-            + jnp.where(lane < 96, a2, 0.0)
-            + pltpu.roll(a3, 16, 1)
-        )
+    def merged(group, i):
+        low = jnp.zeros((padded, TILE), jnp.float32)
+        high = jnp.zeros((padded, TILE), jnp.float32)
+        for which in range(ROWS):
+            for tile in range(3):
+                first_y = max(0, tile * TILE - i * PATCH) + which * QUAD
+                last_y = min(PATCH, (tile + 1) * TILE - i * PATCH) + which * QUAD
+                if first_y >= last_y:
+                    continue
+                part = acc_ref[which, group, :, tile * TILE : (tile + 1) * TILE]
+                shift = (which * QUAD - i * PATCH) % TILE
+                if shift:
+                    part = pltpu.roll(part, shift, 1)
+                if first_y < TILE:
+                    keep = (lane >= first_y) & (lane < last_y)
+                    low = low + jnp.where(keep, part, 0.0)
+                if last_y > TILE:
+                    keep = (lane >= first_y - TILE) & (lane < last_y - TILE)
+                    high = high + jnp.where(keep, part, 0.0)
+        row = 4 * group + i
         merged_ref[row, :, 0:TILE] = low
         merged_ref[row, :, TILE:RING] = high
         edge_ref[...] = jnp.where(
@@ -171,24 +168,25 @@
         )
         return high
 
-    def own_copy(pair):
-        place = pl.ds(2 * pair, 2)
+    def own_copy(group):
+        place = pl.ds(4 * group, 4)
         return pltpu.make_async_copy(
-            merged_ref.at[place], own_ref.at[place], merged_sems.at[pair]
+            merged_ref.at[place], own_ref.at[place], merged_sems.at[group]
         )
 
-    @pl.loop(0, rows)
-    def _(pair):
-        even = merged(2 * pair)
-        odd = merged(2 * pair + 1)
-        own_copy(pair).start()
-        up_ref[pair] = jnp.where(lane < 64, pltpu.roll(even, 66, 1), pltpu.roll(odd, 2, 1)).astype(
-            jnp.bfloat16
-        )
-
-    @pl.loop(0, rows)
-    def _(pair):
-        own_copy(pair).wait()
+    @pl.loop(0, rows // 2)
+    def _(group):
+        for i in range(2):
+            even = merged(group, 2 * i)
+            odd = merged(group, 2 * i + 1)
+            up_ref[2 * group + i] = jnp.where(
+                lane < 64, pltpu.roll(even, 66, 1), pltpu.roll(odd, 2, 1)
+            ).astype(jnp.bfloat16)
+        own_copy(group).start()
+
+    @pl.loop(0, rows // 2)
+    def _(group):
+        own_copy(group).wait()
 
     down_ref[...] = edge_ref[...].astype(jnp.bfloat16)
 
@@ -209,16 +207,16 @@
         + [whole] * 4,
         out_specs=(pl.BlockSpec(memory_space=pl.ANY), whole, whole),
         scratch_shapes=[
-            pltpu.VMEM((ROWS, 2 * rows, padded, TILE), jnp.float32),
+            pltpu.VMEM((ROWS, rows // 2, padded, 4 * PATCH), jnp.float32),
             pltpu.VMEM((padded, TILE), jnp.float32),
-            pltpu.VMEM((head_weight.shape[1], rows * TILE), jnp.bfloat16),
-            pltpu.VMEM((head_weight.shape[1], rows * TILE), jnp.bfloat16),
-            pltpu.VMEM((padded, rows * TILE), jnp.float32),
-            pltpu.VMEM((padded, rows * TILE), jnp.float32),
+            pltpu.VMEM((head_weight.shape[1], rows * PATCH), jnp.bfloat16),
+            pltpu.VMEM((head_weight.shape[1], rows * PATCH), jnp.bfloat16),
+            pltpu.VMEM((padded, rows * PATCH), jnp.float32),
+            pltpu.VMEM((padded, rows * PATCH), jnp.float32),
             pltpu.VMEM(recv.shape, recv.dtype),
             pltpu.SemaphoreType.DMA(recv.shape[:1]),
             pltpu.VMEM((2 * rows, padded, RING), jnp.float32),
-            pltpu.SemaphoreType.DMA((rows,)),
+            pltpu.SemaphoreType.DMA((rows // 2,)),
         ],
         compiler_params=pltpu.CompilerParams(vmem_limit_bytes=VMEM_LIMIT),
         cost_estimate=pl.CostEstimate(
@@ -558,7 +556,8 @@
 
     def head_at(chunk):
         return head_of(
-            received[chunk], codes, mlp_weight, bias_tile, head_weight, table, *CHUNKS[chunk], classes
+            received[chunk], codes, mlp_weight, bias_tile, head_weight,
+            table[:, :PATCH].reshape(-1, 3, 1, TILE), *CHUNKS[chunk], classes
         )
 
     heads = []

time: 291 us -> 286 us (0.983)
  Pallas kernels: 110 us -> 102 us
    pallas_call x3, Pallas kernels: 47.7 us -> 40.2 us  [head_of(): pl.pallas_call(functools.partial(head_kernel, first, rows, classes), out_...]
    all_to_all x1, starting transfers between devices: 19.1 us -> 12.1 us  [on_device(): lax.all_to_all(whole, ('wide', 'narrow'), 0, 0, tiled=True)]
    ppermute x10, starting transfers between devices: 50.7 us -> 56.1 us  [shifted(): return lax.ppermute(block, axis, pairs)]
  transfers between devices with their start and end apart: 15 -> 15, of which waited for: 4 -> 4; matrix products, arithmetic and copies ran while one was open for 4% -> 4% of each run, Pallas kernels for 33% -> 32%
where the time goes in v6:
time: 286 us; the launch traced here: 285 us
  Pallas kernels  102 us (36%)
  starting transfers between devices  93.7 us (33%)
  waiting for transfers between devices  71 us (25%)
  local copies, waits for them, and re-layouts  7.89 us (3%)
  other arithmetic  7.8 us (3%)
    all_to_all x3, waiting for transfers between devices, exchange(): return lax.all_to_all(payload, 'wide', 0, 0, tiled=True).reshape(shape)  68 us
    ppermute x10, starting transfers between devices, shifted(): return lax.ppermute(block, axis, pairs)  56.1 us
    pallas_call x3, Pallas kernels, head_of(): pl.pallas_call(functools.partial(head_kernel, first, rows, classes), out_...  40.2 us
    pallas_call x3, Pallas kernels, dice_of(): pl.pallas_call(dice_kernel, out_shape=jax.ShapeDtypeStruct((2, padded, TI...  24.3 us
    all_to_all x3, starting transfers between devices, exchange(): return lax.all_to_all(payload, 'wide', 0, 0, tiled=True).reshape(shape)  18 us
    pallas_call x3, Pallas kernels, pack(): pl.pallas_call(functools.partial(pack_kernel, first, rows), out_shape=jax...  13.7 us
    pallas_call x2, Pallas kernels, emit(): pl.pallas_call(functools.partial(emit_kernel, chunks), out_shape=jax.Shap...  13.3 us
    all_to_all x1, starting transfers between devices, on_device(): lax.all_to_all(whole, ('wide', 'narrow'), 0, 0, tiled=True)  12.1 us
  transfers between devices with their start and end apart: 15, of which 4 were waited for; matrix products, arithmetic and copies ran while one was open for 4% of the time, Pallas kernels for 32%

profile of v6, /device:TPU:1, one launch (start us, length us, event | category | flops | bytes accessed | tf_op | source)
XLA Modules:
  0.0 284.7 jit_solution(17459536554284484722)
XLA Ops:
  4.1 7.6 %all-to-all-start = ((s32[16,1,386]{2,1,0:T(1,128)}), s32[16,1,386]{2,1,0:T(1,128)S(1)}, u32[]{:S(2)}, u32[]{:S(2)}) async-start(s32[16,1,386]{2,1,0:T(1,128)} %all_to_all.20), calls=%async_computation | async-start | bytes 65536 | tf_op jit(solution)/shard_map/all_to_all | solution.py:517
  11.6 4.1 %pack.4 = bf16[32,48,1152]{2,1,0:T(8,128)(2,1)} custom-call(s32[32]{0:T(128)S(1)} %get-tuple-element.34.pick_ref, bf16[8,48,9216]{2,1,0:T(8,128)(2,1)} %bitcast.61), custom_call_target="tpu_custom_call" | custom-call | bytes 7077888 | tf_op jit(solution)/shard_map/pack/pallas_call | solution.py:48
  18.1 4.5 %all-to-all-start.2 = ((bf16[16,2,48,1152]{3,2,1,0:T(8,128)(2,1)}), bf16[16,2,48,1152]{3,2,1,0:T(8,128)(2,1)}, u32[]{:S(2)}, u32[]{:S(2)}) async-start(bf16[16,2,48,1152]{3,2,1,0:T(8,128)(2,1)} %bitcast.25), calls=%async_computation.2 | async-start | bytes 7077888 | tf_op jit(solution)/shard_map/all_to_all | solution.py:507
  22.6 5.1 %pack.3 = bf16[32,48,1920]{2,1,0:T(8,128)(2,1)} custom-call(s32[32]{0:T(128)S(1)} %get-tuple-element.34.pick_ref, bf16[8,48,9216]{2,1,0:T(8,128)(2,1)} %bitcast.62), custom_call_target="tpu_custom_call" | custom-call | bytes 11796480 | tf_op jit(solution)/shard_map/pack/pallas_call | solution.py:48
  27.8 38.7 %all-to-all-done.2 = bf16[16,2,48,1152]{3,2,1,0:T(8,128)(2,1)} async-done(((bf16[16,2,48,1152]{3,2,1,0:T(8,128)(2,1)}), bf16[16,2,48,1152]{3,2,1,0:T(8,128)(2,1)}, u32[]{:S(2)}, u32[]{:S(2)}) %all-to-all-start.2) | async-done | bytes 3538976 | tf_op jit(solution)/shard_map/all_to_all | solution.py:507
  66.5 4.8 %all-to-all-start.1 = ((bf16[16,2,48,1920]{3,2,1,0:T(8,128)(2,1)}), bf16[16,2,48,1920]{3,2,1,0:T(8,128)(2,1)}, u32[]{:S(2)}, u32[]{:S(2)}) async-start(bf16[16,2,48,1920]{3,2,1,0:T(8,128)(2,1)} %bitcast.64), calls=%async_computation.1 | async-start | bytes 11796480 | tf_op jit(solution)/shard_map/all_to_all | solution.py:507
  74.0 8.1 %collective-permute-start.2 = (f32[108,2]{1,0:T(8,128)S(1)}, f32[108,2]{1,0:T(8,128)S(1)}, u32[]{:S(2)}, u32[]{:S(2)}) collective-permute-start(f32[108,2]{1,0:T(8,128)S(1)} %get-tuple-element.63), channel_id=1, source_target_pairs={{0,1},{1,2},{2,3},{3,4},{4,5},{5,6},{6,7},{8,9},{9,10},{10,11},{11... | collective-permute-start | bytes 2600 | tf_op jit(solution)/shard_map/ppermute | solution.py:440
  85.3 12.1 %head.4 = (f32[24,120,256]{2,1,0:T(8,128)S(1)}, bf16[12,120,128]{2,1,0:T(8,128)(2,1)S(1)}, bf16[120,128]{1,0:T(8,128)(2,1)S(1)}) custom-call(s32[33]{0:T(128)S(1)} %pad_add_fusion.11.code_ref, bf16[32,48,1152]{2,1,0:T(8,128)(2,1)} %bitcast.26.recv_ref, bf16[48,48]{1,0:T(8,128)(2,1)S(1)} %copy-done.2, f32[48,128]{1,0:T(8,128)S(1)} %broadcast_in_dim.157.bias_ref, ...), custom_call_target="tpu_custom_call" | custom-call | flops 225000000 | bytes 6250000 | tf_op jit(solution)/shard_map/head/pallas_call | solution.py:197
  99.3 4.5 %pack.5 = bf16[32,48,1536]{2,1,0:T(8,128)(2,1)} custom-call(s32[32]{0:T(128)S(1)} %get-tuple-element.34.pick_ref, bf16[8,48,9216]{2,1,0:T(8,128)(2,1)} %bitcast.63, bf16[120,128]{1,0:T(8,128)(2,1)S(1)} %get-tuple-element.19.refs_0_), custom_call_target="tpu_custom_call" | custom-call | bytes 9437184 | tf_op jit(solution)/shard_map/pack/pallas_call | solution.py:48
  103.8 6.3 %collective-permute-start.6 = (bf16[12,120,128]{2,1,0:T(8,128)(2,1)S(1)}, bf16[12,120,128]{2,1,0:T(8,128)(2,1)S(1)}, u32[]{:S(2)}, u32[]{:S(2)}) collective-permute-start(bf16[12,120,128]{2,1,0:T(8,128)(2,1)S(1)} %get-tuple-element.24), channel_id=1, source_target_pairs={{0,1},{1,2},{2,3},{3,4},{4,5},{5,6},{6,7},{8,9},{9,10},{10,11},{11... | collective-permute-start | bytes 1105928 | tf_op jit(solution)/shard_map/ppermute | solution.py:440
  110.1 29.3 %all-to-all-done.1 = bf16[16,2,48,1920]{3,2,1,0:T(8,128)(2,1)} async-done(((bf16[16,2,48,1920]{3,2,1,0:T(8,128)(2,1)}), bf16[16,2,48,1920]{3,2,1,0:T(8,128)(2,1)}, u32[]{:S(2)}, u32[]{:S(2)}) %all-to-all-start.1) | async-done | bytes 5898272 | tf_op jit(solution)/shard_map/all_to_all | solution.py:507
  139.4 8.7 %all-to-all-start.3 = ((bf16[16,2,48,1536]{3,2,1,0:T(8,128)(2,1)}), bf16[16,2,48,1536]{3,2,1,0:T(8,128)(2,1)}, u32[]{:S(2)}, u32[]{:S(2)}) async-start(bf16[16,2,48,1536]{3,2,1,0:T(8,128)(2,1)} %bitcast.65), calls=%async_computation.3 | async-start | bytes 9437184 | tf_op jit(solution)/shard_map/all_to_all | solution.py:507
  148.1 15.0 %head.3 = (f32[40,120,256]{2,1,0:T(8,128)}, bf16[20,120,128]{2,1,0:T(8,128)(2,1)S(1)}, bf16[120,128]{1,0:T(8,128)(2,1)S(1)}) custom-call(s32[33]{0:T(128)S(1)} %pad_add_fusion.11.code_ref, bf16[32,48,1920]{2,1,0:T(8,128)(2,1)} %bitcast.5.recv_ref, bf16[48,48]{1,0:T(8,128)(2,1)S(1)} %copy-done.2, f32[48,128]{1,0:T(8,128)S(1)} %broadcast_in_dim.157.bias_ref, ...), custom_call_target="tpu_custom_call" | custom-call | flops 375000000 | bytes 10416666 | tf_op jit(solution)/shard_map/head/pallas_call | solution.py:197
  164.1 4.1 %collective-permute-start.1 = (bf16[120,128]{1,0:T(8,128)(2,1)S(1)}, bf16[120,128]{1,0:T(8,128)(2,1)S(1)}, u32[]{:S(2)}, u32[]{:S(2)}) collective-permute-start(bf16[120,128]{1,0:T(8,128)(2,1)S(1)} %get-tuple-element.16), channel_id=1, source_target_pairs={{1,0},{2,1},{3,2},{4,3},{5,4},{6,5},{7,6},{9,8},{10,9},{11,10},{12... | collective-permute-start | bytes 92168 | tf_op jit(solution)/shard_map/ppermute | solution.py:440
  172.1 8.9 %collective-permute-start.8 = (bf16[2,120,256]{2,1,0:T(8,128)(2,1)}, bf16[2,120,256]{2,1,0:T(8,128)(2,1)}, u32[]{:S(2)}, u32[]{:S(2)}) collective-permute-start(bf16[2,120,256]{2,1,0:T(8,128)(2,1)} %get-tuple-element.40), channel_id=1, source_target_pairs={{0,8},{8,16},{16,24},{24,32},{32,40},{40,48},{48,56},{56,64},{64,7... | collective-permute-start | bytes 368648 | tf_op jit(solution)/shard_map/ppermute | solution.py:440
  180.9 8.3 %collective-permute-start = (bf16[20,120,128]{2,1,0:T(8,128)(2,1)S(1)}, bf16[20,120,128]{2,1,0:T(8,128)(2,1)S(1)}, u32[]{:S(2)}, u32[]{:S(2)}) collective-permute-start(bf16[20,120,128]{2,1,0:T(8,128)(2,1)S(1)} %get-tuple-element.15), channel_id=1, source_target_pairs={{0,1},{1,2},{2,3},{3,4},{4,5},{5,6},{6,7},{8,9},{9,10},{10,11},{11... | collective-permute-start | bytes 1843208 | tf_op jit(solution)/shard_map/ppermute | solution.py:440
  196.3 4.5 %blend.3.refs_0_ = bf16[40,120,256]{2,1,0:T(8,128)(2,1)S(1)} custom-call(f32[40,120,256]{2,1,0:T(8,128)} %get-tuple-element.14.own_ref, bf16[20,120,128]{2,1,0:T(8,128)(2,1)S(1)} %collective-permute-done.up_ref, bf16[120,128]{1,0:T(8,128)(2,1)S(1)} %collective-permute-done.1.down_ref, f32[40,256]{1,0:T(8,128)S(1)} %pad_maximum_fusion.6.inv_ref), custom_call_target="tpu_custom_call" | custom-call | flops 4915200 | bytes 8601600 | tf_op jit(solution)/shard_map/blend/pallas_call | solution.py:254
  202.6 13.1 %head.5 = (f32[32,120,256]{2,1,0:T(8,128)}, bf16[16,120,128]{2,1,0:T(8,128)(2,1)S(1)}, bf16[120,128]{1,0:T(8,128)(2,1)S(1)}) custom-call(s32[33]{0:T(128)S(1)} %pad_add_fusion.11.code_ref, bf16[32,48,1536]{2,1,0:T(8,128)(2,1)} %bitcast.28.recv_ref, bf16[48,48]{1,0:T(8,128)(2,1)S(1)} %copy-done.2, f32[48,128]{1,0:T(8,128)S(1)} %broadcast_in_dim.157.bias_ref, ...), custom_call_target="tpu_custom_call" | custom-call | flops 300000000 | bytes 8333333 | tf_op jit(solution)/shard_map/head/pallas_call | solution.py:197
  215.7 13.2 %collective-permute-start.4 = (bf16[16,120,128]{2,1,0:T(8,128)(2,1)S(1)}, bf16[16,120,128]{2,1,0:T(8,128)(2,1)S(1)}, u32[]{:S(2)}, u32[]{:S(2)}) collective-permute-start(bf16[16,120,128]{2,1,0:T(8,128)(2,1)S(1)} %get-tuple-element.21), channel_id=1, source_target_pairs={{0,1},{1,2},{2,3},{3,4},{4,5},{5,6},{6,7},{8,9},{9,10},{10,11},{11... | collective-permute-start | bytes 1474568 | tf_op jit(solution)/shard_map/ppermute | solution.py:440
  232.6 7.6 %dice.3 = f32[2,120,128]{2,1,0:T(8,128)S(1)} custom-call(bf16[34,120,256]{2,1,0:T(8,128)(2,1)S(1)} %pad_maximum_fusion.1.prob_ref, s32[32,256]{1,0:T(8,128)S(1)} %get-tuple-element.44.label_ref), custom_call_target="tpu_custom_call" | custom-call | flops 31334400 | bytes 2088960 | tf_op jit(solution)/shard_map/dice/pallas_call | solution.py:366
  240.2 7.6 %dice.4 = f32[2,120,128]{2,1,0:T(8,128)S(1)} custom-call(bf16[34,120,256]{2,1,0:T(8,128)(2,1)S(1)} %pad_maximum_fusion.2.prob_ref, s32[32,256]{1,0:T(8,128)S(1)} %get-tuple-element.45.label_ref), custom_call_target="tpu_custom_call" | custom-call | flops 31334400 | bytes 2088960 | tf_op jit(solution)/shard_map/dice/pallas_call | solution.py:366
  251.5 9.1 %dice.5 = f32[2,120,128]{2,1,0:T(8,128)S(1)} custom-call(bf16[40,120,256]{2,1,0:T(8,128)(2,1)S(1)} %pad_maximum_fusion.prob_ref, s32[38,256]{1,0:T(8,128)S(1)} %slice.275.label_ref), custom_call_target="tpu_custom_call" | custom-call | flops 36864000 | bytes 2457600 | tf_op jit(solution)/shard_map/dice/pallas_call | solution.py:366
  261.4 12.1 %all-to-all-start.4 = ((f32[128,2,120]{2,1,0:T(2,128)}), f32[128,2,120]{2,1,0:T(2,128)S(1)}, u32[]{:S(2)}, u32[]{:S(2)}) async-start(f32[128,2,120]{2,1,0:T(2,128)} %broadcast_in_dim.165), calls=%async_computation.4 | async-start | bytes 262144 | tf_op jit(solution)/shard_map/all_to_all | solution.py:630
  273.5 10.0 %emit.3 = bf16[96,192,118]{2,1,0:T(8,128)(2,1)} custom-call(bf16[40,120,256]{2,1,0:T(8,128)(2,1)} %copy-done, bf16[32,120,256]{2,1,0:T(8,128)(2,1)S(1)} %blend.4.refs_1_, bf16[96,192,118]{2,1,0:T(8,128)(2,1)} %emit.2.refs_2_), custom_call_target="tpu_custom_call", output_to_operand_aliasing={{}: (2, {})} | custom-call | flops 8847360 | bytes 8847360 | tf_op jit(solution)/shard_map/emit/pallas_call | solution.py:419
  (139 shorter events, 35.5 us)
Async XLA Ops:
  4.1 14.1 %all-to-all-start = ((s32[16,1,386]{2,1,0:T(1,128)}), s32[16,1,386]{2,1,0:T(1,128)S(1)}, u32[]{:S(2)}, u32[]{:S(2)}) async-start(s32[16,1,386]{2,1,0:T(1,128)} %all_to_all.20), calls=%async_computation | async-start | bytes 65536 | tf_op jit(solution)/shard_map/all_to_all | solution.py:517
  18.1 48.4 %all-to-all-start.2 = ((bf16[16,2,48,1152]{3,2,1,0:T(8,128)(2,1)}), bf16[16,2,48,1152]{3,2,1,0:T(8,128)(2,1)}, u32[]{:S(2)}, u32[]{:S(2)}) async-start(bf16[16,2,48,1152]{3,2,1,0:T(8,128)(2,1)} %bitcast.25), calls=%async_computation.2 | async-start | bytes 7077888 | tf_op jit(solution)/shard_map/all_to_all | solution.py:507
  66.5 4.8 %copy-start.9 = (f32[118]{0:T(128)S(1)}, f32[118]{0:T(128)}, u32[]{:S(2)}) copy-start(f32[118]{0:T(128)} %param.15) | copy-start | bytes 1420
  66.5 5.2 %copy-start.7 = (bf16[118,48]{0,1:T(8,128)(2,1)S(1)}, bf16[118,48]{0,1:T(8,128)(2,1)}, u32[]{:S(2)}) copy-start(bf16[118,48]{0,1:T(8,128)(2,1)} %param.14) | copy-start | bytes 33988
  66.5 18.7 %copy-start.8 = (f32[48]{0:T(128)S(1)}, f32[48]{0:T(128)}, u32[]{:S(2)}) copy-start(f32[48]{0:T(128)} %param.13) | copy-start | bytes 580
  66.5 18.8 %copy-start.2 = (bf16[48,48]{1,0:T(8,128)(2,1)S(1)}, bf16[48,48]{1,0:T(8,128)(2,1)}, u32[]{:S(2)}) copy-start(bf16[48,48]{1,0:T(8,128)(2,1)} %mlp_ref.5) | copy-start | bytes 13828
  66.5 72.9 %all-to-all-start.1 = ((bf16[16,2,48,1920]{3,2,1,0:T(8,128)(2,1)}), bf16[16,2,48,1920]{3,2,1,0:T(8,128)(2,1)}, u32[]{:S(2)}, u32[]{:S(2)}) async-start(bf16[16,2,48,1920]{3,2,1,0:T(8,128)(2,1)} %bitcast.64), calls=%async_computation.1 | async-start | bytes 11796480 | tf_op jit(solution)/shard_map/all_to_all | solution.py:507
  74.0 89.1 %collective-permute-start.2 = (f32[108,2]{1,0:T(8,128)S(1)}, f32[108,2]{1,0:T(8,128)S(1)}, u32[]{:S(2)}, u32[]{:S(2)}) collective-permute-start(f32[108,2]{1,0:T(8,128)S(1)} %get-tuple-element.63), channel_id=1, source_target_pairs={{0,1},{1,2},{2,3},{3,4},{4,5},{5,6},{6,7},{8,9},{9,10},{10,11},{11... | collective-permute-start | bytes 2600 | tf_op jit(solution)/shard_map/ppermute | solution.py:440
  82.2 81.0 %collective-permute-start.3 = (f32[108,2]{1,0:T(8,128)S(1)}, f32[108,2]{1,0:T(8,128)S(1)}, u32[]{:S(2)}, u32[]{:S(2)}) collective-permute-start(f32[108,2]{1,0:T(8,128)S(1)} %get-tuple-element.62), channel_id=1, source_target_pairs={{1,0},{2,1},{3,2},{4,3},{5,4},{6,5},{7,6},{9,8},{10,9},{11,10},{12... | collective-permute-start | bytes 2600 | tf_op jit(solution)/shard_map/ppermute | solution.py:440
  97.3 6.5 %copy-start.1 = (f32[24,120,256]{2,1,0:T(8,128)}, f32[24,120,256]{2,1,0:T(8,128)S(1)}, u32[]{:S(2)}) copy-start(f32[24,120,256]{2,1,0:T(8,128)S(1)} %get-tuple-element.23.own_ref) | copy-start | bytes 8847364
  97.4 71.0 %collective-permute-start.7 = (bf16[120,128]{1,0:T(8,128)(2,1)S(1)}, bf16[120,128]{1,0:T(8,128)(2,1)S(1)}, u32[]{:S(2)}, u32[]{:S(2)}) collective-permute-start(bf16[120,128]{1,0:T(8,128)(2,1)S(1)} %get-tuple-element.19.refs_0_), channel_id=1, source_target_pairs={{1,0},{2,1},{3,2},{4,3},{5,4},{6,5},{7,6},{9,8},{10,9},{11,10},{12... | collective-permute-start | bytes 92168 | tf_op jit(solution)/shard_map/ppermute | solution.py:440
  103.8 64.5 %collective-permute-start.6 = (bf16[12,120,128]{2,1,0:T(8,128)(2,1)S(1)}, bf16[12,120,128]{2,1,0:T(8,128)(2,1)S(1)}, u32[]{:S(2)}, u32[]{:S(2)}) collective-permute-start(bf16[12,120,128]{2,1,0:T(8,128)(2,1)S(1)} %get-tuple-element.24), channel_id=1, source_target_pairs={{0,1},{1,2},{2,3},{3,4},{4,5},{5,6},{6,7},{8,9},{9,10},{10,11},{11... | collective-permute-start | bytes 1105928 | tf_op jit(solution)/shard_map/ppermute | solution.py:440
  139.4 63.2 %all-to-all-start.3 = ((bf16[16,2,48,1536]{3,2,1,0:T(8,128)(2,1)}), bf16[16,2,48,1536]{3,2,1,0:T(8,128)(2,1)}, u32[]{:S(2)}, u32[]{:S(2)}) async-start(bf16[16,2,48,1536]{3,2,1,0:T(8,128)(2,1)} %bitcast.65), calls=%async_computation.3 | async-start | bytes 9437184 | tf_op jit(solution)/shard_map/all_to_all | solution.py:507
  164.1 31.7 %collective-permute-start.1 = (bf16[120,128]{1,0:T(8,128)(2,1)S(1)}, bf16[120,128]{1,0:T(8,128)(2,1)S(1)}, u32[]{:S(2)}, u32[]{:S(2)}) collective-permute-start(bf16[120,128]{1,0:T(8,128)(2,1)S(1)} %get-tuple-element.16), channel_id=1, source_target_pairs={{1,0},{2,1},{3,2},{4,3},{5,4},{6,5},{7,6},{9,8},{10,9},{11,10},{12... | collective-permute-start | bytes 92168 | tf_op jit(solution)/shard_map/ppermute | solution.py:440
  172.1 56.8 %collective-permute-start.8 = (bf16[2,120,256]{2,1,0:T(8,128)(2,1)}, bf16[2,120,256]{2,1,0:T(8,128)(2,1)}, u32[]{:S(2)}, u32[]{:S(2)}) collective-permute-start(bf16[2,120,256]{2,1,0:T(8,128)(2,1)} %get-tuple-element.40), channel_id=1, source_target_pairs={{0,8},{8,16},{16,24},{24,32},{32,40},{40,48},{48,56},{56,64},{64,7... | collective-permute-start | bytes 368648 | tf_op jit(solution)/shard_map/ppermute | solution.py:440
  180.9 15.4 %collective-permute-start = (bf16[20,120,128]{2,1,0:T(8,128)(2,1)S(1)}, bf16[20,120,128]{2,1,0:T(8,128)(2,1)S(1)}, u32[]{:S(2)}, u32[]{:S(2)}) collective-permute-start(bf16[20,120,128]{2,1,0:T(8,128)(2,1)S(1)} %get-tuple-element.15), channel_id=1, source_target_pairs={{0,1},{1,2},{2,3},{3,4},{4,5},{5,6},{6,7},{8,9},{9,10},{10,11},{11... | collective-permute-start | bytes 1843208 | tf_op jit(solution)/shard_map/ppermute | solution.py:440
  189.3 43.0 %collective-permute-start.9 = (bf16[2,120,256]{2,1,0:T(8,128)(2,1)}, bf16[2,120,256]{2,1,0:T(8,128)(2,1)S(1)}, u32[]{:S(2)}, u32[]{:S(2)}) collective-permute-start(bf16[2,120,256]{2,1,0:T(8,128)(2,1)} %get-tuple-element.41), channel_id=1, source_target_pairs={{8,0},{16,8},{24,16},{32,24},{40,32},{48,40},{56,48},{64,56},{72,6... | collective-permute-start | bytes 368648 | tf_op jit(solution)/shard_map/ppermute | solution.py:440
  200.8 28.0 %copy-start = (bf16[40,120,256]{2,1,0:T(8,128)(2,1)}, bf16[40,120,256]{2,1,0:T(8,128)(2,1)S(1)}, u32[]{:S(2)}) copy-start(bf16[40,120,256]{2,1,0:T(8,128)(2,1)S(1)} %blend.3.refs_0_) | copy-start | bytes 7372804
  202.6 26.3 %copy-start.4 = (bf16[20,120,256]{2,1,0:T(8,128)(2,1)S(1)}, bf16[20,120,256]{2,1,0:T(8,128)(2,1)}, u32[]{:S(2)}) copy-start(bf16[20,120,256]{2,1,0:T(8,128)(2,1)} %get-tuple-element.36) | copy-start | bytes 3686404
  202.6 26.3 %copy-start.6 = (bf16[12,120,256]{2,1,0:T(8,128)(2,1)S(1)}, bf16[12,120,256]{2,1,0:T(8,128)(2,1)}, u32[]{:S(2)}) copy-start(bf16[12,120,256]{2,1,0:T(8,128)(2,1)} %get-tuple-element.42) | copy-start | bytes 2211844
  215.7 32.2 %collective-permute-start.4 = (bf16[16,120,128]{2,1,0:T(8,128)(2,1)S(1)}, bf16[16,120,128]{2,1,0:T(8,128)(2,1)S(1)}, u32[]{:S(2)}, u32[]{:S(2)}) collective-permute-start(bf16[16,120,128]{2,1,0:T(8,128)(2,1)S(1)} %get-tuple-element.21), channel_id=1, source_target_pairs={{0,1},{1,2},{2,3},{3,4},{4,5},{5,6},{6,7},{8,9},{9,10},{10,11},{11... | collective-permute-start | bytes 1474568 | tf_op jit(solution)/shard_map/ppermute | solution.py:440
  228.9 3.4 %copy-start.3 = (bf16[20,120,256]{2,1,0:T(8,128)(2,1)S(1)}, bf16[20,120,256]{2,1,0:T(8,128)(2,1)}, u32[]{:S(2)}) copy-start(bf16[20,120,256]{2,1,0:T(8,128)(2,1)} %get-tuple-element.37) | copy-start | bytes 3686404
  230.2 17.7 %collective-permute-start.5 = (bf16[120,128]{1,0:T(8,128)(2,1)S(1)}, bf16[120,128]{1,0:T(8,128)(2,1)S(1)}, u32[]{:S(2)}, u32[]{:S(2)}) collective-permute-start(bf16[120,128]{1,0:T(8,128)(2,1)S(1)} %get-tuple-element.22), channel_id=1, source_target_pairs={{1,0},{2,1},{3,2},{4,3},{5,4},{6,5},{7,6},{9,8},{10,9},{11,10},{12... | collective-permute-start | bytes 92168 | tf_op jit(solution)/shard_map/ppermute | solution.py:440
  261.4 22.6 %all-to-all-start.4 = ((f32[128,2,120]{2,1,0:T(2,128)}), f32[128,2,120]{2,1,0:T(2,128)S(1)}, u32[]{:S(2)}, u32[]{:S(2)}) async-start(f32[128,2,120]{2,1,0:T(2,128)} %broadcast_in_dim.165), calls=%async_computation.4 | async-start | bytes 262144 | tf_op jit(solution)/shard_map/all_to_all | solution.py:630
  (1 other events, 3.4 us)

commit v7 on v6

--- a/solution.py
+++ b/solution.py
@@ -624,8 +624,8 @@
         + dice_of(middle, boundary[last - 2 : span_x - last + 4])
     )[:, :, 0]
     shape = (span_x, span_y, classes)
-    blended = emit(probs[:-2], CHUNKS[:-2], shape)
-    blended = emit(probs[-2:], CHUNKS[-2:], shape, blended)
+    blended = emit(probs[:-1], CHUNKS[:-1], shape)
+    blended = emit(probs[-1:], CHUNKS[-1:], shape, blended)
     whole = jnp.broadcast_to(sums[None], (wide * narrow,) + sums.shape)
     whole = jnp.sum(lax.all_to_all(whole, ("wide", "narrow"), 0, 0, tiled=True), axis=0)
     dice = ((whole[0] + 1.0) / (whole[1] + 1.0))[:classes]

time: 286 us -> 294 us (1.028)
  waiting for transfers between devices: 71 us -> 80.5 us
    ppermute x10, starting transfers between devices: 56.1 us -> 50.8 us  [shifted(): return lax.ppermute(block, axis, pairs)]
    all_to_all x3, waiting for transfers between devices: 68 us -> 73.1 us  [exchange(): return lax.all_to_all(payload, 'wide', 0, 0, tiled=True).reshape(shape)]
    all_to_all x1, waiting for transfers between devices: 0.01 us -> 5 us  [on_device(): lax.all_to_all(whole, ('wide', 'narrow'), 0, 0, tiled=True)]
    all_to_all x1, starting transfers between devices: 12.1 us -> 15.3 us  [on_device(): lax.all_to_all(whole, ('wide', 'narrow'), 0, 0, tiled=True)]
    pallas_call x3, Pallas kernels: 40.2 us -> 43.3 us  [head_of(): pl.pallas_call(functools.partial(head_kernel, first, rows, classes), out_...]
  transfers between devices with their start and end apart: 15 -> 15, of which waited for: 4 -> 5; matrix products, arithmetic and copies ran while one was open for 4% -> 3% of each run, Pallas kernels for 32% -> 31%
where the time goes in v7:
time: 294 us
  Pallas kernels  104 us (35%)
  starting transfers between devices  91.7 us (31%)
  waiting for transfers between devices  80.5 us (27%)
  local copies, waits for them, and re-layouts  8.91 us (3%)
  other arithmetic  6.76 us (2%)
    all_to_all x3, waiting for transfers between devices, exchange(): return lax.all_to_all(payload, 'wide', 0, 0, tiled=True).reshape(shape)  73.1 us
    ppermute x10, starting transfers between devices, shifted(): return lax.ppermute(block, axis, pairs)  50.8 us
    pallas_call x3, Pallas kernels, head_of(): pl.pallas_call(functools.partial(head_kernel, first, rows, classes), out_...  43.3 us
    pallas_call x3, Pallas kernels, dice_of(): pl.pallas_call(dice_kernel, out_shape=jax.ShapeDtypeStruct((2, padded, TI...  24.3 us
    all_to_all x3, starting transfers between devices, exchange(): return lax.all_to_all(payload, 'wide', 0, 0, tiled=True).reshape(shape)  18 us
    all_to_all x1, starting transfers between devices, on_device(): lax.all_to_all(whole, ('wide', 'narrow'), 0, 0, tiled=True)  15.3 us
    pallas_call x3, Pallas kernels, pack(): pl.pallas_call(functools.partial(pack_kernel, first, rows), out_shape=jax...  13.8 us
    pallas_call x2, Pallas kernels, emit(): pl.pallas_call(functools.partial(emit_kernel, chunks), out_shape=jax.Shap...  11.7 us
  transfers between devices with their start and end apart: 15, of which 5 were waited for; matrix products, arithmetic and copies ran while one was open for 3% of the time, Pallas kernels for 31%

profile of v7, /device:TPU:1, one launch (start us, length us, event | category | flops | bytes accessed | tf_op | source)
XLA Modules:
  0.0 293.9 jit_solution(9817102026257391386)
XLA Ops:
  4.1 7.6 %all-to-all-start = ((s32[16,1,386]{2,1,0:T(1,128)}), s32[16,1,386]{2,1,0:T(1,128)S(1)}, u32[]{:S(2)}, u32[]{:S(2)}) async-start(s32[16,1,386]{2,1,0:T(1,128)} %all_to_all.20), calls=%async_computation | async-start | bytes 65536 | tf_op jit(solution)/shard_map/all_to_all | solution.py:517
  18.1 4.5 %all-to-all-start.1 = ((bf16[16,2,48,1152]{3,2,1,0:T(8,128)(2,1)}), bf16[16,2,48,1152]{3,2,1,0:T(8,128)(2,1)}, u32[]{:S(2)}, u32[]{:S(2)}) async-start(bf16[16,2,48,1152]{3,2,1,0:T(8,128)(2,1)} %bitcast.4), calls=%async_computation.1 | async-start | bytes 7077888 | tf_op jit(solution)/shard_map/all_to_all | solution.py:507
  22.6 5.1 %pack.5 = bf16[32,48,1920]{2,1,0:T(8,128)(2,1)} custom-call(s32[32]{0:T(128)S(1)} %get-tuple-element.34.pick_ref, bf16[8,48,9216]{2,1,0:T(8,128)(2,1)} %bitcast.62), custom_call_target="tpu_custom_call" | custom-call | bytes 11796480 | tf_op jit(solution)/shard_map/pack/pallas_call | solution.py:48
  27.8 38.6 %all-to-all-done.1 = bf16[16,2,48,1152]{3,2,1,0:T(8,128)(2,1)} async-done(((bf16[16,2,48,1152]{3,2,1,0:T(8,128)(2,1)}), bf16[16,2,48,1152]{3,2,1,0:T(8,128)(2,1)}, u32[]{:S(2)}, u32[]{:S(2)}) %all-to-all-start.1) | async-done | bytes 3538976 | tf_op jit(solution)/shard_map/all_to_all | solution.py:507
  66.4 4.8 %all-to-all-start.3 = ((bf16[16,2,48,1920]{3,2,1,0:T(8,128)(2,1)}), bf16[16,2,48,1920]{3,2,1,0:T(8,128)(2,1)}, u32[]{:S(2)}, u32[]{:S(2)}) async-start(bf16[16,2,48,1920]{3,2,1,0:T(8,128)(2,1)} %bitcast.64), calls=%async_computation.3 | async-start | bytes 11796480 | tf_op jit(solution)/shard_map/all_to_all | solution.py:507
  73.9 8.4 %collective-permute-start.2 = (f32[108,2]{1,0:T(8,128)S(1)}, f32[108,2]{1,0:T(8,128)S(1)}, u32[]{:S(2)}, u32[]{:S(2)}) collective-permute-start(f32[108,2]{1,0:T(8,128)S(1)} %get-tuple-element.63), channel_id=1, source_target_pairs={{0,1},{1,2},{2,3},{3,4},{4,5},{5,6},{6,7},{8,9},{9,10},{10,11},{11... | collective-permute-start | bytes 2600 | tf_op jit(solution)/shard_map/ppermute | solution.py:440
  85.4 12.9 %head.3 = (f32[24,120,256]{2,1,0:T(8,128)S(1)}, bf16[12,120,128]{2,1,0:T(8,128)(2,1)S(1)}, bf16[120,128]{1,0:T(8,128)(2,1)S(1)}) custom-call(s32[33]{0:T(128)S(1)} %pad_add_fusion.11.code_ref, bf16[32,48,1152]{2,1,0:T(8,128)(2,1)} %bitcast.5.recv_ref, bf16[48,48]{1,0:T(8,128)(2,1)S(1)} %copy-done.3, f32[48,128]{1,0:T(8,128)S(1)} %broadcast_in_dim.157.bias_ref, ...), custom_call_target="tpu_custom_call" | custom-call | flops 225000000 | bytes 6250000 | tf_op jit(solution)/shard_map/head/pallas_call | solution.py:197
  100.3 4.6 %pack.4 = bf16[32,48,1536]{2,1,0:T(8,128)(2,1)} custom-call(s32[32]{0:T(128)S(1)} %get-tuple-element.34.pick_ref, bf16[8,48,9216]{2,1,0:T(8,128)(2,1)} %bitcast.63, bf16[120,128]{1,0:T(8,128)(2,1)S(1)} %get-tuple-element.14.refs_0_), custom_call_target="tpu_custom_call" | custom-call | bytes 9437184 | tf_op jit(solution)/shard_map/pack/pallas_call | solution.py:48
  104.9 4.6 %collective-permute-start.4 = (bf16[12,120,128]{2,1,0:T(8,128)(2,1)S(1)}, bf16[12,120,128]{2,1,0:T(8,128)(2,1)S(1)}, u32[]{:S(2)}, u32[]{:S(2)}) collective-permute-start(bf16[12,120,128]{2,1,0:T(8,128)(2,1)S(1)} %get-tuple-element.22), channel_id=1, source_target_pairs={{0,1},{1,2},{2,3},{3,4},{4,5},{5,6},{6,7},{8,9},{9,10},{10,11},{11... | collective-permute-start | bytes 1105928 | tf_op jit(solution)/shard_map/ppermute | solution.py:440
  109.5 29.7 %all-to-all-done.3 = bf16[16,2,48,1920]{3,2,1,0:T(8,128)(2,1)} async-done(((bf16[16,2,48,1920]{3,2,1,0:T(8,128)(2,1)}), bf16[16,2,48,1920]{3,2,1,0:T(8,128)(2,1)}, u32[]{:S(2)}, u32[]{:S(2)}) %all-to-all-start.3) | async-done | bytes 5898272 | tf_op jit(solution)/shard_map/all_to_all | solution.py:507
  139.2 8.7 %all-to-all-start.2 = ((bf16[16,2,48,1536]{3,2,1,0:T(8,128)(2,1)}), bf16[16,2,48,1536]{3,2,1,0:T(8,128)(2,1)}, u32[]{:S(2)}, u32[]{:S(2)}) async-start(bf16[16,2,48,1536]{3,2,1,0:T(8,128)(2,1)} %bitcast.65), calls=%async_computation.2 | async-start | bytes 9437184 | tf_op jit(solution)/shard_map/all_to_all | solution.py:507
  147.9 16.2 %head.5 = (f32[40,120,256]{2,1,0:T(8,128)}, bf16[20,120,128]{2,1,0:T(8,128)(2,1)S(1)}, bf16[120,128]{1,0:T(8,128)(2,1)S(1)}) custom-call(s32[33]{0:T(128)S(1)} %pad_add_fusion.11.code_ref, bf16[32,48,1920]{2,1,0:T(8,128)(2,1)} %bitcast.12.recv_ref, bf16[48,48]{1,0:T(8,128)(2,1)S(1)} %copy-done.3, f32[48,128]{1,0:T(8,128)S(1)} %broadcast_in_dim.157.bias_ref, ...), custom_call_target="tpu_custom_call" | custom-call | flops 375000000 | bytes 10416666 | tf_op jit(solution)/shard_map/head/pallas_call | solution.py:197
  165.2 6.5 %collective-permute-start.7 = (bf16[120,128]{1,0:T(8,128)(2,1)S(1)}, bf16[120,128]{1,0:T(8,128)(2,1)S(1)}, u32[]{:S(2)}, u32[]{:S(2)}) collective-permute-start(bf16[120,128]{1,0:T(8,128)(2,1)S(1)} %get-tuple-element.18), channel_id=1, source_target_pairs={{1,0},{2,1},{3,2},{4,3},{5,4},{6,5},{7,6},{9,8},{10,9},{11,10},{12... | collective-permute-start | bytes 92168 | tf_op jit(solution)/shard_map/ppermute | solution.py:440
  171.6 4.7 %collective-permute-start.6 = (bf16[20,120,128]{2,1,0:T(8,128)(2,1)S(1)}, bf16[20,120,128]{2,1,0:T(8,128)(2,1)S(1)}, u32[]{:S(2)}, u32[]{:S(2)}) collective-permute-start(bf16[20,120,128]{2,1,0:T(8,128)(2,1)S(1)} %get-tuple-element.24), channel_id=1, source_target_pairs={{0,1},{1,2},{2,3},{3,4},{4,5},{5,6},{6,7},{8,9},{9,10},{10,11},{11... | collective-permute-start | bytes 1843208 | tf_op jit(solution)/shard_map/ppermute | solution.py:440
  180.3 5.9 %collective-permute-start.8 = (bf16[2,120,256]{2,1,0:T(8,128)(2,1)}, bf16[2,120,256]{2,1,0:T(8,128)(2,1)S(1)}, u32[]{:S(2)}, u32[]{:S(2)}) collective-permute-start(bf16[2,120,256]{2,1,0:T(8,128)(2,1)} %get-tuple-element.40), channel_id=1, source_target_pairs={{0,8},{8,16},{16,24},{24,32},{32,40},{40,48},{48,56},{56,64},{64,7... | collective-permute-start | bytes 368648 | tf_op jit(solution)/shard_map/ppermute | solution.py:440
  195.5 4.8 %all-to-all-done.2 = bf16[16,2,48,1536]{3,2,1,0:T(8,128)(2,1)} async-done(((bf16[16,2,48,1536]{3,2,1,0:T(8,128)(2,1)}), bf16[16,2,48,1536]{3,2,1,0:T(8,128)(2,1)}, u32[]{:S(2)}, u32[]{:S(2)}) %all-to-all-start.2) | async-done | bytes 4718624 | tf_op jit(solution)/shard_map/all_to_all | solution.py:507
  200.3 14.1 %head.4 = (f32[32,120,256]{2,1,0:T(8,128)}, bf16[16,120,128]{2,1,0:T(8,128)(2,1)S(1)}, bf16[120,128]{1,0:T(8,128)(2,1)S(1)}) custom-call(s32[33]{0:T(128)S(1)} %pad_add_fusion.11.code_ref, bf16[32,48,1536]{2,1,0:T(8,128)(2,1)} %bitcast.10.recv_ref, bf16[48,48]{1,0:T(8,128)(2,1)S(1)} %copy-done.3, f32[48,128]{1,0:T(8,128)S(1)} %broadcast_in_dim.157.bias_ref, ...), custom_call_target="tpu_custom_call" | custom-call | flops 300000000 | bytes 8333333 | tf_op jit(solution)/shard_map/head/pallas_call | solution.py:197
  214.5 13.3 %collective-permute-start = (bf16[16,120,128]{2,1,0:T(8,128)(2,1)S(1)}, bf16[16,120,128]{2,1,0:T(8,128)(2,1)S(1)}, u32[]{:S(2)}, u32[]{:S(2)}) collective-permute-start(bf16[16,120,128]{2,1,0:T(8,128)(2,1)S(1)} %get-tuple-element.16), channel_id=1, source_target_pairs={{0,1},{1,2},{2,3},{3,4},{4,5},{5,6},{6,7},{8,9},{9,10},{10,11},{11... | collective-permute-start | bytes 1474568 | tf_op jit(solution)/shard_map/ppermute | solution.py:440
  231.7 7.5 %emit.2.refs_1_ = bf16[96,192,118]{2,1,0:T(8,128)(2,1)} custom-call(bf16[24,120,256]{2,1,0:T(8,128)(2,1)S(1)} %copy-done.1, bf16[40,120,256]{2,1,0:T(8,128)(2,1)S(1)} %blend.5.refs_1_), custom_call_target="tpu_custom_call" | custom-call | flops 7864320 | bytes 7864320 | tf_op jit(solution)/shard_map/emit/pallas_call | solution.py:419
  239.3 7.6 %dice.3 = f32[2,120,128]{2,1,0:T(8,128)S(1)} custom-call(bf16[34,120,256]{2,1,0:T(8,128)(2,1)S(1)} %pad_maximum_fusion.1.prob_ref, s32[32,256]{1,0:T(8,128)S(1)} %get-tuple-element.44.label_ref), custom_call_target="tpu_custom_call" | custom-call | flops 31334400 | bytes 2088960 | tf_op jit(solution)/shard_map/dice/pallas_call | solution.py:366
  246.9 7.6 %dice.4 = f32[2,120,128]{2,1,0:T(8,128)S(1)} custom-call(bf16[34,120,256]{2,1,0:T(8,128)(2,1)S(1)} %pad_maximum_fusion.2.prob_ref, s32[32,256]{1,0:T(8,128)S(1)} %get-tuple-element.45.label_ref), custom_call_target="tpu_custom_call" | custom-call | flops 31334400 | bytes 2088960 | tf_op jit(solution)/shard_map/dice/pallas_call | solution.py:366
  258.2 9.1 %dice.5 = f32[2,120,128]{2,1,0:T(8,128)S(1)} custom-call(bf16[40,120,256]{2,1,0:T(8,128)(2,1)S(1)} %pad_maximum_fusion.prob_ref, s32[38,256]{1,0:T(8,128)S(1)} %slice.275.label_ref), custom_call_target="tpu_custom_call" | custom-call | flops 36864000 | bytes 2457600 | tf_op jit(solution)/shard_map/dice/pallas_call | solution.py:366
  268.1 15.3 %all-to-all-start.4 = ((f32[128,2,120]{2,1,0:T(2,128)}), f32[128,2,120]{2,1,0:T(2,128)S(1)}, u32[]{:S(2)}, u32[]{:S(2)}) async-start(f32[128,2,120]{2,1,0:T(2,128)} %broadcast_in_dim.165), calls=%async_computation.4 | async-start | bytes 262144 | tf_op jit(solution)/shard_map/all_to_all | solution.py:630
  288.2 5.0 %all-to-all-done.4 = f32[128,2,120]{2,1,0:T(2,128)S(1)} async-done(((f32[128,2,120]{2,1,0:T(2,128)}), f32[128,2,120]{2,1,0:T(2,128)S(1)}, u32[]{:S(2)}, u32[]{:S(2)}) %all-to-all-start.4) | async-done | bytes 122912 | tf_op jit(solution)/shard_map/all_to_all | solution.py:630
  (141 shorter events, 44.5 us)
Async XLA Ops:
  4.1 14.1 %all-to-all-start = ((s32[16,1,386]{2,1,0:T(1,128)}), s32[16,1,386]{2,1,0:T(1,128)S(1)}, u32[]{:S(2)}, u32[]{:S(2)}) async-start(s32[16,1,386]{2,1,0:T(1,128)} %all_to_all.20), calls=%async_computation | async-start | bytes 65536 | tf_op jit(solution)/shard_map/all_to_all | solution.py:517
  18.1 48.2 %all-to-all-start.1 = ((bf16[16,2,48,1152]{3,2,1,0:T(8,128)(2,1)}), bf16[16,2,48,1152]{3,2,1,0:T(8,128)(2,1)}, u32[]{:S(2)}, u32[]{:S(2)}) async-start(bf16[16,2,48,1152]{3,2,1,0:T(8,128)(2,1)} %bitcast.4), calls=%async_computation.1 | async-start | bytes 7077888 | tf_op jit(solution)/shard_map/all_to_all | solution.py:507
  66.3 4.8 %copy-start.10 = (f32[118]{0:T(128)S(1)}, f32[118]{0:T(128)}, u32[]{:S(2)}) copy-start(f32[118]{0:T(128)} %param.15) | copy-start | bytes 1420
  66.3 5.2 %copy-start.8 = (bf16[118,48]{0,1:T(8,128)(2,1)S(1)}, bf16[118,48]{0,1:T(8,128)(2,1)}, u32[]{:S(2)}) copy-start(bf16[118,48]{0,1:T(8,128)(2,1)} %param.14) | copy-start | bytes 33988
  66.3 19.0 %copy-start.9 = (f32[48]{0:T(128)S(1)}, f32[48]{0:T(128)}, u32[]{:S(2)}) copy-start(f32[48]{0:T(128)} %param.13) | copy-start | bytes 580
  66.4 19.1 %copy-start.3 = (bf16[48,48]{1,0:T(8,128)(2,1)S(1)}, bf16[48,48]{1,0:T(8,128)(2,1)}, u32[]{:S(2)}) copy-start(bf16[48,48]{1,0:T(8,128)(2,1)} %mlp_ref.5) | copy-start | bytes 13828
  66.4 72.9 %all-to-all-start.3 = ((bf16[16,2,48,1920]{3,2,1,0:T(8,128)(2,1)}), bf16[16,2,48,1920]{3,2,1,0:T(8,128)(2,1)}, u32[]{:S(2)}, u32[]{:S(2)}) async-start(bf16[16,2,48,1920]{3,2,1,0:T(8,128)(2,1)} %bitcast.64), calls=%async_computation.3 | async-start | bytes 11796480 | tf_op jit(solution)/shard_map/all_to_all | solution.py:507
  73.9 90.3 %collective-permute-start.2 = (f32[108,2]{1,0:T(8,128)S(1)}, f32[108,2]{1,0:T(8,128)S(1)}, u32[]{:S(2)}, u32[]{:S(2)}) collective-permute-start(f32[108,2]{1,0:T(8,128)S(1)} %get-tuple-element.63), channel_id=1, source_target_pairs={{0,1},{1,2},{2,3},{3,4},{4,5},{5,6},{6,7},{8,9},{9,10},{10,11},{11... | collective-permute-start | bytes 2600 | tf_op jit(solution)/shard_map/ppermute | solution.py:440
  82.3 81.9 %collective-permute-start.3 = (f32[108,2]{1,0:T(8,128)S(1)}, f32[108,2]{1,0:T(8,128)S(1)}, u32[]{:S(2)}, u32[]{:S(2)}) collective-permute-start(f32[108,2]{1,0:T(8,128)S(1)} %get-tuple-element.62), channel_id=1, source_target_pairs={{1,0},{2,1},{3,2},{4,3},{5,4},{6,5},{7,6},{9,8},{10,9},{11,10},{12... | collective-permute-start | bytes 2600 | tf_op jit(solution)/shard_map/ppermute | solution.py:440
  98.3 6.5 %copy-start.2 = (f32[24,120,256]{2,1,0:T(8,128)}, f32[24,120,256]{2,1,0:T(8,128)S(1)}, u32[]{:S(2)}) copy-start(f32[24,120,256]{2,1,0:T(8,128)S(1)} %get-tuple-element.21.own_ref) | copy-start | bytes 8847364
  98.3 78.2 %collective-permute-start.5 = (bf16[120,128]{1,0:T(8,128)(2,1)S(1)}, bf16[120,128]{1,0:T(8,128)(2,1)S(1)}, u32[]{:S(2)}, u32[]{:S(2)}) collective-permute-start(bf16[120,128]{1,0:T(8,128)(2,1)S(1)} %get-tuple-element.14.refs_0_), channel_id=1, source_target_pairs={{1,0},{2,1},{3,2},{4,3},{5,4},{6,5},{7,6},{9,8},{10,9},{11,10},{12... | collective-permute-start | bytes 92168 | tf_op jit(solution)/shard_map/ppermute | solution.py:440
  104.9 71.6 %collective-permute-start.4 = (bf16[12,120,128]{2,1,0:T(8,128)(2,1)S(1)}, bf16[12,120,128]{2,1,0:T(8,128)(2,1)S(1)}, u32[]{:S(2)}, u32[]{:S(2)}) collective-permute-start(bf16[12,120,128]{2,1,0:T(8,128)(2,1)S(1)} %get-tuple-element.22), channel_id=1, source_target_pairs={{0,1},{1,2},{2,3},{3,4},{4,5},{5,6},{6,7},{8,9},{9,10},{10,11},{11... | collective-permute-start | bytes 1105928 | tf_op jit(solution)/shard_map/ppermute | solution.py:440
  139.2 61.1 %all-to-all-start.2 = ((bf16[16,2,48,1536]{3,2,1,0:T(8,128)(2,1)}), bf16[16,2,48,1536]{3,2,1,0:T(8,128)(2,1)}, u32[]{:S(2)}, u32[]{:S(2)}) async-start(bf16[16,2,48,1536]{3,2,1,0:T(8,128)(2,1)} %bitcast.65), calls=%async_computation.2 | async-start | bytes 9437184 | tf_op jit(solution)/shard_map/all_to_all | solution.py:507
  165.2 24.2 %collective-permute-start.7 = (bf16[120,128]{1,0:T(8,128)(2,1)S(1)}, bf16[120,128]{1,0:T(8,128)(2,1)S(1)}, u32[]{:S(2)}, u32[]{:S(2)}) collective-permute-start(bf16[120,128]{1,0:T(8,128)(2,1)S(1)} %get-tuple-element.18), channel_id=1, source_target_pairs={{1,0},{2,1},{3,2},{4,3},{5,4},{6,5},{7,6},{9,8},{10,9},{11,10},{12... | collective-permute-start | bytes 92168 | tf_op jit(solution)/shard_map/ppermute | solution.py:440
  171.6 17.8 %collective-permute-start.6 = (bf16[20,120,128]{2,1,0:T(8,128)(2,1)S(1)}, bf16[20,120,128]{2,1,0:T(8,128)(2,1)S(1)}, u32[]{:S(2)}, u32[]{:S(2)}) collective-permute-start(bf16[20,120,128]{2,1,0:T(8,128)(2,1)S(1)} %get-tuple-element.24), channel_id=1, source_target_pairs={{0,1},{1,2},{2,3},{3,4},{4,5},{5,6},{6,7},{8,9},{9,10},{10,11},{11... | collective-permute-start | bytes 1843208 | tf_op jit(solution)/shard_map/ppermute | solution.py:440
  179.5 9.9 %copy-start = (bf16[24,120,256]{2,1,0:T(8,128)(2,1)}, bf16[24,120,256]{2,1,0:T(8,128)(2,1)S(1)}, u32[]{:S(2)}) copy-start(bf16[24,120,256]{2,1,0:T(8,128)(2,1)S(1)} %blend.4.refs_0_) | copy-start | bytes 4423684
  180.3 47.6 %collective-permute-start.8 = (bf16[2,120,256]{2,1,0:T(8,128)(2,1)}, bf16[2,120,256]{2,1,0:T(8,128)(2,1)S(1)}, u32[]{:S(2)}, u32[]{:S(2)}) collective-permute-start(bf16[2,120,256]{2,1,0:T(8,128)(2,1)} %get-tuple-element.40), channel_id=1, source_target_pairs={{0,8},{8,16},{16,24},{24,32},{32,40},{40,48},{48,56},{56,64},{64,7... | collective-permute-start | bytes 368648 | tf_op jit(solution)/shard_map/ppermute | solution.py:440
  186.2 44.2 %collective-permute-start.9 = (bf16[2,120,256]{2,1,0:T(8,128)(2,1)}, bf16[2,120,256]{2,1,0:T(8,128)(2,1)S(1)}, u32[]{:S(2)}, u32[]{:S(2)}) collective-permute-start(bf16[2,120,256]{2,1,0:T(8,128)(2,1)} %get-tuple-element.41), channel_id=1, source_target_pairs={{8,0},{16,8},{24,16},{32,24},{40,32},{48,40},{56,48},{64,56},{72,6... | collective-permute-start | bytes 368648 | tf_op jit(solution)/shard_map/ppermute | solution.py:440
  200.3 27.5 %copy-start.5 = (bf16[20,120,256]{2,1,0:T(8,128)(2,1)S(1)}, bf16[20,120,256]{2,1,0:T(8,128)(2,1)}, u32[]{:S(2)}) copy-start(bf16[20,120,256]{2,1,0:T(8,128)(2,1)} %get-tuple-element.36) | copy-start | bytes 3686404
  200.3 27.5 %copy-start.7 = (bf16[12,120,256]{2,1,0:T(8,128)(2,1)S(1)}, bf16[12,120,256]{2,1,0:T(8,128)(2,1)}, u32[]{:S(2)}) copy-start(bf16[12,120,256]{2,1,0:T(8,128)(2,1)} %get-tuple-element.42) | copy-start | bytes 2211844
  214.5 40.1 %collective-permute-start = (bf16[16,120,128]{2,1,0:T(8,128)(2,1)S(1)}, bf16[16,120,128]{2,1,0:T(8,128)(2,1)S(1)}, u32[]{:S(2)}, u32[]{:S(2)}) collective-permute-start(bf16[16,120,128]{2,1,0:T(8,128)(2,1)S(1)} %get-tuple-element.16), channel_id=1, source_target_pairs={{0,1},{1,2},{2,3},{3,4},{4,5},{5,6},{6,7},{8,9},{9,10},{10,11},{11... | collective-permute-start | bytes 1474568 | tf_op jit(solution)/shard_map/ppermute | solution.py:440
  227.9 2.5 copy-start.4
  228.1 26.4 %collective-permute-start.1 = (bf16[120,128]{1,0:T(8,128)(2,1)S(1)}, bf16[120,128]{1,0:T(8,128)(2,1)S(1)}, u32[]{:S(2)}, u32[]{:S(2)}) collective-permute-start(bf16[120,128]{1,0:T(8,128)(2,1)S(1)} %get-tuple-element.17), channel_id=1, source_target_pairs={{1,0},{2,1},{3,2},{4,3},{5,4},{6,5},{7,6},{9,8},{10,9},{11,10},{12... | collective-permute-start | bytes 92168 | tf_op jit(solution)/shard_map/ppermute | solution.py:440
  268.1 25.1 %all-to-all-start.4 = ((f32[128,2,120]{2,1,0:T(2,128)}), f32[128,2,120]{2,1,0:T(2,128)S(1)}, u32[]{:S(2)}, u32[]{:S(2)}) async-start(f32[128,2,120]{2,1,0:T(2,128)} %broadcast_in_dim.165), calls=%async_computation.4 | async-start | bytes 262144 | tf_op jit(solution)/shard_map/all_to_all | solution.py:630
  (2 other events, 3.8 us)
